TPU v7x, 256 devices: a whole 4x4x8 slice. The times are simulated.
256 devices in a mesh: tile: 32 (over x, z_lo, core), var: 8 (over y, z_hi).
Axes of the slice: x: 4, y: 4, z: 8 (z_hi: 2, z_lo: 4; z = z_hi * 4 + z_lo), core: 2. Of those that a mesh axis runs over, the one named last changes fastest.
Arguments:
- range_sq: float32 [8, 512, 2048], P('var', 'tile'), may hold values from 0.05 to 4
- state_field: float32 [8, 512, 2048], P('var', 'tile'), may hold values from -6 to 6
- coupling: float32 [8, 8], replicated, may hold values from -2 to 2
- obs_cell: int32 [131072], P('tile'), may hold values from 0 to 32767
- obs_value: float32 [8, 131072], P('var', 'tile'), may hold values from -6 to 6
Outputs:
- adjoint: float32 [8, 512, 2048], P('var', 'tile')
- range_grad: float32 [8, 512, 2048], P('var', 'tile')
Inputs may be any that keep to these rules, and one draw needn't show every extreme that they name: `obs_cell`: each strip's 4096 entries index cells of that strip; cells may repeat.
All inputs are finite; a program needn't handle non-finite values.
Results may differ from a plain program's by a relative error of at most 0.00017.
Values sent between devices are 32-bit elements; how exact they have to be, the bound alone decides.
No kernel may reach another device: no remote copies, remote signals or barrier semaphores. Data moves between devices by JAX's collectives and lax.ppermute only.
A program may use at most 64 MiB of HBM per device.

v0:
```python
import jax
import jax.numpy as jnp
from jax import lax
from jax.sharding import PartitionSpec as P

ITERS = 4


def with_halo(cells, sides, width):
    for axis, dim in sides:
        count = lax.axis_size(axis)
        ends = count - 1
        head = lax.slice_in_dim(cells, 0, width, axis=dim)
        tail = lax.slice_in_dim(cells, cells.shape[dim] - width, cells.shape[dim], axis=dim)
        cells = jnp.concatenate(
            [
                lax.ppermute(tail, axis, [(i, (i + 1) % count) for i in range(ends)]),
                cells,
                lax.ppermute(head, axis, [((i + 1) % count, i) for i in range(ends)]),
            ],
            axis=dim,
        )
    return cells


def apply_block(padded, kappa):
    center = padded[:, 1:-1, 1:-1]
    beside = padded[:, 2:, 1:-1] + padded[:, :-2, 1:-1] + padded[:, 1:-1, 2:] + padded[:, 1:-1, :-2]
    return ((kappa + 4.0) * center - beside) * 0.125


def apply_rows(padded, kappa):
    return apply_block(jnp.pad(padded, ((0, 0), (0, 0), (1, 1))), kappa)


def edge_rows(field):
    return with_halo(field, (("tile", 1),), 1)


def couple(fields, mixing):
    own = fields[0].shape[0]
    start = lax.axis_index("var") * own
    rows_own = lax.dynamic_slice_in_dim(mixing, start, own, 0)
    cols_own = lax.dynamic_slice_in_dim(mixing, start, own, 1)
    gathered = lax.all_gather(fields, "var", axis=0, tiled=True)
    mixed = tuple(
        (
            jnp.einsum("vw,wrc->vrc", rows_own, item, precision=lax.Precision.HIGHEST)
            for item in gathered
        )
    )
    again = lax.all_gather(mixed, "var", axis=0, tiled=True)
    return tuple(
        (
            jnp.einsum("wv,wrc->vrc", cols_own, item, precision=lax.Precision.HIGHEST)
            for item in again
        )
    )


def chebyshev(source, precision_op):
    theta = 4.025
    delta = 3.975
    sigma = theta / delta
    adjoint = jnp.zeros_like(source)
    resid = source
    rho = 1.0 / sigma
    direction = resid / theta
    for step in range(ITERS):
        adjoint = adjoint + direction
        if step < ITERS - 1:
            resid = resid - precision_op(direction)
            rho_new = 1.0 / (2.0 * sigma - rho)
            direction = rho_new * rho * direction + 2.0 * rho_new / delta * resid
            rho = rho_new
    return adjoint


def per_device(range_sq, state_field, coupling, obs_cell, obs_value):
    own, strip_rows, columns = range_sq.shape
    mixing = jnp.eye(coupling.shape[0], dtype=jnp.float32) + coupling
    source = jnp.zeros((own, strip_rows * columns), jnp.float32).at[:, obs_cell].add(obs_value)
    source = source.reshape(own, strip_rows, columns)

    def precision_op(field):
        shaped = apply_rows(edge_rows(field), range_sq)
        coupled = couple((shaped,), mixing)[0]
        return apply_rows(edge_rows(coupled), range_sq)

    adjoint = chebyshev(source, precision_op)
    stacked = jnp.concatenate([adjoint, state_field], axis=0)
    padded = with_halo(stacked, (("tile", 1),), 1)
    shaped_adjoint = apply_rows(padded[:own], range_sq)
    shaped_state = apply_rows(padded[own:], range_sq)
    coupled_adjoint, coupled_state = couple((shaped_adjoint, shaped_state), mixing)
    range_grad = -(coupled_adjoint * state_field + adjoint * coupled_state) * 0.125
    return (adjoint, range_grad)


def solution(mesh):
    return jax.shard_map(
        per_device,
        mesh=mesh,
        in_specs=(P("var", "tile", None), P("var", "tile", None), P(), P("tile"), P("var", "tile")),
        out_specs=(P("var", "tile", None), P("var", "tile", None)),
        check_vma=False,
    )
```

profile of v0, /device:TPU:2, one launch (start us, length us, event | category | flops | bytes accessed | tf_op | source)
XLA Modules:
  0.0 735.8 jit_solution(6599219713589058319)
XLA Ops:
  7.9 22.1 %scatter_custom_fusion = f32[32768]{0:T(1024)S(1)} fusion(s32[4096]{0:T(1024)S(1)} %compare_select_fusion, f32[4096]{0:T(1024)} %bitcast.64, f32[]{:T(128)} %constant.14.clone.1), kind=kCustom, calls=%fused_computation.115 | custom fusion | flops 4096 | bytes 131584 | tf_op jit(solution)/shard_map/scatter-add | solution.py:82
  32.1 6.5 collective-permute-start
  41.6 65.2 %all-gather.16.cloned.1.call-done = f32[8,16,2048]{2,1,0:T(8,128)} async-done(((f32[1,16,2048]{2,1,0:T(8,128)}), f32[8,16,2048]{2,1,0:T(8,128)}) %all-gather.16.cloned.1.call-update) | async-done | bytes 1048592 | tf_op jit(solution)/shard_map/all_gather | solution.py:45
  106.8 2.7 fusion.18
  110.5 57.4 %all-gather.26.cloned.1.call-done = f32[128,2048]{1,0:T(8,128)} async-done(((f32[16,2048]{1,0:T(8,128)}), f32[128,2048]{1,0:T(8,128)}) %all-gather.26.cloned.1.call-update) | async-done | bytes 1048592 | tf_op jit(solution)/shard_map/all_gather | solution.py:52
  167.9 2.7 fusion.16
  172.6 6.3 collective-permute-start.2
  182.6 6.4 collective-permute-start.4
  191.3 61.1 %all-gather.18.cloned.1.call-done = f32[8,16,2048]{2,1,0:T(8,128)} async-done(((f32[1,16,2048]{2,1,0:T(8,128)}), f32[8,16,2048]{2,1,0:T(8,128)}) %all-gather.18.cloned.1.call-update) | async-done | bytes 1048592 | tf_op jit(solution)/shard_map/all_gather | solution.py:45
  255.9 57.6 %all-gather.28.cloned.1.call-done = f32[128,2048]{1,0:T(8,128)} async-done(((f32[16,2048]{1,0:T(8,128)}), f32[128,2048]{1,0:T(8,128)}) %all-gather.28.cloned.1.call-update) | async-done | bytes 1048592 | tf_op jit(solution)/shard_map/all_gather | solution.py:52
  313.5 2.7 fusion.12
  318.2 6.3 collective-permute-start.6
  328.2 6.4 collective-permute-start.8
  336.9 61.1 %all-gather.20.cloned.1.call-done = f32[8,16,2048]{2,1,0:T(8,128)} async-done(((f32[1,16,2048]{2,1,0:T(8,128)}), f32[8,16,2048]{2,1,0:T(8,128)}) %all-gather.20.cloned.1.call-update) | async-done | bytes 1048592 | tf_op jit(solution)/shard_map/all_gather | solution.py:45
  401.6 57.4 %all-gather.30.cloned.1.call-done = f32[128,2048]{1,0:T(8,128)} async-done(((f32[16,2048]{1,0:T(8,128)}), f32[128,2048]{1,0:T(8,128)}) %all-gather.30.cloned.1.call-update) | async-done | bytes 1048592 | tf_op jit(solution)/shard_map/all_gather | solution.py:52
  459.1 2.7 fusion.8
  463.8 6.3 collective-permute-start.10
  474.5 6.3 collective-permute-start.12
  484.1 60.4 %all-gather.22.cloned.1.call-done = f32[8,16,2048]{2,1,0:T(8,128)} async-done(((f32[1,16,2048]{2,1,0:T(8,128)}), f32[8,16,2048]{2,1,0:T(8,128)}) %all-gather.22.cloned.1.call-update) | async-done | bytes 1048592 | tf_op jit(solution)/shard_map/all_gather | solution.py:45
  548.0 56.7 %all-gather.24.cloned.1.call-done = f32[8,16,2048]{2,1,0:T(8,128)} async-done(((f32[1,16,2048]{2,1,0:T(8,128)}), f32[8,16,2048]{2,1,0:T(8,128)}) %all-gather.24.cloned.1.call-update) | async-done | bytes 1048592 | tf_op jit(solution)/shard_map/all_gather | solution.py:45
  604.7 2.7 fusion.2
  608.1 56.7 %all-gather.32.cloned.1.call-done = f32[128,2048]{1,0:T(8,128)} async-done(((f32[16,2048]{1,0:T(8,128)}), f32[128,2048]{1,0:T(8,128)}) %all-gather.32.cloned.1.call-update) | async-done | bytes 1048592 | tf_op jit(solution)/shard_map/all_gather | solution.py:52
  664.9 2.7 fusion.4
  667.6 57.9 %all-gather.34.cloned.1.call-done = f32[128,2048]{1,0:T(8,128)} async-done(((f32[16,2048]{1,0:T(8,128)}), f32[128,2048]{1,0:T(8,128)}) %all-gather.34.cloned.1.call-update) | async-done | bytes 1048592 | tf_op jit(solution)/shard_map/all_gather | solution.py:52
  (89 shorter events, 46.6 us)
Async XLA Ops:
  7.2 99.6 %all-gather.16.cloned.1.call-start = ((), (), s32[]{:S(2)}) async-start(), calls=%async_computation | async-start | bytes 1179648 | tf_op jit(solution)/shard_map/all_gather | solution.py:45
  30.1 8.4 %collective-permute-start.1 = (f32[1,1,2048]{2,1,0:T(1,128)S(1)}, f32[1,1,2048]{2,1,0:T(1,128)S(1)}, u32[]{:S(2)}, u32[]{:S(2)}) collective-permute-start(f32[1,1,2048]{2,1,0:T(1,128)S(1)} %get-tuple-element.22), channel_id=1, source_target_pairs={{0,8},{8,16},{16,24},{24,32},{32,40},{40,48},{48,56},{56,64},{64,7... | collective-permute-start | bytes 24584 | tf_op jit(solution)/shard_map/ppermute | solution.py:17
  32.1 7.8 %collective-permute-start = (f32[1,1,2048]{2,1,0:T(1,128)S(1)}, f32[1,1,2048]{2,1,0:T(1,128)S(1)}, u32[]{:S(2)}, u32[]{:S(2)}) collective-permute-start(f32[1,1,2048]{2,1,0:T(1,128)S(1)} %get-tuple-element.23), channel_id=1, source_target_pairs={{8,0},{16,8},{24,16},{32,24},{40,32},{48,40},{56,48},{64,56},{72,6... | collective-permute-start | bytes 24584 | tf_op jit(solution)/shard_map/ppermute | solution.py:19
  40.9 127.1 %all-gather.26.cloned.1.call-start = ((), (), s32[]{:S(2)}) async-start(), calls=%async_computation.5 | async-start | bytes 1179648 | tf_op jit(solution)/shard_map/all_gather | solution.py:52
  110.2 142.2 %all-gather.18.cloned.1.call-start = ((), (), s32[]{:S(2)}) async-start(), calls=%async_computation.1 | async-start | bytes 1179648 | tf_op jit(solution)/shard_map/all_gather | solution.py:45
  170.7 8.3 %collective-permute-start.3 = (f32[1,1,2048]{2,1,0:T(1,128)S(1)}, f32[1,1,2048]{2,1,0:T(1,128)S(1)}, u32[]{:S(2)}, u32[]{:S(2)}) collective-permute-start(f32[1,1,2048]{2,1,0:T(1,128)S(1)} %get-tuple-element.20), channel_id=1, source_target_pairs={{0,8},{8,16},{16,24},{24,32},{32,40},{40,48},{48,56},{56,64},{64,7... | collective-permute-start | bytes 24584 | tf_op jit(solution)/shard_map/ppermute | solution.py:17
  172.6 7.7 %collective-permute-start.2 = (f32[1,1,2048]{2,1,0:T(1,128)S(1)}, f32[1,1,2048]{2,1,0:T(1,128)S(1)}, u32[]{:S(2)}, u32[]{:S(2)}) collective-permute-start(f32[1,1,2048]{2,1,0:T(1,128)S(1)} %get-tuple-element.21), channel_id=1, source_target_pairs={{8,0},{16,8},{24,16},{32,24},{40,32},{48,40},{56,48},{64,56},{72,6... | collective-permute-start | bytes 24584 | tf_op jit(solution)/shard_map/ppermute | solution.py:19
  180.6 8.3 %collective-permute-start.5 = (f32[1,1,2048]{2,1,0:T(1,128)S(1)}, f32[1,1,2048]{2,1,0:T(1,128)S(1)}, u32[]{:S(2)}, u32[]{:S(2)}) collective-permute-start(f32[1,1,2048]{2,1,0:T(1,128)S(1)} %get-tuple-element.18), channel_id=1, source_target_pairs={{0,8},{8,16},{16,24},{24,32},{32,40},{40,48},{48,56},{56,64},{64,7... | collective-permute-start | bytes 24584 | tf_op jit(solution)/shard_map/ppermute | solution.py:17
  182.6 7.7 %collective-permute-start.4 = (f32[1,1,2048]{2,1,0:T(1,128)S(1)}, f32[1,1,2048]{2,1,0:T(1,128)S(1)}, u32[]{:S(2)}, u32[]{:S(2)}) collective-permute-start(f32[1,1,2048]{2,1,0:T(1,128)S(1)} %get-tuple-element.19), channel_id=1, source_target_pairs={{8,0},{16,8},{24,16},{32,24},{40,32},{48,40},{56,48},{64,56},{72,6... | collective-permute-start | bytes 24584 | tf_op jit(solution)/shard_map/ppermute | solution.py:19
  191.2 122.3 %all-gather.28.cloned.1.call-start = ((), (), s32[]{:S(2)}) async-start(), calls=%async_computation.6 | async-start | bytes 1179648 | tf_op jit(solution)/shard_map/all_gather | solution.py:52
  255.8 142.2 %all-gather.20.cloned.1.call-start = ((), (), s32[]{:S(2)}) async-start(), calls=%async_computation.2 | async-start | bytes 1179648 | tf_op jit(solution)/shard_map/all_gather | solution.py:45
  316.3 8.3 %collective-permute-start.7 = (f32[1,1,2048]{2,1,0:T(1,128)S(1)}, f32[1,1,2048]{2,1,0:T(1,128)S(1)}, u32[]{:S(2)}, u32[]{:S(2)}) collective-permute-start(f32[1,1,2048]{2,1,0:T(1,128)S(1)} %get-tuple-element.16), channel_id=1, source_target_pairs={{0,8},{8,16},{16,24},{24,32},{32,40},{40,48},{48,56},{56,64},{64,7... | collective-permute-start | bytes 24584 | tf_op jit(solution)/shard_map/ppermute | solution.py:17
  318.2 7.7 %collective-permute-start.6 = (f32[1,1,2048]{2,1,0:T(1,128)S(1)}, f32[1,1,2048]{2,1,0:T(1,128)S(1)}, u32[]{:S(2)}, u32[]{:S(2)}) collective-permute-start(f32[1,1,2048]{2,1,0:T(1,128)S(1)} %get-tuple-element.17), channel_id=1, source_target_pairs={{8,0},{16,8},{24,16},{32,24},{40,32},{48,40},{56,48},{64,56},{72,6... | collective-permute-start | bytes 24584 | tf_op jit(solution)/shard_map/ppermute | solution.py:19
  326.2 8.3 %collective-permute-start.9 = (f32[1,1,2048]{2,1,0:T(1,128)S(1)}, f32[1,1,2048]{2,1,0:T(1,128)S(1)}, u32[]{:S(2)}, u32[]{:S(2)}) collective-permute-start(f32[1,1,2048]{2,1,0:T(1,128)S(1)} %get-tuple-element.14), channel_id=1, source_target_pairs={{0,8},{8,16},{16,24},{24,32},{32,40},{40,48},{48,56},{56,64},{64,7... | collective-permute-start | bytes 24584 | tf_op jit(solution)/shard_map/ppermute | solution.py:17
  328.2 7.7 %collective-permute-start.8 = (f32[1,1,2048]{2,1,0:T(1,128)S(1)}, f32[1,1,2048]{2,1,0:T(1,128)S(1)}, u32[]{:S(2)}, u32[]{:S(2)}) collective-permute-start(f32[1,1,2048]{2,1,0:T(1,128)S(1)} %get-tuple-element.15), channel_id=1, source_target_pairs={{8,0},{16,8},{24,16},{32,24},{40,32},{48,40},{56,48},{64,56},{72,6... | collective-permute-start | bytes 24584 | tf_op jit(solution)/shard_map/ppermute | solution.py:19
  336.8 122.3 %all-gather.30.cloned.1.call-start = ((), (), s32[]{:S(2)}) async-start(), calls=%async_computation.7 | async-start | bytes 1179648 | tf_op jit(solution)/shard_map/all_gather | solution.py:52
  401.4 143.1 %all-gather.22.cloned.1.call-start = ((), (), s32[]{:S(2)}) async-start(), calls=%async_computation.3 | async-start | bytes 1179648 | tf_op jit(solution)/shard_map/all_gather | solution.py:45
  461.9 8.3 %collective-permute-start.11 = (f32[1,1,2048]{2,1,0:T(1,128)S(1)}, f32[1,1,2048]{2,1,0:T(1,128)S(1)}, u32[]{:S(2)}, u32[]{:S(2)}) collective-permute-start(f32[1,1,2048]{2,1,0:T(1,128)S(1)} %get-tuple-element.12), channel_id=1, source_target_pairs={{0,8},{8,16},{16,24},{24,32},{32,40},{40,48},{48,56},{56,64},{64,7... | collective-permute-start | bytes 24584 | tf_op jit(solution)/shard_map/ppermute | solution.py:17
  463.8 7.7 %collective-permute-start.10 = (f32[1,1,2048]{2,1,0:T(1,128)S(1)}, f32[1,1,2048]{2,1,0:T(1,128)S(1)}, u32[]{:S(2)}, u32[]{:S(2)}) collective-permute-start(f32[1,1,2048]{2,1,0:T(1,128)S(1)} %get-tuple-element.13), channel_id=1, source_target_pairs={{8,0},{16,8},{24,16},{32,24},{40,32},{48,40},{56,48},{64,56},{72,6... | collective-permute-start | bytes 24584 | tf_op jit(solution)/shard_map/ppermute | solution.py:19
  472.6 8.3 %collective-permute-start.13 = (f32[2,1,2048]{2,1,0:T(1,128)S(1)}, f32[2,1,2048]{2,1,0:T(1,128)S(1)}, u32[]{:S(2)}, u32[]{:S(2)}) collective-permute-start(f32[2,1,2048]{2,1,0:T(1,128)S(1)} %get-tuple-element.10), channel_id=1, source_target_pairs={{0,8},{8,16},{16,24},{24,32},{32,40},{40,48},{48,56},{56,64},{64,7... | collective-permute-start | bytes 49160 | tf_op jit(solution)/shard_map/ppermute | solution.py:17
  474.5 7.8 %collective-permute-start.12 = (f32[2,1,2048]{2,1,0:T(1,128)S(1)}, f32[2,1,2048]{2,1,0:T(1,128)S(1)}, u32[]{:S(2)}, u32[]{:S(2)}) collective-permute-start(f32[2,1,2048]{2,1,0:T(1,128)S(1)} %get-tuple-element.11), channel_id=1, source_target_pairs={{8,0},{16,8},{24,16},{32,24},{40,32},{48,40},{56,48},{64,56},{72,6... | collective-permute-start | bytes 49160 | tf_op jit(solution)/shard_map/ppermute | solution.py:19
  483.3 121.4 %all-gather.24.cloned.1.call-start = ((), (), s32[]{:S(2)}) async-start(), calls=%async_computation.4 | async-start | bytes 1179648 | tf_op jit(solution)/shard_map/all_gather | solution.py:45
  484.1 180.8 %all-gather.32.cloned.1.call-start = ((), (), s32[]{:S(2)}) async-start(), calls=%async_computation.8 | async-start | bytes 1179648 | tf_op jit(solution)/shard_map/all_gather | solution.py:52
  548.0 177.5 %all-gather.34.cloned.1.call-start = ((), (), s32[]{:S(2)}) async-start(), calls=%async_computation.9 | async-start | bytes 1179648 | tf_op jit(solution)/shard_map/all_gather | solution.py:52
  (4 other events, 265.2 us)
Sparse Core Ops, SparseCore 0:
  41.0 65.7 all-gather.15
  110.4 57.5 all-gather.25
  191.3 61.0 all-gather.17
  255.9 57.5 all-gather.27
  336.9 60.9 all-gather.19
  401.5 57.5 all-gather.29
  483.5 61.0 all-gather.21
  547.1 57.5 all-gather.23
  607.3 57.5 all-gather.31
  667.9 57.5 all-gather.33
where the time goes:
time: 737 us; the launch traced here: 736 us
  waiting for transfers between devices  602 us (82%)
  starting transfers between devices  58.6 us (8%)
  other arithmetic  28.2 us (4%)
  matrix products  27.1 us (4%)
  between operations  14.6 us (2%)
    all_gather x5, waiting for transfers between devices, couple(): gathered = lax.all_gather(fields, 'var', axis=0, tiled=True)  305 us
    all_gather x5, waiting for transfers between devices, couple(): again = lax.all_gather(mixed, 'var', axis=0, tiled=True)  287 us
    ppermute x7, starting transfers between devices, with_halo(): lax.ppermute(head, axis, [((i + 1) % count, i) for i in range(ends)])  44.5 us
    scatter-add x1, other arithmetic, per_device(): jnp.zeros((own, strip_rows * columns), jnp.float32).at[:, obs_cell]  22.1 us
  transfers between devices with their start and end apart: 24, of which 17 were waited for; matrix products, arithmetic and copies ran while one was open for 1% of the time, Pallas kernels for 0%

commit v1 on v0

v1 whole, which is shorter than its diff:
```python
import functools

import jax
import jax.numpy as jnp
from jax import lax
from jax.experimental import pallas as pl
from jax.experimental.pallas import tpu as pltpu
from jax.sharding import PartitionSpec as P

ITERS = 4
THETA = 4.025
DELTA = 3.975
VMEM = pl.BlockSpec(memory_space=pltpu.VMEM)
SMEM = pl.BlockSpec(memory_space=pltpu.SMEM)

ROWS, COLS, VARS, GROUPS = 16, 2048, 8, 4
BLOCK = COLS // GROUPS
SIDE = 128
WIDE = BLOCK + SIDE
EDGE = 8
TALL = ROWS + 2 * EDGE
OBS = 4096
OBS_ROWS = OBS // BLOCK


def group_place():
    var = lax.axis_index("var")
    return var // 2, lax.rem(var, 2)


def window(ref, block, rows):
    main = ref[:, pl.ds(pl.multiple_of(block * BLOCK, BLOCK), BLOCK)]
    after = jnp.minimum(block + 1, GROUPS - 1) * BLOCK
    before = jnp.maximum(block * BLOCK - SIDE, 0)
    right = ref[:, pl.ds(pl.multiple_of(after, SIDE), SIDE)]
    left = ref[:, pl.ds(pl.multiple_of(before, SIDE), SIDE)]
    lane = lax.broadcasted_iota(jnp.int32, (rows, SIDE), 1)
    return main, jnp.where(lane < SIDE // 2, right, left)


def pack_state_kernel(state_ref, *outs):
    y, _ = group_place()
    for k in range(GROUPS):
        main, side = window(state_ref, lax.rem(y + k, GROUPS), ROWS)
        outs[k][:, :BLOCK] = main
        outs[k][:, BLOCK:] = side


def pack_kappa_kernel(own_ref, other_ref, own_obs_ref, other_obs_ref, *outs):
    y, _ = group_place()
    for k in range(GROUPS):
        for slot, (ref, obs) in enumerate(((own_ref, own_obs_ref), (other_ref, other_obs_ref))):
            main, side = window(ref, lax.rem(y + k, GROUPS), ROWS)
            outs[k][slot, :ROWS, :BLOCK] = main
            outs[k][slot, :ROWS, BLOCK:] = side
            for i in range(OBS_ROWS):
                outs[k][slot, ROWS + i : ROWS + i + 1, :BLOCK] = obs[:, i * BLOCK : (i + 1) * BLOCK]


def scatter_kernel(cell_ref, k0, k1, k2, k3, sa_ref, sb_ref, source_ref, up_ref, down_ref, acc):
    y, z = group_place()
    pieces = (k0, k1, k2, k3)
    acc[...] = jnp.zeros_like(acc)
    rows = lax.broadcasted_iota(jnp.int32, (ROWS, BLOCK), 0)
    lanes = lax.broadcasted_iota(jnp.int32, (WIDE, BLOCK), 0)
    half = SIDE // 2
    for i in range(OBS_ROWS):
        cell = cell_ref[:, i * BLOCK : (i + 1) * BLOCK]
        row = lax.shift_right_logical(cell, 11)
        col = jnp.bitwise_and(cell, COLS - 1) - y * BLOCK
        place = jnp.where(
            (col >= 0) & (col < BLOCK + half), col, jnp.where((col >= -half) & (col < 0), col + WIDE, -1)
        )
        hit_row = rows == row
        hit_col = jnp.where(lanes == place, 1.0, 0.0).astype(jnp.bfloat16)
        highs, lows = [], []
        for k in range(GROUPS):
            for slot in range(2):
                value = pieces[k][slot, ROWS + i : ROWS + i + 1, :BLOCK]
                high = value.astype(jnp.bfloat16).astype(jnp.float32)
                low = value - high
                highs.append(jnp.where(hit_row, high, 0.0).astype(jnp.bfloat16))
                lows.append(jnp.where(hit_row, low, 0.0).astype(jnp.bfloat16))
        values = jnp.concatenate(highs + lows, axis=0)
        acc[...] += lax.dot_general(
            values, hit_col, (((1,), (1,)), ((), ())), preferred_element_type=jnp.float32
        )
    count = VARS * ROWS
    for k in range(GROUPS):
        for slot in range(2):
            at = (k * 2 + slot) * ROWS
            total = acc[at : at + ROWS] + acc[count + at : count + at + ROWS]
            var = 2 * lax.rem(y - k + GROUPS, GROUPS) + lax.rem(z + slot, 2)
            source_ref[var] = total
            up_ref[0, var] = total[:EDGE]
            down_ref[0, var] = total[EDGE:]
            kappa = pieces[k][slot, :ROWS]
            up_ref[1, var] = kappa[:EDGE]
            down_ref[1, var] = kappa[EDGE:]
            state = (sa_ref, sb_ref)[slot]
            up_ref[2, 0, pl.ds(var, 1), :] = state[k, 0:1, :]
            down_ref[2, 0, pl.ds(var, 1), :] = state[k, ROWS - 1 : ROWS, :]


def shape_rows(u):
    return pltpu.roll(u, 1, 0) + pltpu.roll(u, TALL - 1, 0) + pltpu.roll(u, 1, 1) + pltpu.roll(u, WIDE - 1, 1)


def main_kernel(
    mix_ref, source_ref, above_ref, below_ref, k0, k1, k2, k3, sa_ref, sb_ref, o0, o1, o2, o3,
    kp, adj, res, dirn, tmp, state, mask_ref
):
    y, z = group_place()
    tile = lax.axis_index("tile")
    pieces = (k0, k1, k2, k3)
    row = lax.broadcasted_iota(jnp.int32, (TALL, WIDE), 0)
    lane = lax.broadcasted_iota(jnp.int32, (TALL, WIDE), 1)
    row = jnp.where(row < ROWS + EDGE, row, row - TALL) + tile * ROWS
    lane = jnp.where(lane < BLOCK + SIDE // 2, lane, lane - WIDE) + y * BLOCK
    inside = (row >= 0) & (row < ROWS * lax.axis_size("tile")) & (lane >= 0) & (lane < COLS)
    mask_ref[...] = jnp.where(inside, 1.0, 0.0)
    mask = mask_ref[...]
    for k in range(GROUPS):
        for slot in range(2):
            var = 2 * lax.rem(y - k + GROUPS, GROUPS) + lax.rem(z + slot, 2)
            kp[var, :ROWS] = pieces[k][slot, :ROWS] + 4.0
            state[var, :ROWS] = (sa_ref, sb_ref)[slot][k]
    kp[:, ROWS : ROWS + EDGE] = below_ref[1] + 4.0
    kp[:, ROWS + EDGE :] = above_ref[1] + 4.0
    for var in range(VARS):
        state[var, ROWS : ROWS + 1] = below_ref[2, 0, var : var + 1, :]
        state[var, ROWS + 1 : TALL - 1] = jnp.zeros((TALL - ROWS - 2, WIDE), jnp.float32)
        state[var, TALL - 1 :] = above_ref[2, 0, var : var + 1, :]

    def fill(var, _):
        kp[var] = kp[var] * mask_ref[...]
        state[var] = state[var] * mask_ref[...]
        for at, part in ((0, source_ref[var]), (ROWS, below_ref[0, var]), (ROWS + EDGE, above_ref[0, var])):
            part = part * mask_ref[at : at + part.shape[0]]
            res[var, at : at + part.shape[0]] = part
            part = part * (1.0 / THETA)
            dirn[var, at : at + part.shape[0]] = part
            adj[var, at : at + part.shape[0]] = part
        return 0

    lax.fori_loop(0, VARS, fill, 0)

    def shape(src, var):
        u = src[var]
        return kp[var] * u - shape_rows(u) * mask_ref[...]

    def couple(ref):
        def step(at, _):
            at = pl.multiple_of(at * 8, 8)
            for c in range(WIDE // 128):
                cols = slice(c * 128, (c + 1) * 128)
                fields = [ref[w, pl.ds(at, 8), cols] for w in range(VARS)]
                for v in range(VARS):
                    total = mix_ref[v, 0] * fields[0]
                    for w in range(1, VARS):
                        total = total + mix_ref[v, w] * fields[w]
                    ref[v, pl.ds(at, 8), cols] = total
            return 0

        lax.fori_loop(0, TALL // 8, step, 0)

    sigma = THETA / DELTA
    rho = 1.0 / sigma
    for _ in range(ITERS - 1):
        rho_new = 1.0 / (2.0 * sigma - rho)
        c1, c2 = rho_new * rho, 2.0 * rho_new / DELTA
        rho = rho_new

        def first(var, _):
            tmp[var] = shape(dirn, var)
            return 0

        lax.fori_loop(0, VARS, first, 0)
        couple(tmp)

        def second(var, _):
            r = res[var] - shape(tmp, var)
            res[var] = r
            d = c1 * dirn[var] + c2 * r
            dirn[var] = d
            adj[var] = adj[var] + d
            return 0

        lax.fori_loop(0, VARS, second, 0)

    def last(var, _):
        tmp[var] = shape(adj, var)
        res[var] = shape(state, var)
        return 0

    lax.fori_loop(0, VARS, last, 0)
    for k, out in enumerate((o0, o1, o2, o3)):
        v = 2 * lax.rem(y + k, GROUPS) + z
        for r in range(0, ROWS, 8):
            for c in range(0, BLOCK, 128):
                here = (slice(r, r + 8), slice(c, c + 128))
                first_sum = mix_ref[v, 0] * tmp[(0,) + here]
                second_sum = mix_ref[v, 0] * res[(0,) + here]
                for w in range(1, VARS):
                    first_sum = first_sum + mix_ref[v, w] * tmp[(w,) + here]
                    second_sum = second_sum + mix_ref[v, w] * res[(w,) + here]
                a = adj[v, r : r + 8, c : c + 128]
                out[(0,) + here] = a
                out[(1,) + here] = -(first_sum * state[v, r : r + 8, c : c + 128] + a * second_sum)


def join_kernel(p0, p1, p2, p3, adjoint_ref, grad_ref):
    y, _ = group_place()
    for k, part in enumerate((p0, p1, p2, p3)):
        at = pl.multiple_of(lax.rem(y - k + GROUPS, GROUPS) * BLOCK, BLOCK)
        adjoint_ref[:, pl.ds(at, BLOCK)] = part[0]
        grad_ref[:, pl.ds(at, BLOCK)] = part[1]


def call(kernel, outs, n_in, smem=0, scratch=(), flops=1000, size=100000):
    shapes = [jax.ShapeDtypeStruct(s, jnp.float32) for s in outs]
    return pl.pallas_call(
        kernel,
        out_shape=shapes,
        in_specs=[SMEM] * smem + [VMEM] * (n_in - smem),
        out_specs=[VMEM] * len(shapes),
        scratch_shapes=list(scratch),
        compiler_params=pltpu.CompilerParams(vmem_limit_bytes=32 * 1024 * 1024),
        cost_estimate=pl.CostEstimate(flops=flops, bytes_accessed=size, transcendentals=0),
    )


def across(x):
    return lax.ppermute(x, "var", [(i, i ^ 1) for i in range(VARS)])


def around(x, k):
    return lax.ppermute(x, "var", [(i, (i // 2 + k) % GROUPS * 2 + i % 2) for i in range(VARS)])


def along(x, tiles, forward):
    pairs = []
    for i in range(tiles - 1):
        for v in range(VARS):
            ahead = (i + 1) * VARS + (v ^ 1 if i % 8 == 7 else v)
            pairs.append((i * VARS + v, ahead) if forward else (ahead, i * VARS + v))
    return lax.ppermute(x, ("tile", "var"), pairs)


def per_device(tiles, range_sq, state_field, coupling, obs_cell, obs_value):
    mixing = jnp.eye(VARS, dtype=jnp.float32) + coupling
    mix = jnp.einsum("uv,uw->vw", mixing, mixing, precision=lax.Precision.HIGHEST) * (1.0 / 64.0)
    kappa = range_sq[0]
    other_kappa = across(kappa)
    other_obs = across(obs_value)
    s0, s1, s2, s3 = call(pack_state_kernel, [(ROWS, WIDE)] * 4, 1)(state_field[0])
    states = jnp.stack([s0, around(s1, 1), around(s2, 2), around(s3, 3)])
    other_states = across(states)
    k0, k1, k2, k3 = call(pack_kappa_kernel, [(2, ROWS + OBS_ROWS, WIDE)] * 4, 4)(kappa, other_kappa, obs_value, other_obs)
    k1, k2, k3 = around(k1, 1), around(k2, 2), around(k3, 3)
    pieces = (k0, k1, k2, k3)
    source, up, down = call(
        scatter_kernel,
        [(VARS, ROWS, WIDE), (3, VARS, EDGE, WIDE), (3, VARS, EDGE, WIDE)],
        7,
        scratch=[pltpu.VMEM((2 * VARS * ROWS, WIDE), jnp.float32)],
    )(obs_cell.reshape(1, OBS), *pieces, states, other_states)
    above = along(down, tiles, True)
    below = along(up, tiles, False)
    field = pltpu.VMEM((VARS, TALL, WIDE), jnp.float32)
    parts = call(
        main_kernel,
        [(2, ROWS, BLOCK)] * 4,
        10,
        smem=1,
        scratch=[field] * 6 + [pltpu.VMEM((TALL, WIDE), jnp.float32)],
    )(mix, source, above, below, *pieces, states, other_states)
    parts = [parts[0]] + [around(parts[k], k) for k in range(1, GROUPS)]
    adjoint, grad = call(join_kernel, [(ROWS, COLS)] * 2, 4)(*parts)
    return adjoint[None], grad[None]


def solution(mesh):
    return jax.shard_map(
        functools.partial(per_device, mesh.shape["tile"]),
        mesh=mesh,
        in_specs=(P("var", "tile", None), P("var", "tile", None), P(), P("tile"), P("var", "tile")),
        out_specs=(P("var", "tile", None), P("var", "tile", None)),
        check_vma=False,
    )
```

time: 737 us -> 70.5 us (0.10)
  waiting for transfers between devices: 602 us -> 25.6 us
  other arithmetic: 28.2 us -> 0.01 us
  starting transfers between devices: 58.6 us -> 30.6 us
  matrix products: 27.1 us -> 0.19 us
  between operations: 14.6 us -> 0.72 us
  Pallas kernels: 0 us -> 12.3 us
    all_gather x10 -> x0, waiting for transfers between devices: 592 us -> none  [the longest x5 305 us: couple(): gathered = lax.all_gather(fields, 'var', axis=0, tiled=True)]
    ppermute x14, starting transfers between devices: 58 us -> 30.6 us  [the longest x3 13.2 us: across(): return lax.ppermute(x, 'var', [(i, i ^ 1) for i in range(VARS)])]
    dot_general x10 -> x1, matrix products: 27.1 us -> 0.19 us  [per_device(): jnp.einsum('uv,uw->vw', mixing, mixing, precision=lax.Precision.HIGHEST)]
    scatter-add x1 -> x0, other arithmetic: 22.1 us -> none  [per_device(): jnp.zeros((own, strip_rows * columns), jnp.float32).at[:, obs_cell]]
    ppermute x14, waiting for transfers between devices: 9.43 us -> 25.6 us  [the longest x2 9.64 us: along(): return lax.ppermute(x, ('tile', 'var'), pairs)]
    pallas_call x0 -> x5, Pallas kernels: none -> 12.3 us  [the longest x1 9.55 us: per_device(): call(main_kernel, [(2, ROWS, BLOCK)] * 4, 10, smem=1, scratch=[field] * 6...]
  transfers between devices with their start and end apart: 24 -> 14, of which waited for: 17 -> 8; matrix products, arithmetic and copies ran while one was open for 1% -> 0% of each run, Pallas kernels for 0% -> 0%
where the time goes in v1:
time: 70.5 us; the launch traced here: 70.3 us
  starting transfers between devices  30.6 us (43%)
  waiting for transfers between devices  25.6 us (36%)
  Pallas kernels  12.3 us (17%)
  local copies, waits for them, and re-layouts  0.91 us (1%)
  between operations  0.72 us (1%)
    ppermute x3, starting transfers between devices, across(): return lax.ppermute(x, 'var', [(i, i ^ 1) for i in range(VARS)])  13.2 us
    ppermute x9, starting transfers between devices, around(): lax.ppermute(x, 'var', [(i, (i // 2 + k) % GROUPS * 2 + i % 2) for i in r...  13.1 us
    ppermute x2, waiting for transfers between devices, along(): return lax.ppermute(x, ('tile', 'var'), pairs)  9.64 us
    pallas_call x1, Pallas kernels, per_device(): call(main_kernel, [(2, ROWS, BLOCK)] * 4, 10, smem=1, scratch=[field] * 6...  9.55 us
    ppermute x9, waiting for transfers between devices, around(): lax.ppermute(x, 'var', [(i, (i // 2 + k) % GROUPS * 2 + i % 2) for i in r...  9.33 us
    ppermute x3, waiting for transfers between devices, across(): return lax.ppermute(x, 'var', [(i, i ^ 1) for i in range(VARS)])  6.63 us
    ppermute x2, starting transfers between devices, along(): return lax.ppermute(x, ('tile', 'var'), pairs)  4.33 us
    pallas_call x1, Pallas kernels, per_device(): call(scatter_kernel, [(VARS, ROWS, WIDE), (3, VARS, EDGE, WIDE), (3, VARS...  1.89 us
  transfers between devices with their start and end apart: 14, of which 8 were waited for; matrix products, arithmetic and copies ran while one was open for 0% of the time, Pallas kernels for 0%

profile of v1, /device:TPU:2, one launch (start us, length us, event | category | flops | bytes accessed | tf_op | source)
XLA Modules:
  0.0 70.3 jit_solution(16840870086587048063)
XLA Ops:
  0.6 0.9 %copy-done = f32[1,16,2048]{2,1,0:T(8,128)S(1)} copy-done((f32[1,16,2048]{2,1,0:T(8,128)S(1)}, f32[1,16,2048]{2,1,0:T(8,128)}, u32[]{:S(2)}) %copy-start) | copy-done | bytes 131096
  1.6 1.7 %collective-permute-start.5 = (f32[16,640]{1,0:T(8,128)S(1)}, f32[16,640]{1,0:T(8,128)S(1)}, u32[]{:S(2)}, u32[]{:S(2)}) collective-permute-start(f32[16,640]{1,0:T(8,128)S(1)} %get-tuple-element.24), channel_id=1, source_target_pairs={{0,2},{1,3},{2,4},{3,5},{4,6},{5,7},{6,0},{7,1},{8,10},{9,11},{10,... | collective-permute-start | bytes 122888 | tf_op jit(solution)/shard_map/ppermute | solution.py:238
  3.2 2.9 %collective-permute-start.6 = (f32[16,640]{1,0:T(8,128)S(1)}, f32[16,640]{1,0:T(8,128)S(1)}, u32[]{:S(2)}, u32[]{:S(2)}) collective-permute-start(f32[16,640]{1,0:T(8,128)S(1)} %get-tuple-element.25), channel_id=1, source_target_pairs={{0,4},{1,5},{2,6},{3,7},{4,0},{5,1},{6,2},{7,3},{8,12},{9,13},{10,... | collective-permute-start | bytes 122888 | tf_op jit(solution)/shard_map/ppermute | solution.py:238
  6.1 1.3 %collective-permute-start.7 = (f32[16,640]{1,0:T(8,128)S(1)}, f32[16,640]{1,0:T(8,128)S(1)}, u32[]{:S(2)}, u32[]{:S(2)}) collective-permute-start(f32[16,640]{1,0:T(8,128)S(1)} %get-tuple-element.26), channel_id=1, source_target_pairs={{0,6},{1,7},{2,0},{3,1},{4,2},{5,3},{6,4},{7,5},{8,14},{9,15},{10,... | collective-permute-start | bytes 122888 | tf_op jit(solution)/shard_map/ppermute | solution.py:238
  7.5 7.2 %collective-permute-start = (f32[16,2048]{1,0:T(8,128)S(1)}, f32[16,2048]{1,0:T(8,128)S(1)}, u32[]{:S(2)}, u32[]{:S(2)}) collective-permute-start(f32[16,2048]{1,0:T(8,128)S(1)} %bitcast.10), channel_id=1, source_target_pairs={{0,1},{1,0},{2,3},{3,2},{4,5},{5,4},{6,7},{7,6},{8,9},{9,8},{10,11... | collective-permute-start | bytes 393224 | tf_op jit(solution)/shard_map/ppermute | solution.py:234
  14.7 2.7 %collective-permute-start.8 = (f32[4,16,640]{2,1,0:T(8,128)S(1)}, f32[4,16,640]{2,1,0:T(8,128)S(1)}, u32[]{:S(2)}, u32[]{:S(2)}) collective-permute-start(f32[4,16,640]{2,1,0:T(8,128)S(1)} %pad_maximum_fusion.sa_ref), channel_id=1, source_target_pairs={{0,1},{1,0},{2,3},{3,2},{4,5},{5,4},{6,7},{7,6},{8,9},{9,8},{10,11... | collective-permute-start | bytes 491528 | tf_op jit(solution)/shard_map/ppermute | solution.py:234
  17.4 3.3 %collective-permute-start.1 = (f32[1,4096]{1,0:T(1,128)S(1)}, f32[1,4096]{1,0:T(1,128)S(1)}, u32[]{:S(2)}, u32[]{:S(2)}) collective-permute-start(f32[1,4096]{1,0:T(1,128)S(1)} %copy-done.2), channel_id=1, source_target_pairs={{0,1},{1,0},{2,3},{3,2},{4,5},{5,4},{6,7},{7,6},{8,9},{9,8},{10,11... | collective-permute-start | bytes 49160 | tf_op jit(solution)/shard_map/ppermute | solution.py:234
  20.7 6.6 %collective-permute-done.1.other_obs_ref = f32[1,4096]{1,0:T(1,128)S(1)} collective-permute-done((f32[1,4096]{1,0:T(1,128)S(1)}, f32[1,4096]{1,0:T(1,128)S(1)}, u32[]{:S(2)}, u32[]{:S(2)}) %collective-permute-start.1) | collective-permute-done | bytes 16416 | tf_op jit(solution)/shard_map/ppermute | solution.py:234
  27.7 1.5 %collective-permute-start.3 = (f32[2,24,640]{2,1,0:T(8,128)S(1)}, f32[2,24,640]{2,1,0:T(8,128)S(1)}, u32[]{:S(2)}, u32[]{:S(2)}) collective-permute-start(f32[2,24,640]{2,1,0:T(8,128)S(1)} %get-tuple-element.21), channel_id=1, source_target_pairs={{0,4},{1,5},{2,6},{3,7},{4,0},{5,1},{6,2},{7,3},{8,12},{9,13},{10,... | collective-permute-start | bytes 368648 | tf_op jit(solution)/shard_map/ppermute | solution.py:238
  29.3 1.5 %collective-permute-start.4 = (f32[2,24,640]{2,1,0:T(8,128)S(1)}, f32[2,24,640]{2,1,0:T(8,128)S(1)}, u32[]{:S(2)}, u32[]{:S(2)}) collective-permute-start(f32[2,24,640]{2,1,0:T(8,128)S(1)} %get-tuple-element.22), channel_id=1, source_target_pairs={{0,6},{1,7},{2,0},{3,1},{4,2},{5,3},{6,4},{7,5},{8,14},{9,15},{10,... | collective-permute-start | bytes 368648 | tf_op jit(solution)/shard_map/ppermute | solution.py:238
  30.8 4.2 %collective-permute-done.2.k1 = f32[2,24,640]{2,1,0:T(8,128)S(1)} collective-permute-done((f32[2,24,640]{2,1,0:T(8,128)S(1)}, f32[2,24,640]{2,1,0:T(8,128)S(1)}, u32[]{:S(2)}, u32[]{:S(2)}) %collective-permute-start.2) | collective-permute-done | bytes 122912 | tf_op jit(solution)/shard_map/ppermute | solution.py:238
  34.9 0.9 %collective-permute-done.4.k3 = f32[2,24,640]{2,1,0:T(8,128)S(1)} collective-permute-done((f32[2,24,640]{2,1,0:T(8,128)S(1)}, f32[2,24,640]{2,1,0:T(8,128)S(1)}, u32[]{:S(2)}, u32[]{:S(2)}) %collective-permute-start.4) | collective-permute-done | bytes 122912 | tf_op jit(solution)/shard_map/ppermute | solution.py:238
  35.8 1.9 %shard_map.70 = (f32[8,16,640]{2,1,0:T(8,128)S(1)}, f32[3,8,8,640]{3,2,1,0:T(8,128)S(1)}, f32[3,8,8,640]{3,2,1,0:T(8,128)S(1)}) custom-call(s32[1,4096]{1,0:T(1,128)S(1)} %bitcast.13, f32[2,24,640]{2,1,0:T(8,128)S(1)} %get-tuple-element.19.k0, f32[2,24,640]{2,1,0:T(8,128)S(1)} %collective-permute-done.2.k1, f32[2,24,640]{2,1,0:T(8,128)S(1)} %collective-permute-done.3.k2, ...), custom_call_target="tpu_custom_call" | custom-call | flops 1000 | bytes 100000 | tf_op jit(solution)/shard_map/pallas_call | solution.py:262
  37.7 1.9 %collective-permute-start.10 = (f32[3,8,8,640]{3,2,1,0:T(8,128)S(1)}, f32[3,8,8,640]{3,2,1,0:T(8,128)S(1)}, u32[]{:S(2)}, u32[]{:S(2)}) collective-permute-start(f32[3,8,8,640]{3,2,1,0:T(8,128)S(1)} %get-tuple-element.29), channel_id=1, source_target_pairs={{8,0},{9,1},{10,2},{11,3},{12,4},{13,5},{14,6},{15,7},{16,8},{17,9... | collective-permute-start | bytes 1474568 | tf_op jit(solution)/shard_map/ppermute | solution.py:247
  39.7 2.4 %collective-permute-start.9 = (f32[3,8,8,640]{3,2,1,0:T(8,128)S(1)}, f32[3,8,8,640]{3,2,1,0:T(8,128)S(1)}, u32[]{:S(2)}, u32[]{:S(2)}) collective-permute-start(f32[3,8,8,640]{3,2,1,0:T(8,128)S(1)} %get-tuple-element.28), channel_id=1, source_target_pairs={{0,8},{1,9},{2,10},{3,11},{4,12},{5,13},{6,14},{7,15},{8,16},{9,17... | collective-permute-start | bytes 1474568 | tf_op jit(solution)/shard_map/ppermute | solution.py:247
  42.3 3.7 %collective-permute-done.10.below_ref = f32[3,8,8,640]{3,2,1,0:T(8,128)S(1)} collective-permute-done((f32[3,8,8,640]{3,2,1,0:T(8,128)S(1)}, f32[3,8,8,640]{3,2,1,0:T(8,128)S(1)}, u32[]{:S(2)}, u32[]{:S(2)}) %collective-permute-start.10) | collective-permute-done | bytes 491552 | tf_op jit(solution)/shard_map/ppermute | solution.py:247
  46.0 5.9 %collective-permute-done.9.above_ref = f32[3,8,8,640]{3,2,1,0:T(8,128)S(1)} collective-permute-done((f32[3,8,8,640]{3,2,1,0:T(8,128)S(1)}, f32[3,8,8,640]{3,2,1,0:T(8,128)S(1)}, u32[]{:S(2)}, u32[]{:S(2)}) %collective-permute-start.9) | collective-permute-done | bytes 491552 | tf_op jit(solution)/shard_map/ppermute | solution.py:247
  51.9 9.6 %shard_map.71 = (f32[2,16,512]{2,1,0:T(8,128)S(1)}, f32[2,16,512]{2,1,0:T(8,128)S(1)}, f32[2,16,512]{2,1,0:T(8,128)S(1)}, f32[2,16,512]{2,1,0:T(8,128)S(1)}) custom-call(f32[8,8]{1,0:T(8,128)S(1)} %convolution_multiply_fusion.mix_ref, f32[8,16,640]{2,1,0:T(8,128)S(1)} %get-tuple-element.27.source_ref, f32[3,8,8,640]{3,2,1,0:T(8,128)S(1)} %collective-permute-done.9.above_ref, ...), custom_call_target="tpu_custom_call" | custom-call | flops 1000 | bytes 100000 | tf_op jit(solution)/shard_map/pallas_call | solution.py:271
  61.5 0.7 %collective-permute-start.11 = (f32[2,16,512]{2,1,0:T(8,128)S(1)}, f32[2,16,512]{2,1,0:T(8,128)S(1)}, u32[]{:S(2)}, u32[]{:S(2)}) collective-permute-start(f32[2,16,512]{2,1,0:T(8,128)S(1)} %get-tuple-element.31), channel_id=1, source_target_pairs={{0,2},{1,3},{2,4},{3,5},{4,6},{5,7},{6,0},{7,1},{8,10},{9,11},{10,... | collective-permute-start | bytes 196616 | tf_op jit(solution)/shard_map/ppermute | solution.py:238
  62.2 3.1 %collective-permute-start.12 = (f32[2,16,512]{2,1,0:T(8,128)S(1)}, f32[2,16,512]{2,1,0:T(8,128)S(1)}, u32[]{:S(2)}, u32[]{:S(2)}) collective-permute-start(f32[2,16,512]{2,1,0:T(8,128)S(1)} %get-tuple-element.32), channel_id=1, source_target_pairs={{0,4},{1,5},{2,6},{3,7},{4,0},{5,1},{6,2},{7,3},{8,12},{9,13},{10,... | collective-permute-start | bytes 196616 | tf_op jit(solution)/shard_map/ppermute | solution.py:238
  65.4 1.7 %collective-permute-done.11.p1 = f32[2,16,512]{2,1,0:T(8,128)S(1)} collective-permute-done((f32[2,16,512]{2,1,0:T(8,128)S(1)}, f32[2,16,512]{2,1,0:T(8,128)S(1)}, u32[]{:S(2)}, u32[]{:S(2)}) %collective-permute-start.11) | collective-permute-done | bytes 65568 | tf_op jit(solution)/shard_map/ppermute | solution.py:238
  67.0 1.3 %collective-permute-done.12.p2 = f32[2,16,512]{2,1,0:T(8,128)S(1)} collective-permute-done((f32[2,16,512]{2,1,0:T(8,128)S(1)}, f32[2,16,512]{2,1,0:T(8,128)S(1)}, u32[]{:S(2)}, u32[]{:S(2)}) %collective-permute-start.12) | collective-permute-done | bytes 65568 | tf_op jit(solution)/shard_map/ppermute | solution.py:238
  68.3 1.3 %collective-permute-done.13.p3 = f32[2,16,512]{2,1,0:T(8,128)S(1)} collective-permute-done((f32[2,16,512]{2,1,0:T(8,128)S(1)}, f32[2,16,512]{2,1,0:T(8,128)S(1)}, u32[]{:S(2)}, u32[]{:S(2)}) %collective-permute-start.13) | collective-permute-done | bytes 65568 | tf_op jit(solution)/shard_map/ppermute | solution.py:238
  69.6 0.7 %shard_map.72 = (f32[16,2048]{1,0:T(8,128)}, f32[16,2048]{1,0:T(8,128)}) custom-call(f32[2,16,512]{2,1,0:T(8,128)S(1)} %get-tuple-element.30.p0, f32[2,16,512]{2,1,0:T(8,128)S(1)} %collective-permute-done.11.p1, f32[2,16,512]{2,1,0:T(8,128)S(1)} %collective-permute-done.12.p2, f32[2,16,512]{2,1,0:T(8,128)S(1)} %collective-permute-done.13.p3), custom_call_target="tpu_custom_call" | custom-call | flops 1000 | bytes 100000 | tf_op jit(solution)/shard_map/pallas_call | solution.py:279
  (21 shorter events, 0.6 us)
Async XLA Ops:
  0.6 0.9 %copy-start = (f32[1,16,2048]{2,1,0:T(8,128)S(1)}, f32[1,16,2048]{2,1,0:T(8,128)}, u32[]{:S(2)}) copy-start(f32[1,16,2048]{2,1,0:T(8,128)} %param.6) | copy-start | bytes 393220
  1.5 5.9 %copy-start.1 = (f32[1,16,2048]{2,1,0:T(8,128)S(1)}, f32[1,16,2048]{2,1,0:T(8,128)}, u32[]{:S(2)}) copy-start(f32[1,16,2048]{2,1,0:T(8,128)} %param.5) | copy-start | bytes 393220
  1.6 13.1 %collective-permute-start.5 = (f32[16,640]{1,0:T(8,128)S(1)}, f32[16,640]{1,0:T(8,128)S(1)}, u32[]{:S(2)}, u32[]{:S(2)}) collective-permute-start(f32[16,640]{1,0:T(8,128)S(1)} %get-tuple-element.24), channel_id=1, source_target_pairs={{0,2},{1,3},{2,4},{3,5},{4,6},{5,7},{6,0},{7,1},{8,10},{9,11},{10,... | collective-permute-start | bytes 122888 | tf_op jit(solution)/shard_map/ppermute | solution.py:238
  3.2 11.4 %collective-permute-start.6 = (f32[16,640]{1,0:T(8,128)S(1)}, f32[16,640]{1,0:T(8,128)S(1)}, u32[]{:S(2)}, u32[]{:S(2)}) collective-permute-start(f32[16,640]{1,0:T(8,128)S(1)} %get-tuple-element.25), channel_id=1, source_target_pairs={{0,4},{1,5},{2,6},{3,7},{4,0},{5,1},{6,2},{7,3},{8,12},{9,13},{10,... | collective-permute-start | bytes 122888 | tf_op jit(solution)/shard_map/ppermute | solution.py:238
  6.1 8.6 %collective-permute-start.7 = (f32[16,640]{1,0:T(8,128)S(1)}, f32[16,640]{1,0:T(8,128)S(1)}, u32[]{:S(2)}, u32[]{:S(2)}) collective-permute-start(f32[16,640]{1,0:T(8,128)S(1)} %get-tuple-element.26), channel_id=1, source_target_pairs={{0,6},{1,7},{2,0},{3,1},{4,2},{5,3},{6,4},{7,5},{8,14},{9,15},{10,... | collective-permute-start | bytes 122888 | tf_op jit(solution)/shard_map/ppermute | solution.py:238
  7.5 19.9 %collective-permute-start = (f32[16,2048]{1,0:T(8,128)S(1)}, f32[16,2048]{1,0:T(8,128)S(1)}, u32[]{:S(2)}, u32[]{:S(2)}) collective-permute-start(f32[16,2048]{1,0:T(8,128)S(1)} %bitcast.10), channel_id=1, source_target_pairs={{0,1},{1,0},{2,3},{3,2},{4,5},{5,4},{6,7},{7,6},{8,9},{9,8},{10,11... | collective-permute-start | bytes 393224 | tf_op jit(solution)/shard_map/ppermute | solution.py:234
  14.7 2.7 %copy-start.2 = (f32[1,4096]{1,0:T(1,128)S(1)}, f32[1,4096]{1,0:T(1,128)}, u32[]{:S(2)}) copy-start(f32[1,4096]{1,0:T(1,128)} %own_obs_ref.1) | copy-start | bytes 49156
  14.7 16.0 %collective-permute-start.8 = (f32[4,16,640]{2,1,0:T(8,128)S(1)}, f32[4,16,640]{2,1,0:T(8,128)S(1)}, u32[]{:S(2)}, u32[]{:S(2)}) collective-permute-start(f32[4,16,640]{2,1,0:T(8,128)S(1)} %pad_maximum_fusion.sa_ref), channel_id=1, source_target_pairs={{0,1},{1,0},{2,3},{3,2},{4,5},{5,4},{6,7},{7,6},{8,9},{9,8},{10,11... | collective-permute-start | bytes 491528 | tf_op jit(solution)/shard_map/ppermute | solution.py:234
  17.4 9.9 %collective-permute-start.1 = (f32[1,4096]{1,0:T(1,128)S(1)}, f32[1,4096]{1,0:T(1,128)S(1)}, u32[]{:S(2)}, u32[]{:S(2)}) collective-permute-start(f32[1,4096]{1,0:T(1,128)S(1)} %copy-done.2), channel_id=1, source_target_pairs={{0,1},{1,0},{2,3},{3,2},{4,5},{5,4},{6,7},{7,6},{8,9},{9,8},{10,11... | collective-permute-start | bytes 49160 | tf_op jit(solution)/shard_map/ppermute | solution.py:234
  27.4 8.5 %copy-start.3 = (s32[4096]{0:T(1024)S(1)}, s32[4096]{0:T(1024)}, u32[]{:S(2)}) copy-start(s32[4096]{0:T(1024)} %param.8) | copy-start | bytes 49156
  27.4 7.5 %collective-permute-start.2 = (f32[2,24,640]{2,1,0:T(8,128)S(1)}, f32[2,24,640]{2,1,0:T(8,128)S(1)}, u32[]{:S(2)}, u32[]{:S(2)}) collective-permute-start(f32[2,24,640]{2,1,0:T(8,128)S(1)} %get-tuple-element.20), channel_id=1, source_target_pairs={{0,2},{1,3},{2,4},{3,5},{4,6},{5,7},{6,0},{7,1},{8,10},{9,11},{10,... | collective-permute-start | bytes 368648 | tf_op jit(solution)/shard_map/ppermute | solution.py:238
  27.7 7.2 %collective-permute-start.3 = (f32[2,24,640]{2,1,0:T(8,128)S(1)}, f32[2,24,640]{2,1,0:T(8,128)S(1)}, u32[]{:S(2)}, u32[]{:S(2)}) collective-permute-start(f32[2,24,640]{2,1,0:T(8,128)S(1)} %get-tuple-element.21), channel_id=1, source_target_pairs={{0,4},{1,5},{2,6},{3,7},{4,0},{5,1},{6,2},{7,3},{8,12},{9,13},{10,... | collective-permute-start | bytes 368648 | tf_op jit(solution)/shard_map/ppermute | solution.py:238
  29.3 6.6 %collective-permute-start.4 = (f32[2,24,640]{2,1,0:T(8,128)S(1)}, f32[2,24,640]{2,1,0:T(8,128)S(1)}, u32[]{:S(2)}, u32[]{:S(2)}) collective-permute-start(f32[2,24,640]{2,1,0:T(8,128)S(1)} %get-tuple-element.22), channel_id=1, source_target_pairs={{0,6},{1,7},{2,0},{3,1},{4,2},{5,3},{6,4},{7,5},{8,14},{9,15},{10,... | collective-permute-start | bytes 368648 | tf_op jit(solution)/shard_map/ppermute | solution.py:238
  35.8 6.2 %copy-start.4 = (f32[8,8]{1,0:T(8,128)S(1)}, f32[8,8]{1,0:T(8,128)}, u32[]{:S(2)}) copy-start(f32[8,8]{1,0:T(8,128)} %param.7) | copy-start | bytes 772
  37.7 8.3 %collective-permute-start.10 = (f32[3,8,8,640]{3,2,1,0:T(8,128)S(1)}, f32[3,8,8,640]{3,2,1,0:T(8,128)S(1)}, u32[]{:S(2)}, u32[]{:S(2)}) collective-permute-start(f32[3,8,8,640]{3,2,1,0:T(8,128)S(1)} %get-tuple-element.29), channel_id=1, source_target_pairs={{8,0},{9,1},{10,2},{11,3},{12,4},{13,5},{14,6},{15,7},{16,8},{17,9... | collective-permute-start | bytes 1474568 | tf_op jit(solution)/shard_map/ppermute | solution.py:247
  39.7 12.3 %collective-permute-start.9 = (f32[3,8,8,640]{3,2,1,0:T(8,128)S(1)}, f32[3,8,8,640]{3,2,1,0:T(8,128)S(1)}, u32[]{:S(2)}, u32[]{:S(2)}) collective-permute-start(f32[3,8,8,640]{3,2,1,0:T(8,128)S(1)} %get-tuple-element.28), channel_id=1, source_target_pairs={{0,8},{1,9},{2,10},{3,11},{4,12},{5,13},{6,14},{7,15},{8,16},{9,17... | collective-permute-start | bytes 1474568 | tf_op jit(solution)/shard_map/ppermute | solution.py:247
  61.5 5.6 %collective-permute-start.11 = (f32[2,16,512]{2,1,0:T(8,128)S(1)}, f32[2,16,512]{2,1,0:T(8,128)S(1)}, u32[]{:S(2)}, u32[]{:S(2)}) collective-permute-start(f32[2,16,512]{2,1,0:T(8,128)S(1)} %get-tuple-element.31), channel_id=1, source_target_pairs={{0,2},{1,3},{2,4},{3,5},{4,6},{5,7},{6,0},{7,1},{8,10},{9,11},{10,... | collective-permute-start | bytes 196616 | tf_op jit(solution)/shard_map/ppermute | solution.py:238
  62.2 6.1 %collective-permute-start.12 = (f32[2,16,512]{2,1,0:T(8,128)S(1)}, f32[2,16,512]{2,1,0:T(8,128)S(1)}, u32[]{:S(2)}, u32[]{:S(2)}) collective-permute-start(f32[2,16,512]{2,1,0:T(8,128)S(1)} %get-tuple-element.32), channel_id=1, source_target_pairs={{0,4},{1,5},{2,6},{3,7},{4,0},{5,1},{6,2},{7,3},{8,12},{9,13},{10,... | collective-permute-start | bytes 196616 | tf_op jit(solution)/shard_map/ppermute | solution.py:238
  65.3 4.3 %collective-permute-start.13 = (f32[2,16,512]{2,1,0:T(8,128)S(1)}, f32[2,16,512]{2,1,0:T(8,128)S(1)}, u32[]{:S(2)}, u32[]{:S(2)}) collective-permute-start(f32[2,16,512]{2,1,0:T(8,128)S(1)} %get-tuple-element.33), channel_id=1, source_target_pairs={{0,6},{1,7},{2,0},{3,1},{4,2},{5,3},{6,4},{7,5},{8,14},{9,15},{10,... | collective-permute-start | bytes 196616 | tf_op jit(solution)/shard_map/ppermute | solution.py:238

commit v2 on v1

v2 whole, which is shorter than its diff:
```python
import functools

import jax
import jax.numpy as jnp
from jax import lax
from jax.experimental import pallas as pl
from jax.experimental.pallas import tpu as pltpu
from jax.sharding import PartitionSpec as P

ITERS = 4
THETA = 4.025
DELTA = 3.975
VMEM = pl.BlockSpec(memory_space=pltpu.VMEM)
SMEM = pl.BlockSpec(memory_space=pltpu.SMEM)

ROWS, COLS, VARS, GROUPS = 16, 2048, 8, 4
BLOCK = COLS // GROUPS
SIDE = 128
WIDE = BLOCK + SIDE
EDGE = 8
TALL = ROWS + 2 * EDGE
OBS = 4096
OBS_ROWS = OBS // BLOCK


def group_place():
    var = lax.axis_index("var")
    return var // 2, lax.rem(var, 2)


def ahead(y, k):
    return lax.rem(y + k, GROUPS)


def behind(y, k):
    return lax.rem(y - k + GROUPS, GROUPS)


def window(ref, block, rows):
    main = ref[rows, pl.ds(pl.multiple_of(block * BLOCK, BLOCK), BLOCK)]
    after = jnp.minimum(block + 1, GROUPS - 1) * BLOCK
    before = jnp.maximum(block * BLOCK - SIDE, 0)
    right = ref[rows, pl.ds(pl.multiple_of(after, SIDE), SIDE)]
    left = ref[rows, pl.ds(pl.multiple_of(before, SIDE), SIDE)]
    lane = lax.broadcasted_iota(jnp.int32, (8, SIDE), 1)
    return main, jnp.where(lane < SIDE // 2, right, left)


def extra_kernel(obs_ref, state_ref, extra_ref):
    for i in range(OBS_ROWS):
        extra_ref[i : i + 1, :BLOCK] = obs_ref[:, i * BLOCK : (i + 1) * BLOCK]
    for e, r in enumerate((0, ROWS - 1)):
        for block in range(GROUPS):
            for i in range(BLOCK // SIDE):
                to, at = e * (BLOCK // SIDE) + i, BLOCK + block * SIDE
                col = block * BLOCK + i * SIDE
                extra_ref[to : to + 1, at : at + SIDE] = state_ref[r : r + 1, col : col + SIDE]


def shape_kernel(kappa_ref, state_ref, shaped_ref):
    u = state_ref[...]
    row = lax.broadcasted_iota(jnp.int32, (ROWS, COLS), 0)
    lane = lax.broadcasted_iota(jnp.int32, (ROWS, COLS), 1)
    beside = jnp.where(row > 0, pltpu.roll(u, 1, 0), 0.0) + jnp.where(row < ROWS - 1, pltpu.roll(u, ROWS - 1, 0), 0.0)
    beside = beside + jnp.where(lane > 0, pltpu.roll(u, 1, 1), 0.0)
    beside = beside + jnp.where(lane < COLS - 1, pltpu.roll(u, COLS - 1, 1), 0.0)
    shaped_ref[...] = (kappa_ref[...] + 4.0) * u - beside


def pack_kernel(own_ref, other_ref, own_extra_ref, other_extra_ref, *outs):
    y, _ = group_place()
    for k in range(GROUPS):
        block = ahead(y, k)
        for slot, (ref, extra) in enumerate(((own_ref, own_extra_ref), (other_ref, other_extra_ref))):
            for r in range(0, ROWS, 8):
                main, side = window(ref, block, slice(r, r + 8))
                outs[k][slot, r : r + 8, :BLOCK] = main
                outs[k][slot, r : r + 8, BLOCK:] = side
            outs[k][slot, ROWS : ROWS + OBS_ROWS, :BLOCK] = extra[:, :BLOCK]
            outs[k][slot, ROWS : ROWS + OBS_ROWS, BLOCK:] = extra[:, pl.ds(pl.multiple_of(BLOCK + block * SIDE, SIDE), SIDE)]


def scatter_kernel(cell_ref, k0, k1, k2, k3, source_ref, near_ref, far_ref, acc):
    y, z = group_place()
    core = lax.rem(lax.axis_index("tile"), 2)
    pieces = (k0, k1, k2, k3)
    acc[...] = jnp.zeros_like(acc)
    rows = lax.broadcasted_iota(jnp.int32, (ROWS, BLOCK), 0)
    lanes = lax.broadcasted_iota(jnp.int32, (WIDE, BLOCK), 0)
    half = SIDE // 2
    for i in range(OBS_ROWS):
        cell = cell_ref[:, i * BLOCK : (i + 1) * BLOCK]
        row = lax.shift_right_logical(cell, 11)
        col = jnp.bitwise_and(cell, COLS - 1) - y * BLOCK
        place = jnp.where(
            (col >= 0) & (col < BLOCK + half), col, jnp.where((col >= -half) & (col < 0), col + WIDE, -1)
        )
        hit_row = rows == row
        hit_col = jnp.where(lanes == place, 1.0, 0.0).astype(jnp.bfloat16)
        highs, lows = [], []
        for k in range(GROUPS):
            for slot in range(2):
                value = pieces[k][slot, ROWS + i : ROWS + i + 1, :BLOCK]
                high = value.astype(jnp.bfloat16).astype(jnp.float32)
                low = value - high
                highs.append(jnp.where(hit_row, high, 0.0).astype(jnp.bfloat16))
                lows.append(jnp.where(hit_row, low, 0.0).astype(jnp.bfloat16))
        values = jnp.concatenate(highs + lows, axis=0)
        acc[...] += lax.dot_general(
            values, hit_col, (((1,), (1,)), ((), ())), preferred_element_type=jnp.float32
        )
    count = VARS * ROWS
    for k in range(GROUPS):
        for slot in range(2):
            at = (k * 2 + slot) * ROWS
            total = acc[at : at + ROWS] + acc[count + at : count + at + ROWS]
            var = 2 * behind(y, k) + lax.rem(z + slot, 2)
            source_ref[var] = total
            near, far = pl.multiple_of(EDGE * (1 - core), EDGE), pl.multiple_of(EDGE * core, EDGE)
            near_ref[var] = source_ref[var, pl.ds(near, EDGE)]
            far_ref[var] = source_ref[var, pl.ds(far, EDGE)]
            near_ref[VARS + var] = pieces[k][slot, pl.ds(near, EDGE)]
            far_ref[VARS + var] = pieces[k][slot, pl.ds(far, EDGE)]
    sub = lax.broadcasted_iota(jnp.int32, (VARS, SIDE), 0)
    for i in range(BLOCK // SIDE):
        held = []
        for e in range(2):
            row = ROWS + e * (BLOCK // SIDE) + i
            rows = jnp.zeros((VARS, SIDE), jnp.float32)
            for k in range(GROUPS):
                for slot in range(2):
                    var = 2 * behind(y, k) + lax.rem(z + slot, 2)
                    rows = jnp.where(sub == var, pieces[k][slot, row : row + 1, BLOCK:], rows)
            held.append(rows)
        near_ref[2 * VARS, :, i * SIDE : (i + 1) * SIDE] = jnp.where(core == 0, held[1], held[0])
        far_ref[2 * VARS, :, i * SIDE : (i + 1) * SIDE] = jnp.where(core == 0, held[0], held[1])
    near_ref[2 * VARS, :, BLOCK:] = jnp.zeros((EDGE, SIDE), jnp.float32)
    far_ref[2 * VARS, :, BLOCK:] = jnp.zeros((EDGE, SIDE), jnp.float32)


def share_kernel(mix_ref, own_ref, other_ref, *outs):
    y, z = group_place()
    for k in range(GROUPS):
        v = 2 * ahead(y, k) + z
        one, two = mix_ref[v, 2 * y + z], mix_ref[v, 2 * y + 1 - z]
        for r in range(0, ROWS, 8):
            outs[k][r : r + 8] = one * own_ref[r : r + 8] + two * other_ref[r : r + 8]


def shape_rows(u):
    return pltpu.roll(u, 1, 0) + pltpu.roll(u, TALL - 1, 0) + pltpu.roll(u, 1, 1) + pltpu.roll(u, WIDE - 1, 1)


def main_kernel(
    mix_ref, source_ref, near_ref, far_ref, k0, k1, k2, k3, adj, kp, res, dirn, tmp, mask_ref
):
    y, z = group_place()
    tile = lax.axis_index("tile")
    pieces = (k0, k1, k2, k3)
    row = lax.broadcasted_iota(jnp.int32, (TALL, WIDE), 0)
    lane = lax.broadcasted_iota(jnp.int32, (TALL, WIDE), 1)
    row = jnp.where(row < ROWS + EDGE, row, row - TALL) + tile * ROWS
    lane = jnp.where(lane < BLOCK + SIDE // 2, lane, lane - WIDE) + y * BLOCK
    inside = (row >= 0) & (row < ROWS * lax.axis_size("tile")) & (lane >= 0) & (lane < COLS)
    mask_ref[...] = jnp.where(inside, 1.0, 0.0)
    mask = mask_ref[...]
    for k in range(GROUPS):
        for slot in range(2):
            var = 2 * behind(y, k) + lax.rem(z + slot, 2)
            kp[var, :ROWS] = pieces[k][slot, :ROWS] + 4.0
    core = lax.rem(tile, 2)
    near, far = pl.multiple_of(ROWS + EDGE * core, EDGE), pl.multiple_of(ROWS + EDGE * (1 - core), EDGE)
    kp[:, pl.ds(near, EDGE)] = near_ref[VARS : 2 * VARS] + 4.0
    kp[:, pl.ds(far, EDGE)] = far_ref[VARS : 2 * VARS] + 4.0
    for var in range(VARS):
        kp[var] = kp[var] * mask_ref[...]
        for at, size, ref in ((0, ROWS, source_ref), (near, EDGE, near_ref), (far, EDGE, far_ref)):
            rows = pl.ds(at, size)
            part = ref[var] * mask_ref[rows]
            res[var, rows] = part
            part = part * (1.0 / THETA)
            dirn[var, rows] = part
            adj[var, rows] = part

    def shape(src, var):
        u = src[var]
        return kp[var] * u - shape_rows(u) * mask_ref[...]

    def couple(ref):
        for r in range(0, TALL, 8):
            fields = [ref[w, r : r + 8] for w in range(VARS)]
            for v in range(VARS):
                total = mix_ref[v, 0] * fields[0]
                for w in range(1, VARS):
                    total = total + mix_ref[v, w] * fields[w]
                ref[v, r : r + 8] = total

    sigma = THETA / DELTA
    rho = 1.0 / sigma
    for _ in range(ITERS - 1):
        rho_new = 1.0 / (2.0 * sigma - rho)
        c1, c2 = rho_new * rho, 2.0 * rho_new / DELTA
        rho = rho_new

        for var in range(VARS):
            tmp[var] = shape(dirn, var)
        couple(tmp)

        for var in range(VARS):
            r = res[var] - shape(tmp, var)
            res[var] = r
            d = c1 * dirn[var] + c2 * r
            dirn[var] = d
            adj[var] = adj[var] + d


def final_kernel(mix_ref, adj, kp, near_ref, far_ref, o0, o1, o2, o3, tmp):
    y, z = group_place()
    core = lax.rem(lax.axis_index("tile"), 2)

    for var in range(VARS):
        u = adj[var]
        tmp[var] = kp[var, :ROWS, :BLOCK] * u[:ROWS, :BLOCK] - shape_rows(u)[:ROWS, :BLOCK]
    for k, out in enumerate((o0, o1, o2, o3)):
        v = 2 * ahead(y, k) + z
        for c in range(0, BLOCK, 128):
            cols = slice(c, c + 128)
            near = mix_ref[v, 0] * near_ref[2 * VARS, 0:1, cols]
            far = mix_ref[v, 0] * far_ref[2 * VARS, 0:1, cols]
            for w in range(1, VARS):
                near = near + mix_ref[v, w] * near_ref[2 * VARS, w : w + 1, cols]
                far = far + mix_ref[v, w] * far_ref[2 * VARS, w : w + 1, cols]
            out[4, 0:1, cols] = jnp.where(core == 0, far, near)
            out[4, 1:2, cols] = jnp.where(core == 0, near, far)
            out[4, 2:, cols] = jnp.zeros((6, 128), jnp.float32)
            for half in range(ROWS // 8):
                rows = slice(half * 8, half * 8 + 8)
                total = mix_ref[v, 0] * tmp[0, rows, cols]
                for w in range(1, VARS):
                    total = total + mix_ref[v, w] * tmp[w, rows, cols]
                out[half, :, cols] = adj[v, rows, cols]
                out[2 + half, :, cols] = total


def join_kernel(p0, p1, p2, p3, m0, m1, m2, m3, state_ref, adjoint_ref, grad_ref):
    y, _ = group_place()
    row = lax.broadcasted_iota(jnp.int32, (8, BLOCK), 0)
    for k, part in enumerate((p0, p1, p2, p3)):
        cols = pl.ds(pl.multiple_of(behind(y, k) * BLOCK, BLOCK), BLOCK)
        for half in range(ROWS // 8):
            rows = slice(half * 8, half * 8 + 8)
            mixed = (m0[rows, cols] + m1[rows, cols]) + (m2[rows, cols] + m3[rows, cols])
            mixed = mixed - jnp.where(row == 7 * half, part[4, half : half + 1], 0.0)
            adjoint_ref[rows, cols] = part[half]
            grad_ref[rows, cols] = -(part[2 + half] * state_ref[rows, cols] + part[half] * mixed)


def call(kernel, outs, n_in, smem=0, scratch=(), flops=1000, size=100000):
    shapes = [jax.ShapeDtypeStruct(s, jnp.float32) for s in outs]
    return pl.pallas_call(
        kernel,
        out_shape=shapes,
        in_specs=[SMEM] * smem + [VMEM] * (n_in - smem),
        out_specs=[VMEM] * len(shapes),
        scratch_shapes=list(scratch),
        compiler_params=pltpu.CompilerParams(vmem_limit_bytes=32 * 1024 * 1024),
        cost_estimate=pl.CostEstimate(flops=flops, bytes_accessed=size, transcendentals=0),
    )


def across(x):
    return lax.ppermute(x, "var", [(i, i ^ 1) for i in range(VARS)])


def around(x, k):
    return lax.ppermute(x, "var", [(i, (i // 2 + k) % GROUPS * 2 + i % 2) for i in range(VARS)])


def beside(x, tiles, near):
    pairs = []
    for i in range(0 if near else 1, tiles - 1, 2):
        for v in range(VARS):
            one, two = i * VARS + v, (i + 1) * VARS + (v ^ 1 if i % 8 == 7 else v)
            pairs += [(one, two), (two, one)]
    return lax.ppermute(x, ("tile", "var"), pairs)


def per_device(tiles, range_sq, state_field, coupling, obs_cell, obs_value):
    mixing = jnp.eye(VARS, dtype=jnp.float32) + coupling
    mix = jnp.einsum("uv,uw->vw", mixing, mixing, precision=lax.Precision.HIGHEST) * (1.0 / 64.0)
    kappa, state = range_sq[0], state_field[0]
    other_kappa = across(kappa)
    (shaped,) = call(shape_kernel, [(ROWS, COLS)], 2)(kappa, state)
    (extra,) = call(extra_kernel, [(8, 2 * BLOCK)], 2)(obs_value, state)
    other_extra = across(extra)
    shaped, _ = lax.optimization_barrier((shaped, other_extra))
    other_shaped = across(shaped)
    pieces = call(pack_kernel, [(2, ROWS + OBS_ROWS, WIDE)] * 4, 4)(kappa, other_kappa, extra, other_extra)
    pieces = [pieces[0]] + [around(pieces[k], k) for k in range(1, GROUPS)]
    edges = (2 * VARS + 1, EDGE, WIDE)
    source, near, far = call(
        scatter_kernel,
        [(VARS, ROWS, WIDE), edges, edges],
        5,
        scratch=[pltpu.VMEM((2 * VARS * ROWS, WIDE), jnp.float32)],
    )(obs_cell.reshape(1, OBS), *pieces)
    far = beside(far, tiles, False)
    near = beside(near, tiles, True)
    shaped, other_shaped, _ = lax.optimization_barrier((shaped, other_shaped, source))
    mixed = call(share_kernel, [(ROWS, COLS)] * 4, 3, smem=1)(mix, shaped, other_shaped)
    mixed = [mixed[0]] + [around(mixed[k], k) for k in range(1, GROUPS)]
    field = (VARS, TALL, WIDE)
    adj, kp = call(
        main_kernel,
        [field] * 2,
        8,
        smem=1,
        scratch=[pltpu.VMEM(field, jnp.float32)] * 3 + [pltpu.VMEM((TALL, WIDE), jnp.float32)],
    )(mix, source, near, far, *pieces)
    parts = call(
        final_kernel,
        [(2 * ROWS // 8 + 1, 8, BLOCK)] * 4,
        5,
        smem=1,
        scratch=[pltpu.VMEM((VARS, ROWS, BLOCK), jnp.float32)],
    )(mix, adj, kp, near, far)
    parts = [parts[0]] + [around(parts[k], k) for k in range(1, GROUPS)]
    adjoint, grad = call(join_kernel, [(ROWS, COLS)] * 2, 9)(*parts, *mixed, state)
    return adjoint[None], grad[None]


def solution(mesh):
    return jax.shard_map(
        functools.partial(per_device, mesh.shape["tile"]),
        mesh=mesh,
        in_specs=(P("var", "tile", None), P("var", "tile", None), P(), P("tile"), P("var", "tile")),
        out_specs=(P("var", "tile", None), P("var", "tile", None)),
        check_vma=False,
    )
```

time: 70.5 us -> 56.2 us (0.80)
  starting transfers between devices: 30.6 us -> 24.8 us
  waiting for transfers between devices: 25.6 us -> 19.9 us
  Pallas kernels: 12.3 us -> 8.8 us
  local copies, waits for them, and re-layouts: 0.91 us -> 1.64 us
    ppermute x2, waiting for transfers between devices: 9.64 us -> 2.54 us  [beside(): return lax.ppermute(x, ('tile', 'var'), pairs)]
    ppermute x3, starting transfers between devices: 13.2 us -> 8.45 us  [across(): return lax.ppermute(x, 'var', [(i, i ^ 1) for i in range(VARS)])]
    ppermute x3, waiting for transfers between devices: 6.63 us -> 11.3 us  [across(): return lax.ppermute(x, 'var', [(i, i ^ 1) for i in range(VARS)])]
    pallas_call x5 -> x8, Pallas kernels: 12.3 us -> 8.8 us  [the longest x1 4.24 us: per_device(): call(main_kernel, [field] * 2, 8, smem=1, scratch=[pltpu.VMEM(field, jnp....]
    ppermute x9, waiting for transfers between devices: 9.33 us -> 6 us  [around(): lax.ppermute(x, 'var', [(i, (i // 2 + k) % GROUPS * 2 + i % 2) for i in r...]
    ppermute x2, starting transfers between devices: 4.33 us -> 2.03 us  [beside(): return lax.ppermute(x, ('tile', 'var'), pairs)]
    ppermute x9, starting transfers between devices: 13.1 us -> 14.3 us  [around(): lax.ppermute(x, 'var', [(i, (i // 2 + k) % GROUPS * 2 + i % 2) for i in r...]
    unnamed x10 -> x12, local copies, waits for them, and re-layouts: 0.91 us -> 1.64 us
  transfers between devices with their start and end apart: 14 -> 14, of which waited for: 8 -> 8; matrix products, arithmetic and copies ran while one was open for 0% -> 0% of each run, Pallas kernels for 0% -> 14%
where the time goes in v2:
time: 56.2 us; the launch traced here: 56 us
  starting transfers between devices  24.8 us (44%)
  waiting for transfers between devices  19.9 us (35%)
  Pallas kernels  8.8 us (16%)
  local copies, waits for them, and re-layouts  1.64 us (3%)
  between operations  0.72 us (1%)
    ppermute x9, starting transfers between devices, around(): lax.ppermute(x, 'var', [(i, (i // 2 + k) % GROUPS * 2 + i % 2) for i in r...  14.3 us
    ppermute x3, waiting for transfers between devices, across(): return lax.ppermute(x, 'var', [(i, i ^ 1) for i in range(VARS)])  11.3 us
    ppermute x3, starting transfers between devices, across(): return lax.ppermute(x, 'var', [(i, i ^ 1) for i in range(VARS)])  8.45 us
    ppermute x9, waiting for transfers between devices, around(): lax.ppermute(x, 'var', [(i, (i // 2 + k) % GROUPS * 2 + i % 2) for i in r...  6 us
    pallas_call x1, Pallas kernels, per_device(): call(main_kernel, [field] * 2, 8, smem=1, scratch=[pltpu.VMEM(field, jnp....  4.24 us
    ppermute x2, waiting for transfers between devices, beside(): return lax.ppermute(x, ('tile', 'var'), pairs)  2.54 us
    ppermute x2, starting transfers between devices, beside(): return lax.ppermute(x, ('tile', 'var'), pairs)  2.03 us
    pallas_call x1, Pallas kernels, per_device(): call(scatter_kernel, [(VARS, ROWS, WIDE), edges, edges], 5, scratch=[pltp...  1.91 us
  transfers between devices with their start and end apart: 14, of which 8 were waited for; matrix products, arithmetic and copies ran while one was open for 0% of the time, Pallas kernels for 14%

profile of v2, /device:TPU:2, one launch (start us, length us, event | category | flops | bytes accessed | tf_op | source)
XLA Modules:
  0.0 56.0 jit_solution(2211181271357573102)
XLA Ops:
  0.6 7.3 %collective-permute-start = (f32[16,2048]{1,0:T(8,128)}, f32[16,2048]{1,0:T(8,128)S(1)}, u32[]{:S(2)}, u32[]{:S(2)}) collective-permute-start(f32[16,2048]{1,0:T(8,128)} %bitcast.8), channel_id=1, source_target_pairs={{0,1},{1,0},{2,3},{3,2},{4,5},{5,4},{6,7},{7,6},{8,9},{9,8},{10,11... | collective-permute-start | bytes 393224 | tf_op jit(solution)/shard_map/ppermute | solution.py:272
  7.9 0.9 %copy-done = f32[1,16,2048]{2,1,0:T(8,128)S(1)} copy-done((f32[1,16,2048]{2,1,0:T(8,128)S(1)}, f32[1,16,2048]{2,1,0:T(8,128)}, u32[]{:S(2)}) %copy-start) | copy-done | bytes 131096
  9.7 9.5 %collective-permute-done.1.other_extra_ref = f32[8,1024]{1,0:T(8,128)S(1)} collective-permute-done((f32[8,1024]{1,0:T(8,128)S(1)}, f32[8,1024]{1,0:T(8,128)S(1)}, u32[]{:S(2)}, u32[]{:S(2)}) %collective-permute-start.1) | collective-permute-done | bytes 32800 | tf_op jit(solution)/shard_map/ppermute | solution.py:272
  19.3 1.7 %collective-permute-start.2 = (f32[2,24,640]{2,1,0:T(8,128)S(1)}, f32[2,24,640]{2,1,0:T(8,128)S(1)}, u32[]{:S(2)}, u32[]{:S(2)}) collective-permute-start(f32[2,24,640]{2,1,0:T(8,128)S(1)} %get-tuple-element.25), channel_id=1, source_target_pairs={{0,2},{1,3},{2,4},{3,5},{4,6},{5,7},{6,0},{7,1},{8,10},{9,11},{10,... | collective-permute-start | bytes 368648 | tf_op jit(solution)/shard_map/ppermute | solution.py:276
  20.9 2.9 %collective-permute-start.3 = (f32[2,24,640]{2,1,0:T(8,128)S(1)}, f32[2,24,640]{2,1,0:T(8,128)S(1)}, u32[]{:S(2)}, u32[]{:S(2)}) collective-permute-start(f32[2,24,640]{2,1,0:T(8,128)S(1)} %get-tuple-element.26), channel_id=1, source_target_pairs={{0,4},{1,5},{2,6},{3,7},{4,0},{5,1},{6,2},{7,3},{8,12},{9,13},{10,... | collective-permute-start | bytes 368648 | tf_op jit(solution)/shard_map/ppermute | solution.py:276
  23.8 1.3 %collective-permute-start.4 = (f32[2,24,640]{2,1,0:T(8,128)S(1)}, f32[2,24,640]{2,1,0:T(8,128)S(1)}, u32[]{:S(2)}, u32[]{:S(2)}) collective-permute-start(f32[2,24,640]{2,1,0:T(8,128)S(1)} %get-tuple-element.27), channel_id=1, source_target_pairs={{0,6},{1,7},{2,0},{3,1},{4,2},{5,3},{6,4},{7,5},{8,14},{9,15},{10,... | collective-permute-start | bytes 368648 | tf_op jit(solution)/shard_map/ppermute | solution.py:276
  25.3 1.1 %collective-permute-start.10 = (f32[16,2048]{1,0:T(8,128)S(1)}, f32[16,2048]{1,0:T(8,128)S(1)}, u32[]{:S(2)}, u32[]{:S(2)}) collective-permute-start(f32[16,2048]{1,0:T(8,128)S(1)} %shard_map.73.own_ref), channel_id=1, source_target_pairs={{0,1},{1,0},{2,3},{3,2},{4,5},{5,4},{6,7},{7,6},{8,9},{9,8},{10,11... | collective-permute-start | bytes 393224 | tf_op jit(solution)/shard_map/ppermute | solution.py:272
  26.4 1.6 %collective-permute-done.3.k2 = f32[2,24,640]{2,1,0:T(8,128)S(1)} collective-permute-done((f32[2,24,640]{2,1,0:T(8,128)S(1)}, f32[2,24,640]{2,1,0:T(8,128)S(1)}, u32[]{:S(2)}, u32[]{:S(2)}) %collective-permute-start.3) | collective-permute-done | bytes 122912 | tf_op jit(solution)/shard_map/ppermute | solution.py:276
  28.7 1.9 %shard_map.70 = (f32[8,16,640]{2,1,0:T(8,128)S(1)}, f32[17,8,640]{2,1,0:T(8,128)S(1)}, f32[17,8,640]{2,1,0:T(8,128)S(1)}) custom-call(s32[1,4096]{1,0:T(1,128)S(1)} %bitcast.11, f32[2,24,640]{2,1,0:T(8,128)S(1)} %get-tuple-element.24.k0, f32[2,24,640]{2,1,0:T(8,128)S(1)} %collective-permute-done.2.k1, f32[2,24,640]{2,1,0:T(8,128)S(1)} %collective-permute-done.3.k2, ...), custom_call_target="tpu_custom_call" | custom-call | flops 1000 | bytes 100000 | tf_op jit(solution)/shard_map/pallas_call | solution.py:301
  30.7 1.9 %collective-permute-start.6 = (f32[17,8,640]{2,1,0:T(8,128)S(1)}, f32[17,8,640]{2,1,0:T(8,128)S(1)}, u32[]{:S(2)}, u32[]{:S(2)}) collective-permute-start(f32[17,8,640]{2,1,0:T(8,128)S(1)} %get-tuple-element.30), channel_id=1, source_target_pairs={{8,16},{16,8},{9,17},{17,9},{10,18},{18,10},{11,19},{19,11},{12,20... | collective-permute-start | bytes 1044488 | tf_op jit(solution)/shard_map/ppermute | solution.py:285
  32.9 1.8 %collective-permute-done.10.other_ref = f32[16,2048]{1,0:T(8,128)S(1)} collective-permute-done((f32[16,2048]{1,0:T(8,128)S(1)}, f32[16,2048]{1,0:T(8,128)S(1)}, u32[]{:S(2)}, u32[]{:S(2)}) %collective-permute-start.10) | collective-permute-done | bytes 131104 | tf_op jit(solution)/shard_map/ppermute | solution.py:272
  35.4 0.8 %collective-permute-start.11 = (f32[16,2048]{1,0:T(8,128)S(1)}, f32[16,2048]{1,0:T(8,128)S(1)}, u32[]{:S(2)}, u32[]{:S(2)}) collective-permute-start(f32[16,2048]{1,0:T(8,128)S(1)} %get-tuple-element.41), channel_id=1, source_target_pairs={{0,2},{1,3},{2,4},{3,5},{4,6},{5,7},{6,0},{7,1},{8,10},{9,11},{10,... | collective-permute-start | bytes 393224 | tf_op jit(solution)/shard_map/ppermute | solution.py:276
  36.1 1.5 %collective-permute-start.12 = (f32[16,2048]{1,0:T(8,128)S(1)}, f32[16,2048]{1,0:T(8,128)S(1)}, u32[]{:S(2)}, u32[]{:S(2)}) collective-permute-start(f32[16,2048]{1,0:T(8,128)S(1)} %get-tuple-element.42), channel_id=1, source_target_pairs={{0,4},{1,5},{2,6},{3,7},{4,0},{5,1},{6,2},{7,3},{8,12},{9,13},{10,... | collective-permute-start | bytes 393224 | tf_op jit(solution)/shard_map/ppermute | solution.py:276
  37.7 1.2 %collective-permute-start.13 = (f32[16,2048]{1,0:T(8,128)S(1)}, f32[16,2048]{1,0:T(8,128)S(1)}, u32[]{:S(2)}, u32[]{:S(2)}) collective-permute-start(f32[16,2048]{1,0:T(8,128)S(1)} %get-tuple-element.43), channel_id=1, source_target_pairs={{0,6},{1,7},{2,0},{3,1},{4,2},{5,3},{6,4},{7,5},{8,14},{9,15},{10,... | collective-permute-start | bytes 393224 | tf_op jit(solution)/shard_map/ppermute | solution.py:276
  38.9 2.5 %collective-permute-done.6.far_ref = f32[17,8,640]{2,1,0:T(8,128)S(1)} collective-permute-done((f32[17,8,640]{2,1,0:T(8,128)S(1)}, f32[17,8,640]{2,1,0:T(8,128)S(1)}, u32[]{:S(2)}, u32[]{:S(2)}) %collective-permute-start.6) | collective-permute-done | bytes 348192 | tf_op jit(solution)/shard_map/ppermute | solution.py:285
  41.4 4.2 %shard_map.71 = (f32[8,32,640]{2,1,0:T(8,128)S(1)}, f32[8,32,640]{2,1,0:T(8,128)S(1)}) custom-call(f32[8,8]{1,0:T(8,128)S(1)} %convolution_multiply_fusion.mix_ref, f32[8,16,640]{2,1,0:T(8,128)S(1)} %get-tuple-element.28.source_ref, f32[17,8,640]{2,1,0:T(8,128)S(1)} %collective-permute-done.5.near_ref, f32[17,8,640]{2,1,0:T(8,128)S(1)} %collective-permute-done.6.far_ref, ...), custom_call_target="tpu_custom_call" | custom-call | flops 1000 | bytes 100000 | tf_op jit(solution)/shard_map/pallas_call | solution.py:313
  45.7 1.0 %shard_map.72 = (f32[5,8,512]{2,1,0:T(8,128)S(1)}, f32[5,8,512]{2,1,0:T(8,128)S(1)}, f32[5,8,512]{2,1,0:T(8,128)S(1)}, f32[5,8,512]{2,1,0:T(8,128)S(1)}) custom-call(f32[8,8]{1,0:T(8,128)S(1)} %convolution_multiply_fusion.mix_ref, f32[8,32,640]{2,1,0:T(8,128)S(1)} %get-tuple-element.31.adj, f32[8,32,640]{2,1,0:T(8,128)S(1)} %get-tuple-element.32.kp, ...), custom_call_target="tpu_custom_call" | custom-call | flops 1000 | bytes 100000 | tf_op jit(solution)/shard_map/pallas_call | solution.py:320
  46.7 1.0 %collective-permute-start.7 = (f32[5,8,512]{2,1,0:T(8,128)S(1)}, f32[5,8,512]{2,1,0:T(8,128)S(1)}, u32[]{:S(2)}, u32[]{:S(2)}) collective-permute-start(f32[5,8,512]{2,1,0:T(8,128)S(1)} %get-tuple-element.34), channel_id=1, source_target_pairs={{0,2},{1,3},{2,4},{3,5},{4,6},{5,7},{6,0},{7,1},{8,10},{9,11},{10,... | collective-permute-start | bytes 245768 | tf_op jit(solution)/shard_map/ppermute | solution.py:276
  47.7 3.1 %collective-permute-start.8 = (f32[5,8,512]{2,1,0:T(8,128)S(1)}, f32[5,8,512]{2,1,0:T(8,128)S(1)}, u32[]{:S(2)}, u32[]{:S(2)}) collective-permute-start(f32[5,8,512]{2,1,0:T(8,128)S(1)} %get-tuple-element.35), channel_id=1, source_target_pairs={{0,4},{1,5},{2,6},{3,7},{4,0},{5,1},{6,2},{7,3},{8,12},{9,13},{10,... | collective-permute-start | bytes 245768 | tf_op jit(solution)/shard_map/ppermute | solution.py:276
  50.8 0.8 %collective-permute-start.9 = (f32[5,8,512]{2,1,0:T(8,128)S(1)}, f32[5,8,512]{2,1,0:T(8,128)S(1)}, u32[]{:S(2)}, u32[]{:S(2)}) collective-permute-start(f32[5,8,512]{2,1,0:T(8,128)S(1)} %get-tuple-element.36), channel_id=1, source_target_pairs={{0,6},{1,7},{2,0},{3,1},{4,2},{5,3},{6,4},{7,5},{8,14},{9,15},{10,... | collective-permute-start | bytes 245768 | tf_op jit(solution)/shard_map/ppermute | solution.py:276
  51.5 1.1 %collective-permute-done.7.p1 = f32[5,8,512]{2,1,0:T(8,128)S(1)} collective-permute-done((f32[5,8,512]{2,1,0:T(8,128)S(1)}, f32[5,8,512]{2,1,0:T(8,128)S(1)}, u32[]{:S(2)}, u32[]{:S(2)}) %collective-permute-start.7) | collective-permute-done | bytes 81952 | tf_op jit(solution)/shard_map/ppermute | solution.py:276
  52.7 1.4 %collective-permute-done.8.p2 = f32[5,8,512]{2,1,0:T(8,128)S(1)} collective-permute-done((f32[5,8,512]{2,1,0:T(8,128)S(1)}, f32[5,8,512]{2,1,0:T(8,128)S(1)}, u32[]{:S(2)}, u32[]{:S(2)}) %collective-permute-start.8) | collective-permute-done | bytes 81952 | tf_op jit(solution)/shard_map/ppermute | solution.py:276
  54.1 1.2 %collective-permute-done.9.p3 = f32[5,8,512]{2,1,0:T(8,128)S(1)} collective-permute-done((f32[5,8,512]{2,1,0:T(8,128)S(1)}, f32[5,8,512]{2,1,0:T(8,128)S(1)}, u32[]{:S(2)}, u32[]{:S(2)}) %collective-permute-start.9) | collective-permute-done | bytes 81952 | tf_op jit(solution)/shard_map/ppermute | solution.py:276
  55.2 0.8 %shard_map.75 = (f32[16,2048]{1,0:T(8,128)}, f32[16,2048]{1,0:T(8,128)}) custom-call(f32[5,8,512]{2,1,0:T(8,128)S(1)} %get-tuple-element.33.p0, f32[5,8,512]{2,1,0:T(8,128)S(1)} %collective-permute-done.7.p1, f32[5,8,512]{2,1,0:T(8,128)S(1)} %collective-permute-done.8.p2, f32[5,8,512]{2,1,0:T(8,128)S(1)} %collective-permute-done.9.p3, ...), custom_call_target="tpu_custom_call" | custom-call | flops 1000 | bytes 100000 | tf_op jit(solution)/shard_map/pallas_call | solution.py:328
  (25 shorter events, 2.7 us)
Async XLA Ops:
  0.6 18.6 %collective-permute-start = (f32[16,2048]{1,0:T(8,128)}, f32[16,2048]{1,0:T(8,128)S(1)}, u32[]{:S(2)}, u32[]{:S(2)}) collective-permute-start(f32[16,2048]{1,0:T(8,128)} %bitcast.8), channel_id=1, source_target_pairs={{0,1},{1,0},{2,3},{3,2},{4,5},{5,4},{6,7},{7,6},{8,9},{9,8},{10,11... | collective-permute-start | bytes 393224 | tf_op jit(solution)/shard_map/ppermute | solution.py:272
  7.9 0.9 %copy-start = (f32[1,16,2048]{2,1,0:T(8,128)S(1)}, f32[1,16,2048]{2,1,0:T(8,128)}, u32[]{:S(2)}) copy-start(f32[1,16,2048]{2,1,0:T(8,128)} %param.6) | copy-start | bytes 393220
  8.8 0.7 %copy-start.4 = (f32[1,4096]{1,0:T(1,128)S(1)}, f32[1,4096]{1,0:T(1,128)}, u32[]{:S(2)}) copy-start(f32[1,4096]{1,0:T(1,128)} %obs_ref.1) | copy-start | bytes 49156
  9.5 9.7 %copy-start.2 = (f32[1,16,2048]{2,1,0:T(8,128)S(1)}, f32[1,16,2048]{2,1,0:T(8,128)}, u32[]{:S(2)}) copy-start(f32[1,16,2048]{2,1,0:T(8,128)} %param.5) | copy-start | bytes 393220
  9.5 15.6 %copy-start.1 = (f32[1,16,2048]{2,1,0:T(8,128)S(1)}, f32[1,16,2048]{2,1,0:T(8,128)}, u32[]{:S(2)}) copy-start(f32[1,16,2048]{2,1,0:T(8,128)} %param.6) | copy-start | bytes 393220
  9.6 9.6 %collective-permute-start.1 = (f32[8,1024]{1,0:T(8,128)S(1)}, f32[8,1024]{1,0:T(8,128)S(1)}, u32[]{:S(2)}, u32[]{:S(2)}) collective-permute-start(f32[8,1024]{1,0:T(8,128)S(1)} %shard_map.68.own_extra_ref), channel_id=1, source_target_pairs={{0,1},{1,0},{2,3},{3,2},{4,5},{5,4},{6,7},{7,6},{8,9},{9,8},{10,11... | collective-permute-start | bytes 98312 | tf_op jit(solution)/shard_map/ppermute | solution.py:272
  19.3 7.1 %collective-permute-start.2 = (f32[2,24,640]{2,1,0:T(8,128)S(1)}, f32[2,24,640]{2,1,0:T(8,128)S(1)}, u32[]{:S(2)}, u32[]{:S(2)}) collective-permute-start(f32[2,24,640]{2,1,0:T(8,128)S(1)} %get-tuple-element.25), channel_id=1, source_target_pairs={{0,2},{1,3},{2,4},{3,5},{4,6},{5,7},{6,0},{7,1},{8,10},{9,11},{10,... | collective-permute-start | bytes 368648 | tf_op jit(solution)/shard_map/ppermute | solution.py:276
  20.9 7.1 %collective-permute-start.3 = (f32[2,24,640]{2,1,0:T(8,128)S(1)}, f32[2,24,640]{2,1,0:T(8,128)S(1)}, u32[]{:S(2)}, u32[]{:S(2)}) collective-permute-start(f32[2,24,640]{2,1,0:T(8,128)S(1)} %get-tuple-element.26), channel_id=1, source_target_pairs={{0,4},{1,5},{2,6},{3,7},{4,0},{5,1},{6,2},{7,3},{8,12},{9,13},{10,... | collective-permute-start | bytes 368648 | tf_op jit(solution)/shard_map/ppermute | solution.py:276
  23.8 4.9 %copy-start.3 = (s32[4096]{0:T(1024)S(1)}, s32[4096]{0:T(1024)}, u32[]{:S(2)}) copy-start(s32[4096]{0:T(1024)} %param.8) | copy-start | bytes 49156
  23.8 4.9 %collective-permute-start.4 = (f32[2,24,640]{2,1,0:T(8,128)S(1)}, f32[2,24,640]{2,1,0:T(8,128)S(1)}, u32[]{:S(2)}, u32[]{:S(2)}) collective-permute-start(f32[2,24,640]{2,1,0:T(8,128)S(1)} %get-tuple-element.27), channel_id=1, source_target_pairs={{0,6},{1,7},{2,0},{3,1},{4,2},{5,3},{6,4},{7,5},{8,14},{9,15},{10,... | collective-permute-start | bytes 368648 | tf_op jit(solution)/shard_map/ppermute | solution.py:276
  25.3 9.4 %collective-permute-start.10 = (f32[16,2048]{1,0:T(8,128)S(1)}, f32[16,2048]{1,0:T(8,128)S(1)}, u32[]{:S(2)}, u32[]{:S(2)}) collective-permute-start(f32[16,2048]{1,0:T(8,128)S(1)} %shard_map.73.own_ref), channel_id=1, source_target_pairs={{0,1},{1,0},{2,3},{3,2},{4,5},{5,4},{6,7},{7,6},{8,9},{9,8},{10,11... | collective-permute-start | bytes 393224 | tf_op jit(solution)/shard_map/ppermute | solution.py:272
  28.7 4.0 %copy-start.5 = (f32[8,8]{1,0:T(8,128)S(1)}, f32[8,8]{1,0:T(8,128)}, u32[]{:S(2)}) copy-start(f32[8,8]{1,0:T(8,128)} %param.7) | copy-start | bytes 772
  30.6 8.3 %collective-permute-start.5 = (f32[17,8,640]{2,1,0:T(8,128)S(1)}, f32[17,8,640]{2,1,0:T(8,128)S(1)}, u32[]{:S(2)}, u32[]{:S(2)}) collective-permute-start(f32[17,8,640]{2,1,0:T(8,128)S(1)} %get-tuple-element.29), channel_id=1, source_target_pairs={{0,8},{8,0},{1,9},{9,1},{2,10},{10,2},{3,11},{11,3},{4,12},{12,4},... | collective-permute-start | bytes 1044488 | tf_op jit(solution)/shard_map/ppermute | solution.py:285
  30.7 10.7 %collective-permute-start.6 = (f32[17,8,640]{2,1,0:T(8,128)S(1)}, f32[17,8,640]{2,1,0:T(8,128)S(1)}, u32[]{:S(2)}, u32[]{:S(2)}) collective-permute-start(f32[17,8,640]{2,1,0:T(8,128)S(1)} %get-tuple-element.30), channel_id=1, source_target_pairs={{8,16},{16,8},{9,17},{17,9},{10,18},{18,10},{11,19},{19,11},{12,20... | collective-permute-start | bytes 1044488 | tf_op jit(solution)/shard_map/ppermute | solution.py:285
  35.4 15.4 %collective-permute-start.11 = (f32[16,2048]{1,0:T(8,128)S(1)}, f32[16,2048]{1,0:T(8,128)S(1)}, u32[]{:S(2)}, u32[]{:S(2)}) collective-permute-start(f32[16,2048]{1,0:T(8,128)S(1)} %get-tuple-element.41), channel_id=1, source_target_pairs={{0,2},{1,3},{2,4},{3,5},{4,6},{5,7},{6,0},{7,1},{8,10},{9,11},{10,... | collective-permute-start | bytes 393224 | tf_op jit(solution)/shard_map/ppermute | solution.py:276
  36.1 15.4 %collective-permute-start.12 = (f32[16,2048]{1,0:T(8,128)S(1)}, f32[16,2048]{1,0:T(8,128)S(1)}, u32[]{:S(2)}, u32[]{:S(2)}) collective-permute-start(f32[16,2048]{1,0:T(8,128)S(1)} %get-tuple-element.42), channel_id=1, source_target_pairs={{0,4},{1,5},{2,6},{3,7},{4,0},{5,1},{6,2},{7,3},{8,12},{9,13},{10,... | collective-permute-start | bytes 393224 | tf_op jit(solution)/shard_map/ppermute | solution.py:276
  37.7 13.9 %collective-permute-start.13 = (f32[16,2048]{1,0:T(8,128)S(1)}, f32[16,2048]{1,0:T(8,128)S(1)}, u32[]{:S(2)}, u32[]{:S(2)}) collective-permute-start(f32[16,2048]{1,0:T(8,128)S(1)} %get-tuple-element.43), channel_id=1, source_target_pairs={{0,6},{1,7},{2,0},{3,1},{4,2},{5,3},{6,4},{7,5},{8,14},{9,15},{10,... | collective-permute-start | bytes 393224 | tf_op jit(solution)/shard_map/ppermute | solution.py:276
  46.7 6.0 %collective-permute-start.7 = (f32[5,8,512]{2,1,0:T(8,128)S(1)}, f32[5,8,512]{2,1,0:T(8,128)S(1)}, u32[]{:S(2)}, u32[]{:S(2)}) collective-permute-start(f32[5,8,512]{2,1,0:T(8,128)S(1)} %get-tuple-element.34), channel_id=1, source_target_pairs={{0,2},{1,3},{2,4},{3,5},{4,6},{5,7},{6,0},{7,1},{8,10},{9,11},{10,... | collective-permute-start | bytes 245768 | tf_op jit(solution)/shard_map/ppermute | solution.py:276
  47.7 6.4 %collective-permute-start.8 = (f32[5,8,512]{2,1,0:T(8,128)S(1)}, f32[5,8,512]{2,1,0:T(8,128)S(1)}, u32[]{:S(2)}, u32[]{:S(2)}) collective-permute-start(f32[5,8,512]{2,1,0:T(8,128)S(1)} %get-tuple-element.35), channel_id=1, source_target_pairs={{0,4},{1,5},{2,6},{3,7},{4,0},{5,1},{6,2},{7,3},{8,12},{9,13},{10,... | collective-permute-start | bytes 245768 | tf_op jit(solution)/shard_map/ppermute | solution.py:276
  50.8 4.4 %collective-permute-start.9 = (f32[5,8,512]{2,1,0:T(8,128)S(1)}, f32[5,8,512]{2,1,0:T(8,128)S(1)}, u32[]{:S(2)}, u32[]{:S(2)}) collective-permute-start(f32[5,8,512]{2,1,0:T(8,128)S(1)} %get-tuple-element.36), channel_id=1, source_target_pairs={{0,6},{1,7},{2,0},{3,1},{4,2},{5,3},{6,4},{7,5},{8,14},{9,15},{10,... | collective-permute-start | bytes 245768 | tf_op jit(solution)/shard_map/ppermute | solution.py:276

commit v3 on v2

--- a/solution.py
+++ b/solution.py
@@ -21,11 +21,34 @@
 TALL = ROWS + 2 * EDGE
 OBS = 4096
 OBS_ROWS = OBS // BLOCK
+SLIM = 16
+P_OBS = 4 * BLOCK
+P_STATE = P_OBS + 2 * BLOCK
+P_SIDE = P_STATE + 2 * SIDE
+PIECE = P_SIDE + SIDE
+E_SOURCE = VARS * BLOCK
+E_SIDE = 2 * VARS * BLOCK
+E_STATE = E_SIDE + 2 * SIDE
+EDGES = E_STATE + BLOCK
 
 
 def group_place():
     var = lax.axis_index("var")
     return var // 2, lax.rem(var, 2)
+
+
+def pack_side(packed, side, index):
+    lane = lax.broadcasted_iota(jnp.int32, (8, SIDE), 1)
+    here = (lane >= SLIM * index) & (lane < SLIM * index + SLIM)
+    return jnp.where(here, pltpu.roll(side, lax.rem(SLIM * index + SLIM // 2, SIDE), 1), packed)
+
+
+def unpack_side(packed, index):
+    return pltpu.roll(packed, lax.rem(2 * SIDE - SLIM // 2 - SLIM * index, SIDE), 1)
+
+
+def lanes_at(start, size):
+    return pl.ds(pl.multiple_of(start, SIDE), size)
 
 
 def ahead(y, k):
@@ -71,13 +94,17 @@
     y, _ = group_place()
     for k in range(GROUPS):
         block = ahead(y, k)
+        packed = jnp.zeros((8, SIDE), jnp.float32)
         for slot, (ref, extra) in enumerate(((own_ref, own_extra_ref), (other_ref, other_extra_ref))):
-            for r in range(0, ROWS, 8):
-                main, side = window(ref, block, slice(r, r + 8))
-                outs[k][slot, r : r + 8, :BLOCK] = main
-                outs[k][slot, r : r + 8, BLOCK:] = side
-            outs[k][slot, ROWS : ROWS + OBS_ROWS, :BLOCK] = extra[:, :BLOCK]
-            outs[k][slot, ROWS : ROWS + OBS_ROWS, BLOCK:] = extra[:, pl.ds(pl.multiple_of(BLOCK + block * SIDE, SIDE), SIDE)]
+            for half in range(ROWS // 8):
+                main, side = window(ref, block, slice(half * 8, half * 8 + 8))
+                index = slot * 2 + half
+                outs[k][:, index * BLOCK : (index + 1) * BLOCK] = main
+                packed = pack_side(packed, side, index)
+            outs[k][:, P_OBS + slot * BLOCK : P_OBS + (slot + 1) * BLOCK] = extra[:, :BLOCK]
+            state = extra[:, lanes_at(BLOCK + block * SIDE, SIDE)]
+            outs[k][:, P_STATE + slot * SIDE : P_STATE + (slot + 1) * SIDE] = state
+        outs[k][:, P_SIDE:] = packed
 
 
 def scatter_kernel(cell_ref, k0, k1, k2, k3, source_ref, near_ref, far_ref, acc):
@@ -100,7 +127,7 @@
         highs, lows = [], []
         for k in range(GROUPS):
             for slot in range(2):
-                value = pieces[k][slot, ROWS + i : ROWS + i + 1, :BLOCK]
+                value = pieces[k][i : i + 1, P_OBS + slot * BLOCK : P_OBS + (slot + 1) * BLOCK]
                 high = value.astype(jnp.bfloat16).astype(jnp.float32)
                 low = value - high
                 highs.append(jnp.where(hit_row, high, 0.0).astype(jnp.bfloat16))
@@ -116,26 +143,35 @@
             total = acc[at : at + ROWS] + acc[count + at : count + at + ROWS]
             var = 2 * behind(y, k) + lax.rem(z + slot, 2)
             source_ref[var] = total
-            near, far = pl.multiple_of(EDGE * (1 - core), EDGE), pl.multiple_of(EDGE * core, EDGE)
-            near_ref[var] = source_ref[var, pl.ds(near, EDGE)]
-            far_ref[var] = source_ref[var, pl.ds(far, EDGE)]
-            near_ref[VARS + var] = pieces[k][slot, pl.ds(near, EDGE)]
-            far_ref[VARS + var] = pieces[k][slot, pl.ds(far, EDGE)]
+    for ref, last in ((near_ref, 1 - core), (far_ref, core)):
+        packed_kappa = packed_source = jnp.zeros((8, SIDE), jnp.float32)
+        for k in range(GROUPS):
+            for slot in range(2):
+                var = 2 * behind(y, k) + lax.rem(z + slot, 2)
+                kappa = pieces[k][:, lanes_at((slot * 2 + last) * BLOCK, BLOCK)]
+                ref[:, lanes_at(var * BLOCK, BLOCK)] = kappa
+                side = unpack_side(pieces[k][:, P_SIDE:], slot * 2 + last)
+                packed_kappa = pack_side(packed_kappa, side, var)
+                total = source_ref[var, pl.ds(pl.multiple_of(EDGE * last, EDGE), EDGE)]
+                ref[:, lanes_at(E_SOURCE + var * BLOCK, BLOCK)] = total[:, :BLOCK]
+                packed_source = pack_side(packed_source, total[:, BLOCK:], var)
+        ref[:, E_SIDE : E_SIDE + SIDE] = packed_kappa
+        ref[:, E_SIDE + SIDE : E_STATE] = packed_source
     sub = lax.broadcasted_iota(jnp.int32, (VARS, SIDE), 0)
     for i in range(BLOCK // SIDE):
         held = []
         for e in range(2):
-            row = ROWS + e * (BLOCK // SIDE) + i
+            row = e * (BLOCK // SIDE) + i
             rows = jnp.zeros((VARS, SIDE), jnp.float32)
             for k in range(GROUPS):
                 for slot in range(2):
                     var = 2 * behind(y, k) + lax.rem(z + slot, 2)
-                    rows = jnp.where(sub == var, pieces[k][slot, row : row + 1, BLOCK:], rows)
+                    at = P_STATE + slot * SIDE
+                    rows = jnp.where(sub == var, pieces[k][row : row + 1, at : at + SIDE], rows)
             held.append(rows)
-        near_ref[2 * VARS, :, i * SIDE : (i + 1) * SIDE] = jnp.where(core == 0, held[1], held[0])
-        far_ref[2 * VARS, :, i * SIDE : (i + 1) * SIDE] = jnp.where(core == 0, held[0], held[1])
-    near_ref[2 * VARS, :, BLOCK:] = jnp.zeros((EDGE, SIDE), jnp.float32)
-    far_ref[2 * VARS, :, BLOCK:] = jnp.zeros((EDGE, SIDE), jnp.float32)
+        here = slice(E_STATE + i * SIDE, E_STATE + (i + 1) * SIDE)
+        near_ref[:, here] = jnp.where(core == 0, held[1], held[0])
+        far_ref[:, here] = jnp.where(core == 0, held[0], held[1])
 
 
 def share_kernel(mix_ref, own_ref, other_ref, *outs):
@@ -152,7 +188,7 @@
 
 
 def main_kernel(
-    mix_ref, source_ref, near_ref, far_ref, k0, k1, k2, k3, adj, kp, res, dirn, tmp, mask_ref
+    mix_ref, source_ref, near_ref, far_ref, k0, k1, k2, k3, o0, o1, o2, o3, adj, kp, res, dirn, tmp, mask_ref
 ):
     y, z = group_place()
     tile = lax.axis_index("tile")
@@ -163,24 +199,35 @@
     lane = jnp.where(lane < BLOCK + SIDE // 2, lane, lane - WIDE) + y * BLOCK
     inside = (row >= 0) & (row < ROWS * lax.axis_size("tile")) & (lane >= 0) & (lane < COLS)
     mask_ref[...] = jnp.where(inside, 1.0, 0.0)
-    mask = mask_ref[...]
     for k in range(GROUPS):
         for slot in range(2):
             var = 2 * behind(y, k) + lax.rem(z + slot, 2)
-            kp[var, :ROWS] = pieces[k][slot, :ROWS] + 4.0
+            for half in range(ROWS // 8):
+                rows, index = slice(half * 8, half * 8 + 8), slot * 2 + half
+                mask = mask_ref[rows]
+                kappa = pieces[k][:, index * BLOCK : (index + 1) * BLOCK]
+                kp[var, rows, :BLOCK] = (kappa + 4.0) * mask[:, :BLOCK]
+                kp[var, rows, BLOCK:] = (unpack_side(pieces[k][:, P_SIDE:], index) + 4.0) * mask[:, BLOCK:]
     core = lax.rem(tile, 2)
-    near, far = pl.multiple_of(ROWS + EDGE * core, EDGE), pl.multiple_of(ROWS + EDGE * (1 - core), EDGE)
-    kp[:, pl.ds(near, EDGE)] = near_ref[VARS : 2 * VARS] + 4.0
-    kp[:, pl.ds(far, EDGE)] = far_ref[VARS : 2 * VARS] + 4.0
+
+    def start(var, rows, cols, part):
+        res[var, rows, cols] = part
+        part = part * (1.0 / THETA)
+        dirn[var, rows, cols] = part
+        adj[var, rows, cols] = part
+
+    main, edge = slice(0, BLOCK), slice(BLOCK, WIDE)
+    for at, ref in ((ROWS + EDGE * core, near_ref), (ROWS + EDGE * (1 - core), far_ref)):
+        rows = pl.ds(pl.multiple_of(at, EDGE), EDGE)
+        mask = mask_ref[rows]
+        for var in range(VARS):
+            kp[var, rows, main] = (ref[:, var * BLOCK : (var + 1) * BLOCK] + 4.0) * mask[:, main]
+            kp[var, rows, edge] = (unpack_side(ref[:, E_SIDE : E_SIDE + SIDE], var) + 4.0) * mask[:, edge]
+            at = E_SOURCE + var * BLOCK
+            start(var, rows, main, ref[:, at : at + BLOCK] * mask[:, main])
+            start(var, rows, edge, unpack_side(ref[:, E_SIDE + SIDE : E_STATE], var) * mask[:, edge])
     for var in range(VARS):
-        kp[var] = kp[var] * mask_ref[...]
-        for at, size, ref in ((0, ROWS, source_ref), (near, EDGE, near_ref), (far, EDGE, far_ref)):
-            rows = pl.ds(at, size)
-            part = ref[var] * mask_ref[rows]
-            res[var, rows] = part
-            part = part * (1.0 / THETA)
-            dirn[var, rows] = part
-            adj[var, rows] = part
+        start(var, slice(0, ROWS), slice(0, WIDE), source_ref[var] * mask_ref[:ROWS])
 
     def shape(src, var):
         u = src[var]
@@ -213,23 +260,19 @@
             dirn[var] = d
             adj[var] = adj[var] + d
 
-
-def final_kernel(mix_ref, adj, kp, near_ref, far_ref, o0, o1, o2, o3, tmp):
-    y, z = group_place()
-    core = lax.rem(lax.axis_index("tile"), 2)
-
     for var in range(VARS):
         u = adj[var]
-        tmp[var] = kp[var, :ROWS, :BLOCK] * u[:ROWS, :BLOCK] - shape_rows(u)[:ROWS, :BLOCK]
+        tmp[var, :ROWS, :BLOCK] = kp[var, :ROWS, :BLOCK] * u[:ROWS, :BLOCK] - shape_rows(u)[:ROWS, :BLOCK]
     for k, out in enumerate((o0, o1, o2, o3)):
         v = 2 * ahead(y, k) + z
         for c in range(0, BLOCK, 128):
             cols = slice(c, c + 128)
-            near = mix_ref[v, 0] * near_ref[2 * VARS, 0:1, cols]
-            far = mix_ref[v, 0] * far_ref[2 * VARS, 0:1, cols]
+            here = slice(E_STATE + c, E_STATE + c + 128)
+            near = mix_ref[v, 0] * near_ref[0:1, here]
+            far = mix_ref[v, 0] * far_ref[0:1, here]
             for w in range(1, VARS):
-                near = near + mix_ref[v, w] * near_ref[2 * VARS, w : w + 1, cols]
-                far = far + mix_ref[v, w] * far_ref[2 * VARS, w : w + 1, cols]
+                near = near + mix_ref[v, w] * near_ref[w : w + 1, here]
+                far = far + mix_ref[v, w] * far_ref[w : w + 1, here]
             out[4, 0:1, cols] = jnp.where(core == 0, far, near)
             out[4, 1:2, cols] = jnp.where(core == 0, near, far)
             out[4, 2:, cols] = jnp.zeros((6, 128), jnp.float32)
@@ -295,9 +338,9 @@
     other_extra = across(extra)
     shaped, _ = lax.optimization_barrier((shaped, other_extra))
     other_shaped = across(shaped)
-    pieces = call(pack_kernel, [(2, ROWS + OBS_ROWS, WIDE)] * 4, 4)(kappa, other_kappa, extra, other_extra)
+    pieces = call(pack_kernel, [(8, PIECE)] * 4, 4)(kappa, other_kappa, extra, other_extra)
     pieces = [pieces[0]] + [around(pieces[k], k) for k in range(1, GROUPS)]
-    edges = (2 * VARS + 1, EDGE, WIDE)
+    edges = (EDGE, EDGES)
     source, near, far = call(
         scatter_kernel,
         [(VARS, ROWS, WIDE), edges, edges],
@@ -310,20 +353,13 @@
     mixed = call(share_kernel, [(ROWS, COLS)] * 4, 3, smem=1)(mix, shaped, other_shaped)
     mixed = [mixed[0]] + [around(mixed[k], k) for k in range(1, GROUPS)]
     field = (VARS, TALL, WIDE)
-    adj, kp = call(
+    parts = call(
         main_kernel,
-        [field] * 2,
+        [(2 * ROWS // 8 + 1, 8, BLOCK)] * 4,
         8,
         smem=1,
-        scratch=[pltpu.VMEM(field, jnp.float32)] * 3 + [pltpu.VMEM((TALL, WIDE), jnp.float32)],
+        scratch=[pltpu.VMEM(field, jnp.float32)] * 5 + [pltpu.VMEM((TALL, WIDE), jnp.float32)],
     )(mix, source, near, far, *pieces)
-    parts = call(
-        final_kernel,
-        [(2 * ROWS // 8 + 1, 8, BLOCK)] * 4,
-        5,
-        smem=1,
-        scratch=[pltpu.VMEM((VARS, ROWS, BLOCK), jnp.float32)],
-    )(mix, adj, kp, near, far)
     parts = [parts[0]] + [around(parts[k], k) for k in range(1, GROUPS)]
     adjoint, grad = call(join_kernel, [(ROWS, COLS)] * 2, 9)(*parts, *mixed, state)
     return adjoint[None], grad[None]

time: 56.2 us -> 54.6 us (0.972)
  Pallas kernels: 8.8 us -> 8.03 us
  waiting for transfers between devices: 19.9 us -> 19.2 us
    pallas_call x3 -> x2, Pallas kernels: 5.28 us -> 4.45 us  [the longest x1 4.33 us: per_device(): call(main_kernel, [(2 * ROWS // 8 + 1, 8, BLOCK)] * 4, 8, smem=1, scratch...]
    ppermute x2, waiting for transfers between devices: 2.54 us -> 1.8 us  [beside(): return lax.ppermute(x, ('tile', 'var'), pairs)]
  transfers between devices with their start and end apart: 14 -> 14, of which waited for: 8 -> 8; matrix products, arithmetic and copies ran while one was open for 0% -> 0% of each run, Pallas kernels for 14% -> 13%
where the time goes in v3:
time: 54.6 us; the launch traced here: 54.4 us
  starting transfers between devices  24.6 us (45%)
  waiting for transfers between devices  19.2 us (35%)
  Pallas kernels  8.03 us (15%)
  local copies, waits for them, and re-layouts  1.64 us (3%)
  between operations  0.71 us (1%)
    ppermute x9, starting transfers between devices, around(): lax.ppermute(x, 'var', [(i, (i // 2 + k) % GROUPS * 2 + i % 2) for i in r...  14.2 us
    ppermute x3, waiting for transfers between devices, across(): return lax.ppermute(x, 'var', [(i, i ^ 1) for i in range(VARS)])  11.4 us
    ppermute x3, starting transfers between devices, across(): return lax.ppermute(x, 'var', [(i, i ^ 1) for i in range(VARS)])  8.45 us
    ppermute x9, waiting for transfers between devices, around(): lax.ppermute(x, 'var', [(i, (i // 2 + k) % GROUPS * 2 + i % 2) for i in r...  6 us
    pallas_call x1, Pallas kernels, per_device(): call(main_kernel, [(2 * ROWS // 8 + 1, 8, BLOCK)] * 4, 8, smem=1, scratch...  4.33 us
    ppermute x2, starting transfers between devices, beside(): return lax.ppermute(x, ('tile', 'var'), pairs)  2.01 us
    pallas_call x1, Pallas kernels, per_device(): call(scatter_kernel, [(VARS, ROWS, WIDE), edges, edges], 5, scratch=[pltp...  1.97 us
    ppermute x2, waiting for transfers between devices, beside(): return lax.ppermute(x, ('tile', 'var'), pairs)  1.8 us
  transfers between devices with their start and end apart: 14, of which 8 were waited for; matrix products, arithmetic and copies ran while one was open for 0% of the time, Pallas kernels for 13%

profile of v3, /device:TPU:2, one launch (start us, length us, event | category | flops | bytes accessed | tf_op | source)
XLA Modules:
  0.0 54.4 jit_solution(18153080445335836825)
XLA Ops:
  0.6 7.3 %collective-permute-start = (f32[16,2048]{1,0:T(8,128)}, f32[16,2048]{1,0:T(8,128)S(1)}, u32[]{:S(2)}, u32[]{:S(2)}) collective-permute-start(f32[16,2048]{1,0:T(8,128)} %bitcast.8), channel_id=1, source_target_pairs={{0,1},{1,0},{2,3},{3,2},{4,5},{5,4},{6,7},{7,6},{8,9},{9,8},{10,11... | collective-permute-start | bytes 393224 | tf_op jit(solution)/shard_map/ppermute | solution.py:315
  7.9 0.9 %copy-done = f32[1,16,2048]{2,1,0:T(8,128)S(1)} copy-done((f32[1,16,2048]{2,1,0:T(8,128)S(1)}, f32[1,16,2048]{2,1,0:T(8,128)}, u32[]{:S(2)}) %copy-start) | copy-done | bytes 131096
  8.8 0.7 %copy-done.4 = f32[1,4096]{1,0:T(1,128)S(1)} copy-done((f32[1,4096]{1,0:T(1,128)S(1)}, f32[1,4096]{1,0:T(1,128)}, u32[]{:S(2)}) %copy-start.4) | copy-done | bytes 16408
  9.7 9.5 %collective-permute-done.1.other_extra_ref = f32[8,1024]{1,0:T(8,128)S(1)} collective-permute-done((f32[8,1024]{1,0:T(8,128)S(1)}, f32[8,1024]{1,0:T(8,128)S(1)}, u32[]{:S(2)}, u32[]{:S(2)}) %collective-permute-start.1) | collective-permute-done | bytes 32800 | tf_op jit(solution)/shard_map/ppermute | solution.py:315
  19.3 1.7 %collective-permute-start.2 = (f32[8,3456]{1,0:T(8,128)S(1)}, f32[8,3456]{1,0:T(8,128)S(1)}, u32[]{:S(2)}, u32[]{:S(2)}) collective-permute-start(f32[8,3456]{1,0:T(8,128)S(1)} %get-tuple-element.23), channel_id=1, source_target_pairs={{0,2},{1,3},{2,4},{3,5},{4,6},{5,7},{6,0},{7,1},{8,10},{9,11},{10,... | collective-permute-start | bytes 331784 | tf_op jit(solution)/shard_map/ppermute | solution.py:319
  21.0 2.9 %collective-permute-start.3 = (f32[8,3456]{1,0:T(8,128)S(1)}, f32[8,3456]{1,0:T(8,128)S(1)}, u32[]{:S(2)}, u32[]{:S(2)}) collective-permute-start(f32[8,3456]{1,0:T(8,128)S(1)} %get-tuple-element.24), channel_id=1, source_target_pairs={{0,4},{1,5},{2,6},{3,7},{4,0},{5,1},{6,2},{7,3},{8,12},{9,13},{10,... | collective-permute-start | bytes 331784 | tf_op jit(solution)/shard_map/ppermute | solution.py:319
  23.9 1.3 %collective-permute-start.4 = (f32[8,3456]{1,0:T(8,128)S(1)}, f32[8,3456]{1,0:T(8,128)S(1)}, u32[]{:S(2)}, u32[]{:S(2)}) collective-permute-start(f32[8,3456]{1,0:T(8,128)S(1)} %get-tuple-element.25), channel_id=1, source_target_pairs={{0,6},{1,7},{2,0},{3,1},{4,2},{5,3},{6,4},{7,5},{8,14},{9,15},{10,... | collective-permute-start | bytes 331784 | tf_op jit(solution)/shard_map/ppermute | solution.py:319
  25.4 1.1 %collective-permute-start.10 = (f32[16,2048]{1,0:T(8,128)S(1)}, f32[16,2048]{1,0:T(8,128)S(1)}, u32[]{:S(2)}, u32[]{:S(2)}) collective-permute-start(f32[16,2048]{1,0:T(8,128)S(1)} %shard_map.72.own_ref), channel_id=1, source_target_pairs={{0,1},{1,0},{2,3},{3,2},{4,5},{5,4},{6,7},{7,6},{8,9},{9,8},{10,11... | collective-permute-start | bytes 393224 | tf_op jit(solution)/shard_map/ppermute | solution.py:315
  26.5 1.3 %collective-permute-done.3.k2 = f32[8,3456]{1,0:T(8,128)S(1)} collective-permute-done((f32[8,3456]{1,0:T(8,128)S(1)}, f32[8,3456]{1,0:T(8,128)S(1)}, u32[]{:S(2)}, u32[]{:S(2)}) %collective-permute-start.3) | collective-permute-done | bytes 110624 | tf_op jit(solution)/shard_map/ppermute | solution.py:319
  27.8 0.8 %collective-permute-done.4.k3 = f32[8,3456]{1,0:T(8,128)S(1)} collective-permute-done((f32[8,3456]{1,0:T(8,128)S(1)}, f32[8,3456]{1,0:T(8,128)S(1)}, u32[]{:S(2)}, u32[]{:S(2)}) %collective-permute-start.4) | collective-permute-done | bytes 110624 | tf_op jit(solution)/shard_map/ppermute | solution.py:319
  28.6 2.0 %shard_map.70 = (f32[8,16,640]{2,1,0:T(8,128)S(1)}, f32[8,8960]{1,0:T(8,128)S(1)}, f32[8,8960]{1,0:T(8,128)S(1)}) custom-call(s32[1,4096]{1,0:T(1,128)S(1)} %bitcast.11, f32[8,3456]{1,0:T(8,128)S(1)} %get-tuple-element.22.k0, f32[8,3456]{1,0:T(8,128)S(1)} %collective-permute-done.2.k1, f32[8,3456]{1,0:T(8,128)S(1)} %collective-permute-done.3.k2, ...), custom_call_target="tpu_custom_call" | custom-call | flops 1000 | bytes 100000 | tf_op jit(solution)/shard_map/pallas_call | solution.py:344
  30.7 1.9 %collective-permute-start.6 = (f32[8,8960]{1,0:T(8,128)S(1)}, f32[8,8960]{1,0:T(8,128)S(1)}, u32[]{:S(2)}, u32[]{:S(2)}) collective-permute-start(f32[8,8960]{1,0:T(8,128)S(1)} %get-tuple-element.28), channel_id=1, source_target_pairs={{8,16},{16,8},{9,17},{17,9},{10,18},{18,10},{11,19},{19,11},{12,20... | collective-permute-start | bytes 860168 | tf_op jit(solution)/shard_map/ppermute | solution.py:328
  32.8 1.9 %collective-permute-done.10.other_ref = f32[16,2048]{1,0:T(8,128)S(1)} collective-permute-done((f32[16,2048]{1,0:T(8,128)S(1)}, f32[16,2048]{1,0:T(8,128)S(1)}, u32[]{:S(2)}, u32[]{:S(2)}) %collective-permute-start.10) | collective-permute-done | bytes 131104 | tf_op jit(solution)/shard_map/ppermute | solution.py:315
  35.4 0.8 %collective-permute-start.11 = (f32[16,2048]{1,0:T(8,128)S(1)}, f32[16,2048]{1,0:T(8,128)S(1)}, u32[]{:S(2)}, u32[]{:S(2)}) collective-permute-start(f32[16,2048]{1,0:T(8,128)S(1)} %get-tuple-element.37), channel_id=1, source_target_pairs={{0,2},{1,3},{2,4},{3,5},{4,6},{5,7},{6,0},{7,1},{8,10},{9,11},{10,... | collective-permute-start | bytes 393224 | tf_op jit(solution)/shard_map/ppermute | solution.py:319
  36.2 1.4 %collective-permute-start.12 = (f32[16,2048]{1,0:T(8,128)S(1)}, f32[16,2048]{1,0:T(8,128)S(1)}, u32[]{:S(2)}, u32[]{:S(2)}) collective-permute-start(f32[16,2048]{1,0:T(8,128)S(1)} %get-tuple-element.38), channel_id=1, source_target_pairs={{0,4},{1,5},{2,6},{3,7},{4,0},{5,1},{6,2},{7,3},{8,12},{9,13},{10,... | collective-permute-start | bytes 393224 | tf_op jit(solution)/shard_map/ppermute | solution.py:319
  37.7 1.3 %collective-permute-start.13 = (f32[16,2048]{1,0:T(8,128)S(1)}, f32[16,2048]{1,0:T(8,128)S(1)}, u32[]{:S(2)}, u32[]{:S(2)}) collective-permute-start(f32[16,2048]{1,0:T(8,128)S(1)} %get-tuple-element.39), channel_id=1, source_target_pairs={{0,6},{1,7},{2,0},{3,1},{4,2},{5,3},{6,4},{7,5},{8,14},{9,15},{10,... | collective-permute-start | bytes 393224 | tf_op jit(solution)/shard_map/ppermute | solution.py:319
  39.0 1.8 %collective-permute-done.6.far_ref = f32[8,8960]{1,0:T(8,128)S(1)} collective-permute-done((f32[8,8960]{1,0:T(8,128)S(1)}, f32[8,8960]{1,0:T(8,128)S(1)}, u32[]{:S(2)}, u32[]{:S(2)}) %collective-permute-start.6) | collective-permute-done | bytes 286752 | tf_op jit(solution)/shard_map/ppermute | solution.py:328
  40.8 4.3 %shard_map.71 = (f32[5,8,512]{2,1,0:T(8,128)S(1)}, f32[5,8,512]{2,1,0:T(8,128)S(1)}, f32[5,8,512]{2,1,0:T(8,128)S(1)}, f32[5,8,512]{2,1,0:T(8,128)S(1)}) custom-call(f32[8,8]{1,0:T(8,128)S(1)} %convolution_multiply_fusion.mix_ref, f32[8,16,640]{2,1,0:T(8,128)S(1)} %get-tuple-element.26.source_ref, f32[8,8960]{1,0:T(8,128)S(1)} %collective-permute-done.5.near_ref, ...), custom_call_target="tpu_custom_call" | custom-call | flops 1000 | bytes 100000 | tf_op jit(solution)/shard_map/pallas_call | solution.py:356
  45.1 0.9 %collective-permute-start.7 = (f32[5,8,512]{2,1,0:T(8,128)S(1)}, f32[5,8,512]{2,1,0:T(8,128)S(1)}, u32[]{:S(2)}, u32[]{:S(2)}) collective-permute-start(f32[5,8,512]{2,1,0:T(8,128)S(1)} %get-tuple-element.30), channel_id=1, source_target_pairs={{0,2},{1,3},{2,4},{3,5},{4,6},{5,7},{6,0},{7,1},{8,10},{9,11},{10,... | collective-permute-start | bytes 245768 | tf_op jit(solution)/shard_map/ppermute | solution.py:319
  46.0 3.2 %collective-permute-start.8 = (f32[5,8,512]{2,1,0:T(8,128)S(1)}, f32[5,8,512]{2,1,0:T(8,128)S(1)}, u32[]{:S(2)}, u32[]{:S(2)}) collective-permute-start(f32[5,8,512]{2,1,0:T(8,128)S(1)} %get-tuple-element.31), channel_id=1, source_target_pairs={{0,4},{1,5},{2,6},{3,7},{4,0},{5,1},{6,2},{7,3},{8,12},{9,13},{10,... | collective-permute-start | bytes 245768 | tf_op jit(solution)/shard_map/ppermute | solution.py:319
  49.8 1.2 %collective-permute-done.7.p1 = f32[5,8,512]{2,1,0:T(8,128)S(1)} collective-permute-done((f32[5,8,512]{2,1,0:T(8,128)S(1)}, f32[5,8,512]{2,1,0:T(8,128)S(1)}, u32[]{:S(2)}, u32[]{:S(2)}) %collective-permute-start.7) | collective-permute-done | bytes 81952 | tf_op jit(solution)/shard_map/ppermute | solution.py:319
  51.1 1.4 %collective-permute-done.8.p2 = f32[5,8,512]{2,1,0:T(8,128)S(1)} collective-permute-done((f32[5,8,512]{2,1,0:T(8,128)S(1)}, f32[5,8,512]{2,1,0:T(8,128)S(1)}, u32[]{:S(2)}, u32[]{:S(2)}) %collective-permute-start.8) | collective-permute-done | bytes 81952 | tf_op jit(solution)/shard_map/ppermute | solution.py:319
  52.5 1.2 %collective-permute-done.9.p3 = f32[5,8,512]{2,1,0:T(8,128)S(1)} collective-permute-done((f32[5,8,512]{2,1,0:T(8,128)S(1)}, f32[5,8,512]{2,1,0:T(8,128)S(1)}, u32[]{:S(2)}, u32[]{:S(2)}) %collective-permute-start.9) | collective-permute-done | bytes 81952 | tf_op jit(solution)/shard_map/ppermute | solution.py:319
  53.7 0.8 %shard_map.74 = (f32[16,2048]{1,0:T(8,128)}, f32[16,2048]{1,0:T(8,128)}) custom-call(f32[5,8,512]{2,1,0:T(8,128)S(1)} %get-tuple-element.29.p0, f32[5,8,512]{2,1,0:T(8,128)S(1)} %collective-permute-done.7.p1, f32[5,8,512]{2,1,0:T(8,128)S(1)} %collective-permute-done.8.p2, f32[5,8,512]{2,1,0:T(8,128)S(1)} %collective-permute-done.9.p3, ...), custom_call_target="tpu_custom_call" | custom-call | flops 1000 | bytes 100000 | tf_op jit(solution)/shard_map/pallas_call | solution.py:364
  (24 shorter events, 2.0 us)
Async XLA Ops:
  0.6 18.6 %collective-permute-start = (f32[16,2048]{1,0:T(8,128)}, f32[16,2048]{1,0:T(8,128)S(1)}, u32[]{:S(2)}, u32[]{:S(2)}) collective-permute-start(f32[16,2048]{1,0:T(8,128)} %bitcast.8), channel_id=1, source_target_pairs={{0,1},{1,0},{2,3},{3,2},{4,5},{5,4},{6,7},{7,6},{8,9},{9,8},{10,11... | collective-permute-start | bytes 393224 | tf_op jit(solution)/shard_map/ppermute | solution.py:315
  7.9 0.9 %copy-start = (f32[1,16,2048]{2,1,0:T(8,128)S(1)}, f32[1,16,2048]{2,1,0:T(8,128)}, u32[]{:S(2)}) copy-start(f32[1,16,2048]{2,1,0:T(8,128)} %param.6) | copy-start | bytes 393220
  8.8 0.7 %copy-start.4 = (f32[1,4096]{1,0:T(1,128)S(1)}, f32[1,4096]{1,0:T(1,128)}, u32[]{:S(2)}) copy-start(f32[1,4096]{1,0:T(1,128)} %obs_ref.1) | copy-start | bytes 49156
  9.5 9.7 %copy-start.2 = (f32[1,16,2048]{2,1,0:T(8,128)S(1)}, f32[1,16,2048]{2,1,0:T(8,128)}, u32[]{:S(2)}) copy-start(f32[1,16,2048]{2,1,0:T(8,128)} %param.5) | copy-start | bytes 393220
  9.5 15.7 %copy-start.1 = (f32[1,16,2048]{2,1,0:T(8,128)S(1)}, f32[1,16,2048]{2,1,0:T(8,128)}, u32[]{:S(2)}) copy-start(f32[1,16,2048]{2,1,0:T(8,128)} %param.6) | copy-start | bytes 393220
  9.6 9.6 %collective-permute-start.1 = (f32[8,1024]{1,0:T(8,128)S(1)}, f32[8,1024]{1,0:T(8,128)S(1)}, u32[]{:S(2)}, u32[]{:S(2)}) collective-permute-start(f32[8,1024]{1,0:T(8,128)S(1)} %shard_map.68.own_extra_ref), channel_id=1, source_target_pairs={{0,1},{1,0},{2,3},{3,2},{4,5},{5,4},{6,7},{7,6},{8,9},{9,8},{10,11... | collective-permute-start | bytes 98312 | tf_op jit(solution)/shard_map/ppermute | solution.py:315
  19.3 7.1 %collective-permute-start.2 = (f32[8,3456]{1,0:T(8,128)S(1)}, f32[8,3456]{1,0:T(8,128)S(1)}, u32[]{:S(2)}, u32[]{:S(2)}) collective-permute-start(f32[8,3456]{1,0:T(8,128)S(1)} %get-tuple-element.23), channel_id=1, source_target_pairs={{0,2},{1,3},{2,4},{3,5},{4,6},{5,7},{6,0},{7,1},{8,10},{9,11},{10,... | collective-permute-start | bytes 331784 | tf_op jit(solution)/shard_map/ppermute | solution.py:319
  21.0 6.8 %collective-permute-start.3 = (f32[8,3456]{1,0:T(8,128)S(1)}, f32[8,3456]{1,0:T(8,128)S(1)}, u32[]{:S(2)}, u32[]{:S(2)}) collective-permute-start(f32[8,3456]{1,0:T(8,128)S(1)} %get-tuple-element.24), channel_id=1, source_target_pairs={{0,4},{1,5},{2,6},{3,7},{4,0},{5,1},{6,2},{7,3},{8,12},{9,13},{10,... | collective-permute-start | bytes 331784 | tf_op jit(solution)/shard_map/ppermute | solution.py:319
  23.9 4.8 %copy-start.3 = (s32[4096]{0:T(1024)S(1)}, s32[4096]{0:T(1024)}, u32[]{:S(2)}) copy-start(s32[4096]{0:T(1024)} %param.8) | copy-start | bytes 49156
  23.9 4.7 %collective-permute-start.4 = (f32[8,3456]{1,0:T(8,128)S(1)}, f32[8,3456]{1,0:T(8,128)S(1)}, u32[]{:S(2)}, u32[]{:S(2)}) collective-permute-start(f32[8,3456]{1,0:T(8,128)S(1)} %get-tuple-element.25), channel_id=1, source_target_pairs={{0,6},{1,7},{2,0},{3,1},{4,2},{5,3},{6,4},{7,5},{8,14},{9,15},{10,... | collective-permute-start | bytes 331784 | tf_op jit(solution)/shard_map/ppermute | solution.py:319
  25.4 9.4 %collective-permute-start.10 = (f32[16,2048]{1,0:T(8,128)S(1)}, f32[16,2048]{1,0:T(8,128)S(1)}, u32[]{:S(2)}, u32[]{:S(2)}) collective-permute-start(f32[16,2048]{1,0:T(8,128)S(1)} %shard_map.72.own_ref), channel_id=1, source_target_pairs={{0,1},{1,0},{2,3},{3,2},{4,5},{5,4},{6,7},{7,6},{8,9},{9,8},{10,11... | collective-permute-start | bytes 393224 | tf_op jit(solution)/shard_map/ppermute | solution.py:315
  28.6 4.0 %copy-start.5 = (f32[8,8]{1,0:T(8,128)S(1)}, f32[8,8]{1,0:T(8,128)}, u32[]{:S(2)}) copy-start(f32[8,8]{1,0:T(8,128)} %param.7) | copy-start | bytes 772
  30.6 8.4 %collective-permute-start.5 = (f32[8,8960]{1,0:T(8,128)S(1)}, f32[8,8960]{1,0:T(8,128)S(1)}, u32[]{:S(2)}, u32[]{:S(2)}) collective-permute-start(f32[8,8960]{1,0:T(8,128)S(1)} %get-tuple-element.27), channel_id=1, source_target_pairs={{0,8},{8,0},{1,9},{9,1},{2,10},{10,2},{3,11},{11,3},{4,12},{12,4},... | collective-permute-start | bytes 860168 | tf_op jit(solution)/shard_map/ppermute | solution.py:328
  30.7 10.1 %collective-permute-start.6 = (f32[8,8960]{1,0:T(8,128)S(1)}, f32[8,8960]{1,0:T(8,128)S(1)}, u32[]{:S(2)}, u32[]{:S(2)}) collective-permute-start(f32[8,8960]{1,0:T(8,128)S(1)} %get-tuple-element.28), channel_id=1, source_target_pairs={{8,16},{16,8},{9,17},{17,9},{10,18},{18,10},{11,19},{19,11},{12,20... | collective-permute-start | bytes 860168 | tf_op jit(solution)/shard_map/ppermute | solution.py:328
  35.4 13.8 %collective-permute-start.11 = (f32[16,2048]{1,0:T(8,128)S(1)}, f32[16,2048]{1,0:T(8,128)S(1)}, u32[]{:S(2)}, u32[]{:S(2)}) collective-permute-start(f32[16,2048]{1,0:T(8,128)S(1)} %get-tuple-element.37), channel_id=1, source_target_pairs={{0,2},{1,3},{2,4},{3,5},{4,6},{5,7},{6,0},{7,1},{8,10},{9,11},{10,... | collective-permute-start | bytes 393224 | tf_op jit(solution)/shard_map/ppermute | solution.py:319
  36.2 13.6 %collective-permute-start.12 = (f32[16,2048]{1,0:T(8,128)S(1)}, f32[16,2048]{1,0:T(8,128)S(1)}, u32[]{:S(2)}, u32[]{:S(2)}) collective-permute-start(f32[16,2048]{1,0:T(8,128)S(1)} %get-tuple-element.38), channel_id=1, source_target_pairs={{0,4},{1,5},{2,6},{3,7},{4,0},{5,1},{6,2},{7,3},{8,12},{9,13},{10,... | collective-permute-start | bytes 393224 | tf_op jit(solution)/shard_map/ppermute | solution.py:319
  37.7 12.2 %collective-permute-start.13 = (f32[16,2048]{1,0:T(8,128)S(1)}, f32[16,2048]{1,0:T(8,128)S(1)}, u32[]{:S(2)}, u32[]{:S(2)}) collective-permute-start(f32[16,2048]{1,0:T(8,128)S(1)} %get-tuple-element.39), channel_id=1, source_target_pairs={{0,6},{1,7},{2,0},{3,1},{4,2},{5,3},{6,4},{7,5},{8,14},{9,15},{10,... | collective-permute-start | bytes 393224 | tf_op jit(solution)/shard_map/ppermute | solution.py:319
  45.1 6.0 %collective-permute-start.7 = (f32[5,8,512]{2,1,0:T(8,128)S(1)}, f32[5,8,512]{2,1,0:T(8,128)S(1)}, u32[]{:S(2)}, u32[]{:S(2)}) collective-permute-start(f32[5,8,512]{2,1,0:T(8,128)S(1)} %get-tuple-element.30), channel_id=1, source_target_pairs={{0,2},{1,3},{2,4},{3,5},{4,6},{5,7},{6,0},{7,1},{8,10},{9,11},{10,... | collective-permute-start | bytes 245768 | tf_op jit(solution)/shard_map/ppermute | solution.py:319
  46.0 6.5 %collective-permute-start.8 = (f32[5,8,512]{2,1,0:T(8,128)S(1)}, f32[5,8,512]{2,1,0:T(8,128)S(1)}, u32[]{:S(2)}, u32[]{:S(2)}) collective-permute-start(f32[5,8,512]{2,1,0:T(8,128)S(1)} %get-tuple-element.31), channel_id=1, source_target_pairs={{0,4},{1,5},{2,6},{3,7},{4,0},{5,1},{6,2},{7,3},{8,12},{9,13},{10,... | collective-permute-start | bytes 245768 | tf_op jit(solution)/shard_map/ppermute | solution.py:319
  49.2 4.4 %collective-permute-start.9 = (f32[5,8,512]{2,1,0:T(8,128)S(1)}, f32[5,8,512]{2,1,0:T(8,128)S(1)}, u32[]{:S(2)}, u32[]{:S(2)}) collective-permute-start(f32[5,8,512]{2,1,0:T(8,128)S(1)} %get-tuple-element.32), channel_id=1, source_target_pairs={{0,6},{1,7},{2,0},{3,1},{4,2},{5,3},{6,4},{7,5},{8,14},{9,15},{10,... | collective-permute-start | bytes 245768 | tf_op jit(solution)/shard_map/ppermute | solution.py:319

commit v4 on v3

--- a/solution.py
+++ b/solution.py
@@ -21,10 +21,12 @@
 TALL = ROWS + 2 * EDGE
 OBS = 4096
 OBS_ROWS = OBS // BLOCK
+EXTRA = ROWS // 8 * COLS
+MIB = 1024 * 1024
 SLIM = 16
-P_OBS = 4 * BLOCK
-P_STATE = P_OBS + 2 * BLOCK
-P_SIDE = P_STATE + 2 * SIDE
+P_OBS = 2 * BLOCK
+P_STATE = P_OBS + BLOCK
+P_SIDE = P_STATE + SIDE
 PIECE = P_SIDE + SIDE
 E_SOURCE = VARS * BLOCK
 E_SIDE = 2 * VARS * BLOCK
@@ -59,25 +61,35 @@
     return lax.rem(y - k + GROUPS, GROUPS)
 
 
-def window(ref, block, rows):
-    main = ref[rows, pl.ds(pl.multiple_of(block * BLOCK, BLOCK), BLOCK)]
+def window(ref, block, row):
+    start = row * COLS // 8
+    main = ref[:, pl.ds(pl.multiple_of(start + block * BLOCK, BLOCK), BLOCK)]
     after = jnp.minimum(block + 1, GROUPS - 1) * BLOCK
     before = jnp.maximum(block * BLOCK - SIDE, 0)
-    right = ref[rows, pl.ds(pl.multiple_of(after, SIDE), SIDE)]
-    left = ref[rows, pl.ds(pl.multiple_of(before, SIDE), SIDE)]
+    right = ref[:, pl.ds(pl.multiple_of(start + after, SIDE), SIDE)]
+    left = ref[:, pl.ds(pl.multiple_of(start + before, SIDE), SIDE)]
     lane = lax.broadcasted_iota(jnp.int32, (8, SIDE), 1)
     return main, jnp.where(lane < SIDE // 2, right, left)
 
 
-def extra_kernel(obs_ref, state_ref, extra_ref):
+def first_kernel(kappa_hbm, obs_hbm, state_hbm, sent_ref, kappa_ref, obs_ref, state_ref, sems):
+    edges = [(state_hbm.at[r : r + 1, :], state_ref.at[i : i + 1, :]) for i, r in enumerate((0, ROWS - 1))]
+    pairs = [(kappa_hbm, kappa_ref), (obs_hbm, obs_ref)] + edges
+    copies = [pltpu.make_async_copy(src, dst, sems.at[i]) for i, (src, dst) in enumerate(pairs)]
+    for one in copies:
+        one.start()
+    for one in copies:
+        one.wait()
+    for r in range(0, ROWS, 8):
+        sent_ref[:, r // 8 * COLS : (r // 8 + 1) * COLS] = kappa_ref[r : r + 8]
     for i in range(OBS_ROWS):
-        extra_ref[i : i + 1, :BLOCK] = obs_ref[:, i * BLOCK : (i + 1) * BLOCK]
-    for e, r in enumerate((0, ROWS - 1)):
+        sent_ref[i : i + 1, EXTRA : EXTRA + BLOCK] = obs_ref[:, i * BLOCK : (i + 1) * BLOCK]
+    for e in range(2):
         for block in range(GROUPS):
             for i in range(BLOCK // SIDE):
-                to, at = e * (BLOCK // SIDE) + i, BLOCK + block * SIDE
+                to, at = e * (BLOCK // SIDE) + i, EXTRA + BLOCK + block * SIDE
                 col = block * BLOCK + i * SIDE
-                extra_ref[to : to + 1, at : at + SIDE] = state_ref[r : r + 1, col : col + SIDE]
+                sent_ref[to : to + 1, at : at + SIDE] = state_ref[e : e + 1, col : col + SIDE]
 
 
 def shape_kernel(kappa_ref, state_ref, shaped_ref):
@@ -90,27 +102,28 @@
     shaped_ref[...] = (kappa_ref[...] + 4.0) * u - beside
 
 
-def pack_kernel(own_ref, other_ref, own_extra_ref, other_extra_ref, *outs):
+def hold_kernel(sent_ref, held_ref):
+    held_ref[...] = sent_ref[...]
+
+
+def pack_kernel(ref, *outs):
     y, _ = group_place()
     for k in range(GROUPS):
         block = ahead(y, k)
         packed = jnp.zeros((8, SIDE), jnp.float32)
-        for slot, (ref, extra) in enumerate(((own_ref, own_extra_ref), (other_ref, other_extra_ref))):
-            for half in range(ROWS // 8):
-                main, side = window(ref, block, slice(half * 8, half * 8 + 8))
-                index = slot * 2 + half
-                outs[k][:, index * BLOCK : (index + 1) * BLOCK] = main
-                packed = pack_side(packed, side, index)
-            outs[k][:, P_OBS + slot * BLOCK : P_OBS + (slot + 1) * BLOCK] = extra[:, :BLOCK]
-            state = extra[:, lanes_at(BLOCK + block * SIDE, SIDE)]
-            outs[k][:, P_STATE + slot * SIDE : P_STATE + (slot + 1) * SIDE] = state
+        for half in range(ROWS // 8):
+            main, side = window(ref, block, half * 8)
+            outs[k][:, half * BLOCK : (half + 1) * BLOCK] = main
+            packed = pack_side(packed, side, half)
+        outs[k][:, P_OBS:P_STATE] = ref[:, EXTRA : EXTRA + BLOCK]
+        outs[k][:, P_STATE:P_SIDE] = ref[:, lanes_at(EXTRA + BLOCK + block * SIDE, SIDE)]
         outs[k][:, P_SIDE:] = packed
 
 
-def scatter_kernel(cell_ref, k0, k1, k2, k3, source_ref, near_ref, far_ref, acc):
+def scatter_kernel(cell_ref, *refs):
     y, z = group_place()
     core = lax.rem(lax.axis_index("tile"), 2)
-    pieces = (k0, k1, k2, k3)
+    pieces, (source_ref, near_ref, far_ref, acc) = (refs[:GROUPS], refs[GROUPS : 2 * GROUPS]), refs[2 * GROUPS :]
     acc[...] = jnp.zeros_like(acc)
     rows = lax.broadcasted_iota(jnp.int32, (ROWS, BLOCK), 0)
     lanes = lax.broadcasted_iota(jnp.int32, (WIDE, BLOCK), 0)
@@ -127,7 +140,7 @@
         highs, lows = [], []
         for k in range(GROUPS):
             for slot in range(2):
-                value = pieces[k][i : i + 1, P_OBS + slot * BLOCK : P_OBS + (slot + 1) * BLOCK]
+                value = pieces[slot][k][i : i + 1, P_OBS:P_STATE]
                 high = value.astype(jnp.bfloat16).astype(jnp.float32)
                 low = value - high
                 highs.append(jnp.where(hit_row, high, 0.0).astype(jnp.bfloat16))
@@ -148,9 +161,9 @@
         for k in range(GROUPS):
             for slot in range(2):
                 var = 2 * behind(y, k) + lax.rem(z + slot, 2)
-                kappa = pieces[k][:, lanes_at((slot * 2 + last) * BLOCK, BLOCK)]
+                kappa = pieces[slot][k][:, lanes_at(last * BLOCK, BLOCK)]
                 ref[:, lanes_at(var * BLOCK, BLOCK)] = kappa
-                side = unpack_side(pieces[k][:, P_SIDE:], slot * 2 + last)
+                side = unpack_side(pieces[slot][k][:, P_SIDE:], last)
                 packed_kappa = pack_side(packed_kappa, side, var)
                 total = source_ref[var, pl.ds(pl.multiple_of(EDGE * last, EDGE), EDGE)]
                 ref[:, lanes_at(E_SOURCE + var * BLOCK, BLOCK)] = total[:, :BLOCK]
@@ -166,8 +179,7 @@
             for k in range(GROUPS):
                 for slot in range(2):
                     var = 2 * behind(y, k) + lax.rem(z + slot, 2)
-                    at = P_STATE + slot * SIDE
-                    rows = jnp.where(sub == var, pieces[k][row : row + 1, at : at + SIDE], rows)
+                    rows = jnp.where(sub == var, pieces[slot][k][row : row + 1, P_STATE:P_SIDE], rows)
             held.append(rows)
         here = slice(E_STATE + i * SIDE, E_STATE + (i + 1) * SIDE)
         near_ref[:, here] = jnp.where(core == 0, held[1], held[0])
@@ -187,12 +199,11 @@
     return pltpu.roll(u, 1, 0) + pltpu.roll(u, TALL - 1, 0) + pltpu.roll(u, 1, 1) + pltpu.roll(u, WIDE - 1, 1)
 
 
-def main_kernel(
-    mix_ref, source_ref, near_ref, far_ref, k0, k1, k2, k3, o0, o1, o2, o3, adj, kp, res, dirn, tmp, mask_ref
-):
+def main_kernel(mix_ref, source_ref, near_ref, far_ref, *refs):
+    pieces, outs = (refs[:GROUPS], refs[GROUPS : 2 * GROUPS]), refs[2 * GROUPS : 3 * GROUPS]
+    adj, kp, res, dirn, tmp, mask_ref = refs[3 * GROUPS :]
     y, z = group_place()
     tile = lax.axis_index("tile")
-    pieces = (k0, k1, k2, k3)
     row = lax.broadcasted_iota(jnp.int32, (TALL, WIDE), 0)
     lane = lax.broadcasted_iota(jnp.int32, (TALL, WIDE), 1)
     row = jnp.where(row < ROWS + EDGE, row, row - TALL) + tile * ROWS
@@ -203,11 +214,11 @@
         for slot in range(2):
             var = 2 * behind(y, k) + lax.rem(z + slot, 2)
             for half in range(ROWS // 8):
-                rows, index = slice(half * 8, half * 8 + 8), slot * 2 + half
+                rows, piece = slice(half * 8, half * 8 + 8), pieces[slot][k]
                 mask = mask_ref[rows]
-                kappa = pieces[k][:, index * BLOCK : (index + 1) * BLOCK]
+                kappa = piece[:, half * BLOCK : (half + 1) * BLOCK]
                 kp[var, rows, :BLOCK] = (kappa + 4.0) * mask[:, :BLOCK]
-                kp[var, rows, BLOCK:] = (unpack_side(pieces[k][:, P_SIDE:], index) + 4.0) * mask[:, BLOCK:]
+                kp[var, rows, BLOCK:] = (unpack_side(piece[:, P_SIDE:], half) + 4.0) * mask[:, BLOCK:]
     core = lax.rem(tile, 2)
 
     def start(var, rows, cols, part):
@@ -263,7 +274,7 @@
     for var in range(VARS):
         u = adj[var]
         tmp[var, :ROWS, :BLOCK] = kp[var, :ROWS, :BLOCK] * u[:ROWS, :BLOCK] - shape_rows(u)[:ROWS, :BLOCK]
-    for k, out in enumerate((o0, o1, o2, o3)):
+    for k, out in enumerate(outs):
         v = 2 * ahead(y, k) + z
         for c in range(0, BLOCK, 128):
             cols = slice(c, c + 128)
@@ -298,15 +309,15 @@
             grad_ref[rows, cols] = -(part[2 + half] * state_ref[rows, cols] + part[half] * mixed)
 
 
-def call(kernel, outs, n_in, smem=0, scratch=(), flops=1000, size=100000):
+def call(kernel, outs, n_in, smem=0, scratch=(), flops=1000, size=100000, hbm=0, limit=32):
     shapes = [jax.ShapeDtypeStruct(s, jnp.float32) for s in outs]
     return pl.pallas_call(
         kernel,
         out_shape=shapes,
-        in_specs=[SMEM] * smem + [VMEM] * (n_in - smem),
+        in_specs=[SMEM] * smem + [pl.BlockSpec(memory_space=pl.ANY)] * hbm + [VMEM] * (n_in - smem - hbm),
         out_specs=[VMEM] * len(shapes),
         scratch_shapes=list(scratch),
-        compiler_params=pltpu.CompilerParams(vmem_limit_bytes=32 * 1024 * 1024),
+        compiler_params=pltpu.CompilerParams(vmem_limit_bytes=limit * MIB),
         cost_estimate=pl.CostEstimate(flops=flops, bytes_accessed=size, transcendentals=0),
     )
 
@@ -332,31 +343,43 @@
     mixing = jnp.eye(VARS, dtype=jnp.float32) + coupling
     mix = jnp.einsum("uv,uw->vw", mixing, mixing, precision=lax.Precision.HIGHEST) * (1.0 / 64.0)
     kappa, state = range_sq[0], state_field[0]
-    other_kappa = across(kappa)
+    (sent,) = call(
+        first_kernel,
+        [(8, EXTRA + 2 * BLOCK)],
+        3,
+        hbm=3,
+        limit=56,
+        scratch=[pltpu.VMEM((ROWS, COLS), jnp.float32), pltpu.VMEM((1, OBS), jnp.float32)]
+        + [pltpu.VMEM((2, COLS), jnp.float32), pltpu.SemaphoreType.DMA((4,))],
+    )(kappa, obs_value, state)
+    got = across(sent)
+    (sent,) = call(hold_kernel, [(8, EXTRA + 2 * BLOCK)], 1)(sent)
+    own = call(pack_kernel, [(8, PIECE)] * 4, 1)(sent)
+    own = [own[0]] + [around(own[k], k) for k in range(1, GROUPS)]
     (shaped,) = call(shape_kernel, [(ROWS, COLS)], 2)(kappa, state)
-    (extra,) = call(extra_kernel, [(8, 2 * BLOCK)], 2)(obs_value, state)
-    other_extra = across(extra)
-    shaped, _ = lax.optimization_barrier((shaped, other_extra))
+    shaped, own[1] = lax.optimization_barrier((shaped, own[1]))
     other_shaped = across(shaped)
-    pieces = call(pack_kernel, [(8, PIECE)] * 4, 4)(kappa, other_kappa, extra, other_extra)
-    pieces = [pieces[0]] + [around(pieces[k], k) for k in range(1, GROUPS)]
+    other = call(pack_kernel, [(8, PIECE)] * 4, 1)(got)
+    other = [other[0]] + [around(other[k], k) for k in range(1, GROUPS)]
+    pieces = (*own, *other)
     edges = (EDGE, EDGES)
     source, near, far = call(
         scatter_kernel,
         [(VARS, ROWS, WIDE), edges, edges],
-        5,
+        9,
         scratch=[pltpu.VMEM((2 * VARS * ROWS, WIDE), jnp.float32)],
     )(obs_cell.reshape(1, OBS), *pieces)
     far = beside(far, tiles, False)
-    near = beside(near, tiles, True)
     shaped, other_shaped, _ = lax.optimization_barrier((shaped, other_shaped, source))
     mixed = call(share_kernel, [(ROWS, COLS)] * 4, 3, smem=1)(mix, shaped, other_shaped)
-    mixed = [mixed[0]] + [around(mixed[k], k) for k in range(1, GROUPS)]
+    near, first = lax.optimization_barrier((near, mixed[0]))
+    near = beside(near, tiles, True)
+    mixed = [first] + [around(mixed[k], k) for k in range(1, GROUPS)]
     field = (VARS, TALL, WIDE)
     parts = call(
         main_kernel,
         [(2 * ROWS // 8 + 1, 8, BLOCK)] * 4,
-        8,
+        12,
         smem=1,
         scratch=[pltpu.VMEM(field, jnp.float32)] * 5 + [pltpu.VMEM((TALL, WIDE), jnp.float32)],
     )(mix, source, near, far, *pieces)

time: 54.6 us -> 53.2 us (0.974)
  waiting for transfers between devices: 19.2 us -> 8.99 us
  starting transfers between devices: 24.6 us -> 32.1 us
  Pallas kernels: 8.03 us -> 9.78 us
  local copies, waits for them, and re-layouts: 1.64 us -> 0.97 us
    ppermute x3 -> x2, waiting for transfers between devices: 11.4 us -> 1.98 us  [across(): return lax.ppermute(x, 'var', [(i, i ^ 1) for i in range(VARS)])]
    ppermute x9 -> x12, starting transfers between devices: 14.2 us -> 18.8 us  [around(): lax.ppermute(x, 'var', [(i, (i // 2 + k) % GROUPS * 2 + i % 2) for i in r...]
    ppermute x2, starting transfers between devices: 2.01 us -> 5.96 us  [beside(): return lax.ppermute(x, ('tile', 'var'), pairs)]
    pallas_call x4 -> x6, Pallas kernels: 6.44 us -> 8.19 us  [the longest x1 4.31 us: per_device(): call(main_kernel, [(2 * ROWS // 8 + 1, 8, BLOCK)] * 4, 12, smem=1, scratc...]
    ppermute x2, waiting for transfers between devices: 1.8 us -> 0.07 us  [beside(): return lax.ppermute(x, ('tile', 'var'), pairs)]
    ppermute x3 -> x2, starting transfers between devices: 8.45 us -> 7.35 us  [across(): return lax.ppermute(x, 'var', [(i, i ^ 1) for i in range(VARS)])]
    ppermute x9 -> x12, waiting for transfers between devices: 6 us -> 6.93 us  [around(): lax.ppermute(x, 'var', [(i, (i // 2 + k) % GROUPS * 2 + i % 2) for i in r...]
    unnamed x12 -> x10, local copies, waits for them, and re-layouts: 1.64 us -> 0.97 us
  transfers between devices with their start and end apart: 14 -> 16, of which waited for: 8 -> 7; matrix products, arithmetic and copies ran while one was open for 0% -> 0% of each run, Pallas kernels for 13% -> 13%
where the time goes in v4:
time: 53.2 us; the launch traced here: 52.8 us
  starting transfers between devices  32.1 us (60%)
  Pallas kernels  9.78 us (18%)
  waiting for transfers between devices  8.99 us (17%)
  local copies, waits for them, and re-layouts  0.97 us (2%)
  between operations  0.73 us (1%)
    ppermute x12, starting transfers between devices, around(): lax.ppermute(x, 'var', [(i, (i // 2 + k) % GROUPS * 2 + i % 2) for i in r...  18.8 us
    ppermute x2, starting transfers between devices, across(): return lax.ppermute(x, 'var', [(i, i ^ 1) for i in range(VARS)])  7.35 us
    ppermute x12, waiting for transfers between devices, around(): lax.ppermute(x, 'var', [(i, (i // 2 + k) % GROUPS * 2 + i % 2) for i in r...  6.93 us
    ppermute x2, starting transfers between devices, beside(): return lax.ppermute(x, ('tile', 'var'), pairs)  5.96 us
    pallas_call x1, Pallas kernels, per_device(): call(main_kernel, [(2 * ROWS // 8 + 1, 8, BLOCK)] * 4, 12, smem=1, scratc...  4.31 us
    ppermute x2, waiting for transfers between devices, across(): return lax.ppermute(x, 'var', [(i, i ^ 1) for i in range(VARS)])  1.98 us
    pallas_call x1, Pallas kernels, per_device(): call(scatter_kernel, [(VARS, ROWS, WIDE), edges, edges], 9, scratch=[pltp...  1.97 us
    pallas_call x1, Pallas kernels, per_device(): call(first_kernel, [(8, EXTRA + 2 * BLOCK)], 3, hbm=3, limit=56, scratch=...  1.64 us
  transfers between devices with their start and end apart: 16, of which 7 were waited for; matrix products, arithmetic and copies ran while one was open for 0% of the time, Pallas kernels for 13%

profile of v4, /device:TPU:2, one launch (start us, length us, event | category | flops | bytes accessed | tf_op | source)
XLA Modules:
  0.0 52.8 jit_solution(11587686523713427890)
XLA Ops:
  0.6 1.6 %shard_map.68.sent_ref = f32[8,5120]{1,0:T(8,128)} custom-call(f32[16,2048]{1,0:T(8,128)} %bitcast.8, f32[1,4096]{1,0:T(1,128)} %obs_hbm.1, f32[16,2048]{1,0:T(8,128)} %bitcast.5), custom_call_target="tpu_custom_call" | custom-call | flops 1000 | bytes 100000 | tf_op jit(solution)/shard_map/pallas_call | solution.py:346
  2.3 7.3 %collective-permute-start.3 = (f32[8,5120]{1,0:T(8,128)}, f32[8,5120]{1,0:T(8,128)S(1)}, u32[]{:S(2)}, u32[]{:S(2)}) collective-permute-start(f32[8,5120]{1,0:T(8,128)} %shard_map.68.sent_ref), channel_id=1, source_target_pairs={{0,1},{1,0},{2,3},{3,2},{4,5},{5,4},{6,7},{7,6},{8,9},{9,8},{10,11... | collective-permute-start | bytes 491528 | tf_op jit(solution)/shard_map/ppermute | solution.py:326
  9.6 0.9 %copy-done.1 = f32[8,5120]{1,0:T(8,128)S(1)} copy-done((f32[8,5120]{1,0:T(8,128)S(1)}, f32[8,5120]{1,0:T(8,128)}, u32[]{:S(2)}) %copy-start.1) | copy-done | bytes 163864
  10.7 1.6 %collective-permute-start = (f32[8,1792]{1,0:T(8,128)S(1)}, f32[8,1792]{1,0:T(8,128)S(1)}, u32[]{:S(2)}, u32[]{:S(2)}) collective-permute-start(f32[8,1792]{1,0:T(8,128)S(1)} %get-tuple-element.30), channel_id=1, source_target_pairs={{0,2},{1,3},{2,4},{3,5},{4,6},{5,7},{6,0},{7,1},{8,10},{9,11},{10,... | collective-permute-start | bytes 172040 | tf_op jit(solution)/shard_map/ppermute | solution.py:330
  12.3 2.9 %collective-permute-start.1 = (f32[8,1792]{1,0:T(8,128)S(1)}, f32[8,1792]{1,0:T(8,128)S(1)}, u32[]{:S(2)}, u32[]{:S(2)}) collective-permute-start(f32[8,1792]{1,0:T(8,128)S(1)} %get-tuple-element.32), channel_id=1, source_target_pairs={{0,4},{1,5},{2,6},{3,7},{4,0},{5,1},{6,2},{7,3},{8,12},{9,13},{10,... | collective-permute-start | bytes 172040 | tf_op jit(solution)/shard_map/ppermute | solution.py:330
  15.2 1.3 %collective-permute-start.2 = (f32[8,1792]{1,0:T(8,128)S(1)}, f32[8,1792]{1,0:T(8,128)S(1)}, u32[]{:S(2)}, u32[]{:S(2)}) collective-permute-start(f32[8,1792]{1,0:T(8,128)S(1)} %get-tuple-element.33), channel_id=1, source_target_pairs={{0,6},{1,7},{2,0},{3,1},{4,2},{5,3},{6,4},{7,5},{8,14},{9,15},{10,... | collective-permute-start | bytes 172040 | tf_op jit(solution)/shard_map/ppermute | solution.py:330
  17.0 0.7 %collective-permute-start.4 = (f32[8,1792]{1,0:T(8,128)S(1)}, f32[8,1792]{1,0:T(8,128)S(1)}, u32[]{:S(2)}, u32[]{:S(2)}) collective-permute-start(f32[8,1792]{1,0:T(8,128)S(1)} %get-tuple-element.35), channel_id=1, source_target_pairs={{0,2},{1,3},{2,4},{3,5},{4,6},{5,7},{6,0},{7,1},{8,10},{9,11},{10,... | collective-permute-start | bytes 172040 | tf_op jit(solution)/shard_map/ppermute | solution.py:330
  17.7 2.0 %collective-permute-start.5 = (f32[8,1792]{1,0:T(8,128)S(1)}, f32[8,1792]{1,0:T(8,128)S(1)}, u32[]{:S(2)}, u32[]{:S(2)}) collective-permute-start(f32[8,1792]{1,0:T(8,128)S(1)} %get-tuple-element.36), channel_id=1, source_target_pairs={{0,4},{1,5},{2,6},{3,7},{4,0},{5,1},{6,2},{7,3},{8,12},{9,13},{10,... | collective-permute-start | bytes 172040 | tf_op jit(solution)/shard_map/ppermute | solution.py:330
  19.7 1.3 %collective-permute-start.6 = (f32[8,1792]{1,0:T(8,128)S(1)}, f32[8,1792]{1,0:T(8,128)S(1)}, u32[]{:S(2)}, u32[]{:S(2)}) collective-permute-start(f32[8,1792]{1,0:T(8,128)S(1)} %get-tuple-element.37), channel_id=1, source_target_pairs={{0,6},{1,7},{2,0},{3,1},{4,2},{5,3},{6,4},{7,5},{8,14},{9,15},{10,... | collective-permute-start | bytes 172040 | tf_op jit(solution)/shard_map/ppermute | solution.py:330
  21.1 1.3 %collective-permute-done.4.refs_5_ = f32[8,1792]{1,0:T(8,128)S(1)} collective-permute-done((f32[8,1792]{1,0:T(8,128)S(1)}, f32[8,1792]{1,0:T(8,128)S(1)}, u32[]{:S(2)}, u32[]{:S(2)}) %collective-permute-start.4) | collective-permute-done | bytes 57376 | tf_op jit(solution)/shard_map/ppermute | solution.py:330
  22.4 1.0 %collective-permute-done.5.refs_6_ = f32[8,1792]{1,0:T(8,128)S(1)} collective-permute-done((f32[8,1792]{1,0:T(8,128)S(1)}, f32[8,1792]{1,0:T(8,128)S(1)}, u32[]{:S(2)}, u32[]{:S(2)}) %collective-permute-start.5) | collective-permute-done | bytes 57376 | tf_op jit(solution)/shard_map/ppermute | solution.py:330
  23.9 2.0 %shard_map.73 = (f32[8,16,640]{2,1,0:T(8,128)S(1)}, f32[8,8960]{1,0:T(8,128)S(1)}, f32[8,8960]{1,0:T(8,128)S(1)}) custom-call(s32[1,4096]{1,0:T(1,128)S(1)} %bitcast.10, f32[8,1792]{1,0:T(8,128)S(1)} %get-tuple-element.29.refs_0_, f32[8,1792]{1,0:T(8,128)S(1)} %collective-permute-done.refs_1_, f32[8,1792]{1,0:T(8,128)S(1)} %collective-permute-done.1.refs_2_, ...), custom_call_target="tpu_custom_call" | custom-call | flops 1000 | bytes 100000 | tf_op jit(solution)/shard_map/pallas_call | solution.py:366
  25.9 2.0 %collective-permute-done.7.other_ref = f32[16,2048]{1,0:T(8,128)S(1)} collective-permute-done((f32[16,2048]{1,0:T(8,128)S(1)}, f32[16,2048]{1,0:T(8,128)S(1)}, u32[]{:S(2)}, u32[]{:S(2)}) %collective-permute-start.7) | collective-permute-done | bytes 131104 | tf_op jit(solution)/shard_map/ppermute | solution.py:326
  27.8 0.7 %shard_map.74 = (f32[16,2048]{1,0:T(8,128)S(1)}, f32[16,2048]{1,0:T(8,128)S(1)}, f32[16,2048]{1,0:T(8,128)S(1)}, f32[16,2048]{1,0:T(8,128)S(1)}) custom-call(f32[8,8]{1,0:T(8,128)S(1)} %convolution_multiply_fusion.mix_ref, f32[16,2048]{1,0:T(8,128)S(1)} %shard_map.71.own_ref, f32[16,2048]{1,0:T(8,128)S(1)} %collective-permute-done.7.other_ref), custom_call_target="tpu_custom_call" | custom-call | flops 1000 | bytes 100000 | tf_op jit(solution)/shard_map/pallas_call | solution.py:374
  28.6 5.9 %collective-permute-start.9 = (f32[8,8960]{1,0:T(8,128)S(1)}, f32[8,8960]{1,0:T(8,128)S(1)}, u32[]{:S(2)}, u32[]{:S(2)}) collective-permute-start(f32[8,8960]{1,0:T(8,128)S(1)} %get-tuple-element.45), channel_id=1, source_target_pairs={{8,16},{16,8},{9,17},{17,9},{10,18},{18,10},{11,19},{19,11},{12,20... | collective-permute-start | bytes 860168 | tf_op jit(solution)/shard_map/ppermute | solution.py:339
  34.5 0.8 %collective-permute-start.13 = (f32[16,2048]{1,0:T(8,128)S(1)}, f32[16,2048]{1,0:T(8,128)S(1)}, u32[]{:S(2)}, u32[]{:S(2)}) collective-permute-start(f32[16,2048]{1,0:T(8,128)S(1)} %get-tuple-element.51), channel_id=1, source_target_pairs={{0,2},{1,3},{2,4},{3,5},{4,6},{5,7},{6,0},{7,1},{8,10},{9,11},{10,... | collective-permute-start | bytes 393224 | tf_op jit(solution)/shard_map/ppermute | solution.py:330
  35.3 3.3 %collective-permute-start.14 = (f32[16,2048]{1,0:T(8,128)S(1)}, f32[16,2048]{1,0:T(8,128)S(1)}, u32[]{:S(2)}, u32[]{:S(2)}) collective-permute-start(f32[16,2048]{1,0:T(8,128)S(1)} %get-tuple-element.52), channel_id=1, source_target_pairs={{0,4},{1,5},{2,6},{3,7},{4,0},{5,1},{6,2},{7,3},{8,12},{9,13},{10,... | collective-permute-start | bytes 393224 | tf_op jit(solution)/shard_map/ppermute | solution.py:330
  38.8 4.3 %shard_map.75 = (f32[5,8,512]{2,1,0:T(8,128)S(1)}, f32[5,8,512]{2,1,0:T(8,128)S(1)}, f32[5,8,512]{2,1,0:T(8,128)S(1)}, f32[5,8,512]{2,1,0:T(8,128)S(1)}) custom-call(f32[8,8]{1,0:T(8,128)S(1)} %convolution_multiply_fusion.mix_ref, f32[8,16,640]{2,1,0:T(8,128)S(1)} %get-tuple-element.38.source_ref, f32[8,8960]{1,0:T(8,128)S(1)} %collective-permute-done.8.near_ref, ...), custom_call_target="tpu_custom_call" | custom-call | flops 1000 | bytes 100000 | tf_op jit(solution)/shard_map/pallas_call | solution.py:379
  43.1 1.9 %collective-permute-start.10 = (f32[5,8,512]{2,1,0:T(8,128)S(1)}, f32[5,8,512]{2,1,0:T(8,128)S(1)}, u32[]{:S(2)}, u32[]{:S(2)}) collective-permute-start(f32[5,8,512]{2,1,0:T(8,128)S(1)} %get-tuple-element.47), channel_id=1, source_target_pairs={{0,2},{1,3},{2,4},{3,5},{4,6},{5,7},{6,0},{7,1},{8,10},{9,11},{10,... | collective-permute-start | bytes 245768 | tf_op jit(solution)/shard_map/ppermute | solution.py:330
  45.1 2.2 %collective-permute-start.11 = (f32[5,8,512]{2,1,0:T(8,128)S(1)}, f32[5,8,512]{2,1,0:T(8,128)S(1)}, u32[]{:S(2)}, u32[]{:S(2)}) collective-permute-start(f32[5,8,512]{2,1,0:T(8,128)S(1)} %get-tuple-element.48), channel_id=1, source_target_pairs={{0,4},{1,5},{2,6},{3,7},{4,0},{5,1},{6,2},{7,3},{8,12},{9,13},{10,... | collective-permute-start | bytes 245768 | tf_op jit(solution)/shard_map/ppermute | solution.py:330
  47.3 0.6 %collective-permute-start.12 = (f32[5,8,512]{2,1,0:T(8,128)S(1)}, f32[5,8,512]{2,1,0:T(8,128)S(1)}, u32[]{:S(2)}, u32[]{:S(2)}) collective-permute-start(f32[5,8,512]{2,1,0:T(8,128)S(1)} %get-tuple-element.49), channel_id=1, source_target_pairs={{0,6},{1,7},{2,0},{3,1},{4,2},{5,3},{6,4},{7,5},{8,14},{9,15},{10,... | collective-permute-start | bytes 245768 | tf_op jit(solution)/shard_map/ppermute | solution.py:330
  47.8 1.3 %collective-permute-done.10.p1 = f32[5,8,512]{2,1,0:T(8,128)S(1)} collective-permute-done((f32[5,8,512]{2,1,0:T(8,128)S(1)}, f32[5,8,512]{2,1,0:T(8,128)S(1)}, u32[]{:S(2)}, u32[]{:S(2)}) %collective-permute-start.10) | collective-permute-done | bytes 81952 | tf_op jit(solution)/shard_map/ppermute | solution.py:330
  49.1 2.8 %collective-permute-done.11.p2 = f32[5,8,512]{2,1,0:T(8,128)S(1)} collective-permute-done((f32[5,8,512]{2,1,0:T(8,128)S(1)}, f32[5,8,512]{2,1,0:T(8,128)S(1)}, u32[]{:S(2)}, u32[]{:S(2)}) %collective-permute-start.11) | collective-permute-done | bytes 81952 | tf_op jit(solution)/shard_map/ppermute | solution.py:330
  52.0 0.8 %shard_map.76 = (f32[16,2048]{1,0:T(8,128)}, f32[16,2048]{1,0:T(8,128)}) custom-call(f32[5,8,512]{2,1,0:T(8,128)S(1)} %get-tuple-element.46.p0, f32[5,8,512]{2,1,0:T(8,128)S(1)} %collective-permute-done.10.p1, f32[5,8,512]{2,1,0:T(8,128)S(1)} %collective-permute-done.11.p2, f32[5,8,512]{2,1,0:T(8,128)S(1)} %collective-permute-done.12.p3, ...), custom_call_target="tpu_custom_call" | custom-call | flops 1000 | bytes 100000 | tf_op jit(solution)/shard_map/pallas_call | solution.py:387
  (28 shorter events, 1.5 us)
Async XLA Ops:
  2.3 14.5 %collective-permute-start.3 = (f32[8,5120]{1,0:T(8,128)}, f32[8,5120]{1,0:T(8,128)S(1)}, u32[]{:S(2)}, u32[]{:S(2)}) collective-permute-start(f32[8,5120]{1,0:T(8,128)} %shard_map.68.sent_ref), channel_id=1, source_target_pairs={{0,1},{1,0},{2,3},{3,2},{4,5},{5,4},{6,7},{7,6},{8,9},{9,8},{10,11... | collective-permute-start | bytes 491528 | tf_op jit(solution)/shard_map/ppermute | solution.py:326
  9.6 0.9 %copy-start.1 = (f32[8,5120]{1,0:T(8,128)S(1)}, f32[8,5120]{1,0:T(8,128)}, u32[]{:S(2)}) copy-start(f32[8,5120]{1,0:T(8,128)} %shard_map.68.sent_ref) | copy-start | bytes 491524
  10.5 6.0 %copy-start.2 = (f32[1,16,2048]{2,1,0:T(8,128)S(1)}, f32[1,16,2048]{2,1,0:T(8,128)}, u32[]{:S(2)}) copy-start(f32[1,16,2048]{2,1,0:T(8,128)} %param.5) | copy-start | bytes 393220
  10.5 6.0 %copy-start = (f32[1,16,2048]{2,1,0:T(8,128)S(1)}, f32[1,16,2048]{2,1,0:T(8,128)}, u32[]{:S(2)}) copy-start(f32[1,16,2048]{2,1,0:T(8,128)} %param.6) | copy-start | bytes 393220
  10.7 6.1 %collective-permute-start = (f32[8,1792]{1,0:T(8,128)S(1)}, f32[8,1792]{1,0:T(8,128)S(1)}, u32[]{:S(2)}, u32[]{:S(2)}) collective-permute-start(f32[8,1792]{1,0:T(8,128)S(1)} %get-tuple-element.30), channel_id=1, source_target_pairs={{0,2},{1,3},{2,4},{3,5},{4,6},{5,7},{6,0},{7,1},{8,10},{9,11},{10,... | collective-permute-start | bytes 172040 | tf_op jit(solution)/shard_map/ppermute | solution.py:330
  12.3 7.4 %collective-permute-start.1 = (f32[8,1792]{1,0:T(8,128)S(1)}, f32[8,1792]{1,0:T(8,128)S(1)}, u32[]{:S(2)}, u32[]{:S(2)}) collective-permute-start(f32[8,1792]{1,0:T(8,128)S(1)} %get-tuple-element.32), channel_id=1, source_target_pairs={{0,4},{1,5},{2,6},{3,7},{4,0},{5,1},{6,2},{7,3},{8,12},{9,13},{10,... | collective-permute-start | bytes 172040 | tf_op jit(solution)/shard_map/ppermute | solution.py:330
  15.2 5.9 %collective-permute-start.2 = (f32[8,1792]{1,0:T(8,128)S(1)}, f32[8,1792]{1,0:T(8,128)S(1)}, u32[]{:S(2)}, u32[]{:S(2)}) collective-permute-start(f32[8,1792]{1,0:T(8,128)S(1)} %get-tuple-element.33), channel_id=1, source_target_pairs={{0,6},{1,7},{2,0},{3,1},{4,2},{5,3},{6,4},{7,5},{8,14},{9,15},{10,... | collective-permute-start | bytes 172040 | tf_op jit(solution)/shard_map/ppermute | solution.py:330
  16.7 11.1 %collective-permute-start.7 = (f32[16,2048]{1,0:T(8,128)S(1)}, f32[16,2048]{1,0:T(8,128)S(1)}, u32[]{:S(2)}, u32[]{:S(2)}) collective-permute-start(f32[16,2048]{1,0:T(8,128)S(1)} %shard_map.71.own_ref), channel_id=1, source_target_pairs={{0,1},{1,0},{2,3},{3,2},{4,5},{5,4},{6,7},{7,6},{8,9},{9,8},{10,11... | collective-permute-start | bytes 393224 | tf_op jit(solution)/shard_map/ppermute | solution.py:326
  16.8 4.1 %copy-start.4 = (f32[8,8]{1,0:T(8,128)S(1)}, f32[8,8]{1,0:T(8,128)}, u32[]{:S(2)}) copy-start(f32[8,8]{1,0:T(8,128)} %param.7) | copy-start | bytes 772
  17.0 6.9 %copy-start.3 = (s32[4096]{0:T(1024)S(1)}, s32[4096]{0:T(1024)}, u32[]{:S(2)}) copy-start(s32[4096]{0:T(1024)} %param.8) | copy-start | bytes 49156
  17.0 5.5 %collective-permute-start.4 = (f32[8,1792]{1,0:T(8,128)S(1)}, f32[8,1792]{1,0:T(8,128)S(1)}, u32[]{:S(2)}, u32[]{:S(2)}) collective-permute-start(f32[8,1792]{1,0:T(8,128)S(1)} %get-tuple-element.35), channel_id=1, source_target_pairs={{0,2},{1,3},{2,4},{3,5},{4,6},{5,7},{6,0},{7,1},{8,10},{9,11},{10,... | collective-permute-start | bytes 172040 | tf_op jit(solution)/shard_map/ppermute | solution.py:330
  17.7 5.7 %collective-permute-start.5 = (f32[8,1792]{1,0:T(8,128)S(1)}, f32[8,1792]{1,0:T(8,128)S(1)}, u32[]{:S(2)}, u32[]{:S(2)}) collective-permute-start(f32[8,1792]{1,0:T(8,128)S(1)} %get-tuple-element.36), channel_id=1, source_target_pairs={{0,4},{1,5},{2,6},{3,7},{4,0},{5,1},{6,2},{7,3},{8,12},{9,13},{10,... | collective-permute-start | bytes 172040 | tf_op jit(solution)/shard_map/ppermute | solution.py:330
  19.7 4.2 %collective-permute-start.6 = (f32[8,1792]{1,0:T(8,128)S(1)}, f32[8,1792]{1,0:T(8,128)S(1)}, u32[]{:S(2)}, u32[]{:S(2)}) collective-permute-start(f32[8,1792]{1,0:T(8,128)S(1)} %get-tuple-element.37), channel_id=1, source_target_pairs={{0,6},{1,7},{2,0},{3,1},{4,2},{5,3},{6,4},{7,5},{8,14},{9,15},{10,... | collective-permute-start | bytes 172040 | tf_op jit(solution)/shard_map/ppermute | solution.py:330
  28.5 10.2 %collective-permute-start.8 = (f32[8,8960]{1,0:T(8,128)S(1)}, f32[8,8960]{1,0:T(8,128)S(1)}, u32[]{:S(2)}, u32[]{:S(2)}) collective-permute-start(f32[8,8960]{1,0:T(8,128)S(1)} %get-tuple-element.44), channel_id=1, source_target_pairs={{0,8},{8,0},{1,9},{9,1},{2,10},{10,2},{3,11},{11,3},{4,12},{12,4},... | collective-permute-start | bytes 860168 | tf_op jit(solution)/shard_map/ppermute | solution.py:339
  28.6 10.2 %collective-permute-start.9 = (f32[8,8960]{1,0:T(8,128)S(1)}, f32[8,8960]{1,0:T(8,128)S(1)}, u32[]{:S(2)}, u32[]{:S(2)}) collective-permute-start(f32[8,8960]{1,0:T(8,128)S(1)} %get-tuple-element.45), channel_id=1, source_target_pairs={{8,16},{16,8},{9,17},{17,9},{10,18},{18,10},{11,19},{19,11},{12,20... | collective-permute-start | bytes 860168 | tf_op jit(solution)/shard_map/ppermute | solution.py:339
  34.5 12.8 %collective-permute-start.13 = (f32[16,2048]{1,0:T(8,128)S(1)}, f32[16,2048]{1,0:T(8,128)S(1)}, u32[]{:S(2)}, u32[]{:S(2)}) collective-permute-start(f32[16,2048]{1,0:T(8,128)S(1)} %get-tuple-element.51), channel_id=1, source_target_pairs={{0,2},{1,3},{2,4},{3,5},{4,6},{5,7},{6,0},{7,1},{8,10},{9,11},{10,... | collective-permute-start | bytes 393224 | tf_op jit(solution)/shard_map/ppermute | solution.py:330
  35.3 12.5 %collective-permute-start.14 = (f32[16,2048]{1,0:T(8,128)S(1)}, f32[16,2048]{1,0:T(8,128)S(1)}, u32[]{:S(2)}, u32[]{:S(2)}) collective-permute-start(f32[16,2048]{1,0:T(8,128)S(1)} %get-tuple-element.52), channel_id=1, source_target_pairs={{0,4},{1,5},{2,6},{3,7},{4,0},{5,1},{6,2},{7,3},{8,12},{9,13},{10,... | collective-permute-start | bytes 393224 | tf_op jit(solution)/shard_map/ppermute | solution.py:330
  38.6 9.2 %collective-permute-start.15 = (f32[16,2048]{1,0:T(8,128)S(1)}, f32[16,2048]{1,0:T(8,128)S(1)}, u32[]{:S(2)}, u32[]{:S(2)}) collective-permute-start(f32[16,2048]{1,0:T(8,128)S(1)} %get-tuple-element.53), channel_id=1, source_target_pairs={{0,6},{1,7},{2,0},{3,1},{4,2},{5,3},{6,4},{7,5},{8,14},{9,15},{10,... | collective-permute-start | bytes 393224 | tf_op jit(solution)/shard_map/ppermute | solution.py:330
  43.1 6.0 %collective-permute-start.10 = (f32[5,8,512]{2,1,0:T(8,128)S(1)}, f32[5,8,512]{2,1,0:T(8,128)S(1)}, u32[]{:S(2)}, u32[]{:S(2)}) collective-permute-start(f32[5,8,512]{2,1,0:T(8,128)S(1)} %get-tuple-element.47), channel_id=1, source_target_pairs={{0,2},{1,3},{2,4},{3,5},{4,6},{5,7},{6,0},{7,1},{8,10},{9,11},{10,... | collective-permute-start | bytes 245768 | tf_op jit(solution)/shard_map/ppermute | solution.py:330
  45.1 6.9 %collective-permute-start.11 = (f32[5,8,512]{2,1,0:T(8,128)S(1)}, f32[5,8,512]{2,1,0:T(8,128)S(1)}, u32[]{:S(2)}, u32[]{:S(2)}) collective-permute-start(f32[5,8,512]{2,1,0:T(8,128)S(1)} %get-tuple-element.48), channel_id=1, source_target_pairs={{0,4},{1,5},{2,6},{3,7},{4,0},{5,1},{6,2},{7,3},{8,12},{9,13},{10,... | collective-permute-start | bytes 245768 | tf_op jit(solution)/shard_map/ppermute | solution.py:330
  47.3 4.7 %collective-permute-start.12 = (f32[5,8,512]{2,1,0:T(8,128)S(1)}, f32[5,8,512]{2,1,0:T(8,128)S(1)}, u32[]{:S(2)}, u32[]{:S(2)}) collective-permute-start(f32[5,8,512]{2,1,0:T(8,128)S(1)} %get-tuple-element.49), channel_id=1, source_target_pairs={{0,6},{1,7},{2,0},{3,1},{4,2},{5,3},{6,4},{7,5},{8,14},{9,15},{10,... | collective-permute-start | bytes 245768 | tf_op jit(solution)/shard_map/ppermute | solution.py:330

commit v5 on v4

--- a/solution.py
+++ b/solution.py
@@ -199,6 +199,10 @@
     return pltpu.roll(u, 1, 0) + pltpu.roll(u, TALL - 1, 0) + pltpu.roll(u, 1, 1) + pltpu.roll(u, WIDE - 1, 1)
 
 
+def far_kernel(far_ref, out_ref):
+    out_ref[...] = far_ref[...]
+
+
 def main_kernel(mix_ref, source_ref, near_ref, far_ref, *refs):
     pieces, outs = (refs[:GROUPS], refs[GROUPS : 2 * GROUPS]), refs[2 * GROUPS : 3 * GROUPS]
     adj, kp, res, dirn, tmp, mask_ref = refs[3 * GROUPS :]
@@ -369,12 +373,14 @@
         9,
         scratch=[pltpu.VMEM((2 * VARS * ROWS, WIDE), jnp.float32)],
     )(obs_cell.reshape(1, OBS), *pieces)
+    far, other_shaped = lax.optimization_barrier((far, other_shaped))
     far = beside(far, tiles, False)
     shaped, other_shaped, _ = lax.optimization_barrier((shaped, other_shaped, source))
     mixed = call(share_kernel, [(ROWS, COLS)] * 4, 3, smem=1)(mix, shaped, other_shaped)
     near, first = lax.optimization_barrier((near, mixed[0]))
     near = beside(near, tiles, True)
     mixed = [first] + [around(mixed[k], k) for k in range(1, GROUPS)]
+    (far,) = call(far_kernel, [edges], 1, flops=1_000_000_000)(far)
     field = (VARS, TALL, WIDE)
     parts = call(
         main_kernel,

time: 53.2 us -> 52.7 us (level)
  starting transfers between devices: 32.1 us -> 31.2 us
  waiting for transfers between devices: 8.99 us -> 9.65 us
    ppermute x12, waiting for transfers between devices: 6.93 us -> 9.64 us  [around(): lax.ppermute(x, 'var', [(i, (i // 2 + k) % GROUPS * 2 + i % 2) for i in r...]
    ppermute x2, waiting for transfers between devices: 1.98 us -> 0.01 us  [across(): return lax.ppermute(x, 'var', [(i, i ^ 1) for i in range(VARS)])]
    ppermute x12, starting transfers between devices: 18.8 us -> 17.9 us  [around(): lax.ppermute(x, 'var', [(i, (i // 2 + k) % GROUPS * 2 + i % 2) for i in r...]
  transfers between devices with their start and end apart: 16 -> 16, of which waited for: 7 -> 7; matrix products, arithmetic and copies ran while one was open for 0% -> 0% of each run, Pallas kernels for 13% -> 14%
where the time goes in v5:
time: 52.7 us; the launch traced here: 52.6 us
  starting transfers between devices  31.2 us (59%)
  Pallas kernels  9.82 us (19%)
  waiting for transfers between devices  9.65 us (18%)
  local copies, waits for them, and re-layouts  0.97 us (2%)
  between operations  0.73 us (1%)
    ppermute x12, starting transfers between devices, around(): lax.ppermute(x, 'var', [(i, (i // 2 + k) % GROUPS * 2 + i % 2) for i in r...  17.9 us
    ppermute x12, waiting for transfers between devices, around(): lax.ppermute(x, 'var', [(i, (i // 2 + k) % GROUPS * 2 + i % 2) for i in r...  9.64 us
    ppermute x2, starting transfers between devices, across(): return lax.ppermute(x, 'var', [(i, i ^ 1) for i in range(VARS)])  7.28 us
    ppermute x2, starting transfers between devices, beside(): return lax.ppermute(x, ('tile', 'var'), pairs)  5.98 us
    pallas_call x1, Pallas kernels, per_device(): call(main_kernel, [(2 * ROWS // 8 + 1, 8, BLOCK)] * 4, 12, smem=1, scratc...  4.33 us
    pallas_call x1, Pallas kernels, per_device(): call(scatter_kernel, [(VARS, ROWS, WIDE), edges, edges], 9, scratch=[pltp...  1.97 us
    pallas_call x1, Pallas kernels, per_device(): call(first_kernel, [(8, EXTRA + 2 * BLOCK)], 3, hbm=3, limit=56, scratch=...  1.64 us
  transfers between devices with their start and end apart: 16, of which 7 were waited for; matrix products, arithmetic and copies ran while one was open for 0% of the time, Pallas kernels for 14%

profile of v5, /device:TPU:2, one launch (start us, length us, event | category | flops | bytes accessed | tf_op | source)
XLA Modules:
  0.0 52.6 jit_solution(13354292546079833158)
XLA Ops:
  0.6 1.6 %shard_map.68.sent_ref = f32[8,5120]{1,0:T(8,128)} custom-call(f32[16,2048]{1,0:T(8,128)} %bitcast.8, f32[1,4096]{1,0:T(1,128)} %obs_hbm.1, f32[16,2048]{1,0:T(8,128)} %bitcast.5), custom_call_target="tpu_custom_call" | custom-call | flops 1000 | bytes 100000 | tf_op jit(solution)/shard_map/pallas_call | solution.py:350
  2.3 7.3 %collective-permute-start.3 = (f32[8,5120]{1,0:T(8,128)}, f32[8,5120]{1,0:T(8,128)S(1)}, u32[]{:S(2)}, u32[]{:S(2)}) collective-permute-start(f32[8,5120]{1,0:T(8,128)} %shard_map.68.sent_ref), channel_id=1, source_target_pairs={{0,1},{1,0},{2,3},{3,2},{4,5},{5,4},{6,7},{7,6},{8,9},{9,8},{10,11... | collective-permute-start | bytes 491528 | tf_op jit(solution)/shard_map/ppermute | solution.py:330
  9.6 0.9 %copy-done.1 = f32[8,5120]{1,0:T(8,128)S(1)} copy-done((f32[8,5120]{1,0:T(8,128)S(1)}, f32[8,5120]{1,0:T(8,128)}, u32[]{:S(2)}) %copy-start.1) | copy-done | bytes 163864
  10.7 1.6 %collective-permute-start = (f32[8,1792]{1,0:T(8,128)S(1)}, f32[8,1792]{1,0:T(8,128)S(1)}, u32[]{:S(2)}, u32[]{:S(2)}) collective-permute-start(f32[8,1792]{1,0:T(8,128)S(1)} %get-tuple-element.32), channel_id=1, source_target_pairs={{0,2},{1,3},{2,4},{3,5},{4,6},{5,7},{6,0},{7,1},{8,10},{9,11},{10,... | collective-permute-start | bytes 172040 | tf_op jit(solution)/shard_map/ppermute | solution.py:334
  12.4 3.7 %collective-permute-done.refs_1_ = f32[8,1792]{1,0:T(8,128)S(1)} collective-permute-done((f32[8,1792]{1,0:T(8,128)S(1)}, f32[8,1792]{1,0:T(8,128)S(1)}, u32[]{:S(2)}, u32[]{:S(2)}) %collective-permute-start) | collective-permute-done | bytes 57376 | tf_op jit(solution)/shard_map/ppermute | solution.py:334
  16.1 2.0 %collective-permute-start.1 = (f32[8,1792]{1,0:T(8,128)S(1)}, f32[8,1792]{1,0:T(8,128)S(1)}, u32[]{:S(2)}, u32[]{:S(2)}) collective-permute-start(f32[8,1792]{1,0:T(8,128)S(1)} %get-tuple-element.34), channel_id=1, source_target_pairs={{0,4},{1,5},{2,6},{3,7},{4,0},{5,1},{6,2},{7,3},{8,12},{9,13},{10,... | collective-permute-start | bytes 172040 | tf_op jit(solution)/shard_map/ppermute | solution.py:334
  18.1 1.1 %collective-permute-start.2 = (f32[8,1792]{1,0:T(8,128)S(1)}, f32[8,1792]{1,0:T(8,128)S(1)}, u32[]{:S(2)}, u32[]{:S(2)}) collective-permute-start(f32[8,1792]{1,0:T(8,128)S(1)} %get-tuple-element.35), channel_id=1, source_target_pairs={{0,6},{1,7},{2,0},{3,1},{4,2},{5,3},{6,4},{7,5},{8,14},{9,15},{10,... | collective-permute-start | bytes 172040 | tf_op jit(solution)/shard_map/ppermute | solution.py:334
  19.3 1.0 %collective-permute-start.4 = (f32[8,1792]{1,0:T(8,128)S(1)}, f32[8,1792]{1,0:T(8,128)S(1)}, u32[]{:S(2)}, u32[]{:S(2)}) collective-permute-start(f32[8,1792]{1,0:T(8,128)S(1)} %get-tuple-element.37), channel_id=1, source_target_pairs={{0,2},{1,3},{2,4},{3,5},{4,6},{5,7},{6,0},{7,1},{8,10},{9,11},{10,... | collective-permute-start | bytes 172040 | tf_op jit(solution)/shard_map/ppermute | solution.py:334
  20.3 1.5 %collective-permute-start.5 = (f32[8,1792]{1,0:T(8,128)S(1)}, f32[8,1792]{1,0:T(8,128)S(1)}, u32[]{:S(2)}, u32[]{:S(2)}) collective-permute-start(f32[8,1792]{1,0:T(8,128)S(1)} %get-tuple-element.38), channel_id=1, source_target_pairs={{0,4},{1,5},{2,6},{3,7},{4,0},{5,1},{6,2},{7,3},{8,12},{9,13},{10,... | collective-permute-start | bytes 172040 | tf_op jit(solution)/shard_map/ppermute | solution.py:334
  21.9 1.8 %collective-permute-start.6 = (f32[8,1792]{1,0:T(8,128)S(1)}, f32[8,1792]{1,0:T(8,128)S(1)}, u32[]{:S(2)}, u32[]{:S(2)}) collective-permute-start(f32[8,1792]{1,0:T(8,128)S(1)} %get-tuple-element.39), channel_id=1, source_target_pairs={{0,6},{1,7},{2,0},{3,1},{4,2},{5,3},{6,4},{7,5},{8,14},{9,15},{10,... | collective-permute-start | bytes 172040 | tf_op jit(solution)/shard_map/ppermute | solution.py:334
  23.7 1.1 %collective-permute-done.4.refs_5_ = f32[8,1792]{1,0:T(8,128)S(1)} collective-permute-done((f32[8,1792]{1,0:T(8,128)S(1)}, f32[8,1792]{1,0:T(8,128)S(1)}, u32[]{:S(2)}, u32[]{:S(2)}) %collective-permute-start.4) | collective-permute-done | bytes 57376 | tf_op jit(solution)/shard_map/ppermute | solution.py:334
  24.7 1.3 %collective-permute-done.5.refs_6_ = f32[8,1792]{1,0:T(8,128)S(1)} collective-permute-done((f32[8,1792]{1,0:T(8,128)S(1)}, f32[8,1792]{1,0:T(8,128)S(1)}, u32[]{:S(2)}, u32[]{:S(2)}) %collective-permute-start.5) | collective-permute-done | bytes 57376 | tf_op jit(solution)/shard_map/ppermute | solution.py:334
  26.2 2.0 %shard_map.73 = (f32[8,16,640]{2,1,0:T(8,128)S(1)}, f32[8,8960]{1,0:T(8,128)S(1)}, f32[8,8960]{1,0:T(8,128)S(1)}) custom-call(s32[1,4096]{1,0:T(1,128)S(1)} %bitcast.10, f32[8,1792]{1,0:T(8,128)S(1)} %get-tuple-element.31.refs_0_, f32[8,1792]{1,0:T(8,128)S(1)} %collective-permute-done.refs_1_, f32[8,1792]{1,0:T(8,128)S(1)} %collective-permute-done.1.refs_2_, ...), custom_call_target="tpu_custom_call" | custom-call | flops 1000 | bytes 100000 | tf_op jit(solution)/shard_map/pallas_call | solution.py:370
  28.2 3.1 %collective-permute-start.9 = (f32[8,8960]{1,0:T(8,128)S(1)}, f32[8,8960]{1,0:T(8,128)S(1)}, u32[]{:S(2)}, u32[]{:S(2)}) collective-permute-start(f32[8,8960]{1,0:T(8,128)S(1)} %get-tuple-element.49), channel_id=1, source_target_pairs={{8,16},{16,8},{9,17},{17,9},{10,18},{18,10},{11,19},{19,11},{12,20... | collective-permute-start | bytes 860168 | tf_op jit(solution)/shard_map/ppermute | solution.py:343
  31.5 0.7 %shard_map.74 = (f32[16,2048]{1,0:T(8,128)S(1)}, f32[16,2048]{1,0:T(8,128)S(1)}, f32[16,2048]{1,0:T(8,128)S(1)}, f32[16,2048]{1,0:T(8,128)S(1)}) custom-call(f32[8,8]{1,0:T(8,128)S(1)} %convolution_multiply_fusion.mix_ref, f32[16,2048]{1,0:T(8,128)S(1)} %shard_map.71.own_ref, f32[16,2048]{1,0:T(8,128)S(1)} %collective-permute-done.7.other_ref), custom_call_target="tpu_custom_call" | custom-call | flops 1000 | bytes 100000 | tf_op jit(solution)/shard_map/pallas_call | solution.py:379
  32.2 2.9 %collective-permute-start.8 = (f32[8,8960]{1,0:T(8,128)S(1)}, f32[8,8960]{1,0:T(8,128)S(1)}, u32[]{:S(2)}, u32[]{:S(2)}) collective-permute-start(f32[8,8960]{1,0:T(8,128)S(1)} %get-tuple-element.48), channel_id=1, source_target_pairs={{0,8},{8,0},{1,9},{9,1},{2,10},{10,2},{3,11},{11,3},{4,12},{12,4},... | collective-permute-start | bytes 860168 | tf_op jit(solution)/shard_map/ppermute | solution.py:343
  35.3 3.8 %collective-permute-start.14 = (f32[16,2048]{1,0:T(8,128)S(1)}, f32[16,2048]{1,0:T(8,128)S(1)}, u32[]{:S(2)}, u32[]{:S(2)}) collective-permute-start(f32[16,2048]{1,0:T(8,128)S(1)} %get-tuple-element.56), channel_id=1, source_target_pairs={{0,4},{1,5},{2,6},{3,7},{4,0},{5,1},{6,2},{7,3},{8,12},{9,13},{10,... | collective-permute-start | bytes 393224 | tf_op jit(solution)/shard_map/ppermute | solution.py:334
  39.3 4.3 %shard_map.76 = (f32[5,8,512]{2,1,0:T(8,128)S(1)}, f32[5,8,512]{2,1,0:T(8,128)S(1)}, f32[5,8,512]{2,1,0:T(8,128)S(1)}, f32[5,8,512]{2,1,0:T(8,128)S(1)}) custom-call(f32[8,8]{1,0:T(8,128)S(1)} %convolution_multiply_fusion.mix_ref, f32[8,16,640]{2,1,0:T(8,128)S(1)} %get-tuple-element.40.source_ref, f32[8,8960]{1,0:T(8,128)S(1)} %collective-permute-done.8.near_ref, ...), custom_call_target="tpu_custom_call" | custom-call | flops 1000 | bytes 100000 | tf_op jit(solution)/shard_map/pallas_call | solution.py:385
  43.6 2.0 %collective-permute-start.10 = (f32[5,8,512]{2,1,0:T(8,128)S(1)}, f32[5,8,512]{2,1,0:T(8,128)S(1)}, u32[]{:S(2)}, u32[]{:S(2)}) collective-permute-start(f32[5,8,512]{2,1,0:T(8,128)S(1)} %get-tuple-element.51), channel_id=1, source_target_pairs={{0,2},{1,3},{2,4},{3,5},{4,6},{5,7},{6,0},{7,1},{8,10},{9,11},{10,... | collective-permute-start | bytes 245768 | tf_op jit(solution)/shard_map/ppermute | solution.py:334
  45.6 1.4 %collective-permute-start.11 = (f32[5,8,512]{2,1,0:T(8,128)S(1)}, f32[5,8,512]{2,1,0:T(8,128)S(1)}, u32[]{:S(2)}, u32[]{:S(2)}) collective-permute-start(f32[5,8,512]{2,1,0:T(8,128)S(1)} %get-tuple-element.52), channel_id=1, source_target_pairs={{0,4},{1,5},{2,6},{3,7},{4,0},{5,1},{6,2},{7,3},{8,12},{9,13},{10,... | collective-permute-start | bytes 245768 | tf_op jit(solution)/shard_map/ppermute | solution.py:334
  47.0 1.3 %collective-permute-start.12 = (f32[5,8,512]{2,1,0:T(8,128)S(1)}, f32[5,8,512]{2,1,0:T(8,128)S(1)}, u32[]{:S(2)}, u32[]{:S(2)}) collective-permute-start(f32[5,8,512]{2,1,0:T(8,128)S(1)} %get-tuple-element.53), channel_id=1, source_target_pairs={{0,6},{1,7},{2,0},{3,1},{4,2},{5,3},{6,4},{7,5},{8,14},{9,15},{10,... | collective-permute-start | bytes 245768 | tf_op jit(solution)/shard_map/ppermute | solution.py:334
  48.4 1.6 %collective-permute-done.10.p1 = f32[5,8,512]{2,1,0:T(8,128)S(1)} collective-permute-done((f32[5,8,512]{2,1,0:T(8,128)S(1)}, f32[5,8,512]{2,1,0:T(8,128)S(1)}, u32[]{:S(2)}, u32[]{:S(2)}) %collective-permute-start.10) | collective-permute-done | bytes 81952 | tf_op jit(solution)/shard_map/ppermute | solution.py:334
  50.0 1.5 %collective-permute-done.11.p2 = f32[5,8,512]{2,1,0:T(8,128)S(1)} collective-permute-done((f32[5,8,512]{2,1,0:T(8,128)S(1)}, f32[5,8,512]{2,1,0:T(8,128)S(1)}, u32[]{:S(2)}, u32[]{:S(2)}) %collective-permute-start.11) | collective-permute-done | bytes 81952 | tf_op jit(solution)/shard_map/ppermute | solution.py:334
  51.8 0.8 %shard_map.77 = (f32[16,2048]{1,0:T(8,128)}, f32[16,2048]{1,0:T(8,128)}) custom-call(f32[5,8,512]{2,1,0:T(8,128)S(1)} %get-tuple-element.50.p0, f32[5,8,512]{2,1,0:T(8,128)S(1)} %collective-permute-done.10.p1, f32[5,8,512]{2,1,0:T(8,128)S(1)} %collective-permute-done.11.p2, f32[5,8,512]{2,1,0:T(8,128)S(1)} %collective-permute-done.12.p3, ...), custom_call_target="tpu_custom_call" | custom-call | flops 1000 | bytes 100000 | tf_op jit(solution)/shard_map/pallas_call | solution.py:393
  (29 shorter events, 1.5 us)
Async XLA Ops:
  2.3 16.9 %collective-permute-start.3 = (f32[8,5120]{1,0:T(8,128)}, f32[8,5120]{1,0:T(8,128)S(1)}, u32[]{:S(2)}, u32[]{:S(2)}) collective-permute-start(f32[8,5120]{1,0:T(8,128)} %shard_map.68.sent_ref), channel_id=1, source_target_pairs={{0,1},{1,0},{2,3},{3,2},{4,5},{5,4},{6,7},{7,6},{8,9},{9,8},{10,11... | collective-permute-start | bytes 491528 | tf_op jit(solution)/shard_map/ppermute | solution.py:330
  9.6 0.9 %copy-start.1 = (f32[8,5120]{1,0:T(8,128)S(1)}, f32[8,5120]{1,0:T(8,128)}, u32[]{:S(2)}) copy-start(f32[8,5120]{1,0:T(8,128)} %shard_map.68.sent_ref) | copy-start | bytes 491524
  10.5 1.8 %copy-start.2 = (f32[1,16,2048]{2,1,0:T(8,128)S(1)}, f32[1,16,2048]{2,1,0:T(8,128)}, u32[]{:S(2)}) copy-start(f32[1,16,2048]{2,1,0:T(8,128)} %param.5) | copy-start | bytes 393220
  10.5 1.8 %copy-start = (f32[1,16,2048]{2,1,0:T(8,128)S(1)}, f32[1,16,2048]{2,1,0:T(8,128)}, u32[]{:S(2)}) copy-start(f32[1,16,2048]{2,1,0:T(8,128)} %param.6) | copy-start | bytes 393220
  10.7 5.4 %collective-permute-start = (f32[8,1792]{1,0:T(8,128)S(1)}, f32[8,1792]{1,0:T(8,128)S(1)}, u32[]{:S(2)}, u32[]{:S(2)}) collective-permute-start(f32[8,1792]{1,0:T(8,128)S(1)} %get-tuple-element.32), channel_id=1, source_target_pairs={{0,2},{1,3},{2,4},{3,5},{4,6},{5,7},{6,0},{7,1},{8,10},{9,11},{10,... | collective-permute-start | bytes 172040 | tf_op jit(solution)/shard_map/ppermute | solution.py:334
  16.1 12.1 %collective-permute-start.7 = (f32[16,2048]{1,0:T(8,128)S(1)}, f32[16,2048]{1,0:T(8,128)S(1)}, u32[]{:S(2)}, u32[]{:S(2)}) collective-permute-start(f32[16,2048]{1,0:T(8,128)S(1)} %shard_map.71.own_ref), channel_id=1, source_target_pairs={{0,1},{1,0},{2,3},{3,2},{4,5},{5,4},{6,7},{7,6},{8,9},{9,8},{10,11... | collective-permute-start | bytes 393224 | tf_op jit(solution)/shard_map/ppermute | solution.py:330
  16.1 5.7 %collective-permute-start.1 = (f32[8,1792]{1,0:T(8,128)S(1)}, f32[8,1792]{1,0:T(8,128)S(1)}, u32[]{:S(2)}, u32[]{:S(2)}) collective-permute-start(f32[8,1792]{1,0:T(8,128)S(1)} %get-tuple-element.34), channel_id=1, source_target_pairs={{0,4},{1,5},{2,6},{3,7},{4,0},{5,1},{6,2},{7,3},{8,12},{9,13},{10,... | collective-permute-start | bytes 172040 | tf_op jit(solution)/shard_map/ppermute | solution.py:334
  18.1 5.6 %collective-permute-start.2 = (f32[8,1792]{1,0:T(8,128)S(1)}, f32[8,1792]{1,0:T(8,128)S(1)}, u32[]{:S(2)}, u32[]{:S(2)}) collective-permute-start(f32[8,1792]{1,0:T(8,128)S(1)} %get-tuple-element.35), channel_id=1, source_target_pairs={{0,6},{1,7},{2,0},{3,1},{4,2},{5,3},{6,4},{7,5},{8,14},{9,15},{10,... | collective-permute-start | bytes 172040 | tf_op jit(solution)/shard_map/ppermute | solution.py:334
  19.2 7.0 %copy-start.3 = (s32[4096]{0:T(1024)S(1)}, s32[4096]{0:T(1024)}, u32[]{:S(2)}) copy-start(s32[4096]{0:T(1024)} %param.8) | copy-start | bytes 49156
  19.3 5.4 %collective-permute-start.4 = (f32[8,1792]{1,0:T(8,128)S(1)}, f32[8,1792]{1,0:T(8,128)S(1)}, u32[]{:S(2)}, u32[]{:S(2)}) collective-permute-start(f32[8,1792]{1,0:T(8,128)S(1)} %get-tuple-element.37), channel_id=1, source_target_pairs={{0,2},{1,3},{2,4},{3,5},{4,6},{5,7},{6,0},{7,1},{8,10},{9,11},{10,... | collective-permute-start | bytes 172040 | tf_op jit(solution)/shard_map/ppermute | solution.py:334
  20.3 5.7 %collective-permute-start.5 = (f32[8,1792]{1,0:T(8,128)S(1)}, f32[8,1792]{1,0:T(8,128)S(1)}, u32[]{:S(2)}, u32[]{:S(2)}) collective-permute-start(f32[8,1792]{1,0:T(8,128)S(1)} %get-tuple-element.38), channel_id=1, source_target_pairs={{0,4},{1,5},{2,6},{3,7},{4,0},{5,1},{6,2},{7,3},{8,12},{9,13},{10,... | collective-permute-start | bytes 172040 | tf_op jit(solution)/shard_map/ppermute | solution.py:334
  21.9 4.3 %collective-permute-start.6 = (f32[8,1792]{1,0:T(8,128)S(1)}, f32[8,1792]{1,0:T(8,128)S(1)}, u32[]{:S(2)}, u32[]{:S(2)}) collective-permute-start(f32[8,1792]{1,0:T(8,128)S(1)} %get-tuple-element.39), channel_id=1, source_target_pairs={{0,6},{1,7},{2,0},{3,1},{4,2},{5,3},{6,4},{7,5},{8,14},{9,15},{10,... | collective-permute-start | bytes 172040 | tf_op jit(solution)/shard_map/ppermute | solution.py:334
  26.2 5.1 %copy-start.4 = (f32[8,8]{1,0:T(8,128)S(1)}, f32[8,8]{1,0:T(8,128)}, u32[]{:S(2)}) copy-start(f32[8,8]{1,0:T(8,128)} %param.7) | copy-start | bytes 772
  28.2 11.0 %collective-permute-start.9 = (f32[8,8960]{1,0:T(8,128)S(1)}, f32[8,8960]{1,0:T(8,128)S(1)}, u32[]{:S(2)}, u32[]{:S(2)}) collective-permute-start(f32[8,8960]{1,0:T(8,128)S(1)} %get-tuple-element.49), channel_id=1, source_target_pairs={{8,16},{16,8},{9,17},{17,9},{10,18},{18,10},{11,19},{19,11},{12,20... | collective-permute-start | bytes 860168 | tf_op jit(solution)/shard_map/ppermute | solution.py:343
  32.2 7.0 %collective-permute-start.8 = (f32[8,8960]{1,0:T(8,128)S(1)}, f32[8,8960]{1,0:T(8,128)S(1)}, u32[]{:S(2)}, u32[]{:S(2)}) collective-permute-start(f32[8,8960]{1,0:T(8,128)S(1)} %get-tuple-element.48), channel_id=1, source_target_pairs={{0,8},{8,0},{1,9},{9,1},{2,10},{10,2},{3,11},{11,3},{4,12},{12,4},... | collective-permute-start | bytes 860168 | tf_op jit(solution)/shard_map/ppermute | solution.py:343
  35.1 11.9 %collective-permute-start.13 = (f32[16,2048]{1,0:T(8,128)S(1)}, f32[16,2048]{1,0:T(8,128)S(1)}, u32[]{:S(2)}, u32[]{:S(2)}) collective-permute-start(f32[16,2048]{1,0:T(8,128)S(1)} %get-tuple-element.55), channel_id=1, source_target_pairs={{0,2},{1,3},{2,4},{3,5},{4,6},{5,7},{6,0},{7,1},{8,10},{9,11},{10,... | collective-permute-start | bytes 393224 | tf_op jit(solution)/shard_map/ppermute | solution.py:334
  35.3 13.1 %collective-permute-start.14 = (f32[16,2048]{1,0:T(8,128)S(1)}, f32[16,2048]{1,0:T(8,128)S(1)}, u32[]{:S(2)}, u32[]{:S(2)}) collective-permute-start(f32[16,2048]{1,0:T(8,128)S(1)} %get-tuple-element.56), channel_id=1, source_target_pairs={{0,4},{1,5},{2,6},{3,7},{4,0},{5,1},{6,2},{7,3},{8,12},{9,13},{10,... | collective-permute-start | bytes 393224 | tf_op jit(solution)/shard_map/ppermute | solution.py:334
  39.1 9.3 %collective-permute-start.15 = (f32[16,2048]{1,0:T(8,128)S(1)}, f32[16,2048]{1,0:T(8,128)S(1)}, u32[]{:S(2)}, u32[]{:S(2)}) collective-permute-start(f32[16,2048]{1,0:T(8,128)S(1)} %get-tuple-element.57), channel_id=1, source_target_pairs={{0,6},{1,7},{2,0},{3,1},{4,2},{5,3},{6,4},{7,5},{8,14},{9,15},{10,... | collective-permute-start | bytes 393224 | tf_op jit(solution)/shard_map/ppermute | solution.py:334
  43.6 6.4 %collective-permute-start.10 = (f32[5,8,512]{2,1,0:T(8,128)S(1)}, f32[5,8,512]{2,1,0:T(8,128)S(1)}, u32[]{:S(2)}, u32[]{:S(2)}) collective-permute-start(f32[5,8,512]{2,1,0:T(8,128)S(1)} %get-tuple-element.51), channel_id=1, source_target_pairs={{0,2},{1,3},{2,4},{3,5},{4,6},{5,7},{6,0},{7,1},{8,10},{9,11},{10,... | collective-permute-start | bytes 245768 | tf_op jit(solution)/shard_map/ppermute | solution.py:334
  45.6 5.9 %collective-permute-start.11 = (f32[5,8,512]{2,1,0:T(8,128)S(1)}, f32[5,8,512]{2,1,0:T(8,128)S(1)}, u32[]{:S(2)}, u32[]{:S(2)}) collective-permute-start(f32[5,8,512]{2,1,0:T(8,128)S(1)} %get-tuple-element.52), channel_id=1, source_target_pairs={{0,4},{1,5},{2,6},{3,7},{4,0},{5,1},{6,2},{7,3},{8,12},{9,13},{10,... | collective-permute-start | bytes 245768 | tf_op jit(solution)/shard_map/ppermute | solution.py:334
  47.0 4.8 %collective-permute-start.12 = (f32[5,8,512]{2,1,0:T(8,128)S(1)}, f32[5,8,512]{2,1,0:T(8,128)S(1)}, u32[]{:S(2)}, u32[]{:S(2)}) collective-permute-start(f32[5,8,512]{2,1,0:T(8,128)S(1)} %get-tuple-element.53), channel_id=1, source_target_pairs={{0,6},{1,7},{2,0},{3,1},{4,2},{5,3},{6,4},{7,5},{8,14},{9,15},{10,... | collective-permute-start | bytes 245768 | tf_op jit(solution)/shard_map/ppermute | solution.py:334

commit v6 on v5

--- a/solution.py
+++ b/solution.py
@@ -288,29 +288,34 @@
             for w in range(1, VARS):
                 near = near + mix_ref[v, w] * near_ref[w : w + 1, here]
                 far = far + mix_ref[v, w] * far_ref[w : w + 1, here]
-            out[4, 0:1, cols] = jnp.where(core == 0, far, near)
-            out[4, 1:2, cols] = jnp.where(core == 0, near, far)
-            out[4, 2:, cols] = jnp.zeros((6, 128), jnp.float32)
+            i = c // SIDE
+            out[i : i + 1, 4 * BLOCK :] = jnp.where(core == 0, far, near)
+            out[4 + i : 5 + i, 4 * BLOCK :] = jnp.where(core == 0, near, far)
             for half in range(ROWS // 8):
                 rows = slice(half * 8, half * 8 + 8)
                 total = mix_ref[v, 0] * tmp[0, rows, cols]
                 for w in range(1, VARS):
                     total = total + mix_ref[v, w] * tmp[w, rows, cols]
-                out[half, :, cols] = adj[v, rows, cols]
-                out[2 + half, :, cols] = total
+                out[:, half * BLOCK + c : half * BLOCK + c + 128] = adj[v, rows, cols]
+                out[:, (2 + half) * BLOCK + c : (2 + half) * BLOCK + c + 128] = total
 
 
 def join_kernel(p0, p1, p2, p3, m0, m1, m2, m3, state_ref, adjoint_ref, grad_ref):
     y, _ = group_place()
-    row = lax.broadcasted_iota(jnp.int32, (8, BLOCK), 0)
+    row = lax.broadcasted_iota(jnp.int32, (8, SIDE), 0)
     for k, part in enumerate((p0, p1, p2, p3)):
-        cols = pl.ds(pl.multiple_of(behind(y, k) * BLOCK, BLOCK), BLOCK)
         for half in range(ROWS // 8):
             rows = slice(half * 8, half * 8 + 8)
-            mixed = (m0[rows, cols] + m1[rows, cols]) + (m2[rows, cols] + m3[rows, cols])
-            mixed = mixed - jnp.where(row == 7 * half, part[4, half : half + 1], 0.0)
-            adjoint_ref[rows, cols] = part[half]
-            grad_ref[rows, cols] = -(part[2 + half] * state_ref[rows, cols] + part[half] * mixed)
+            for i in range(BLOCK // SIDE):
+                cols = lanes_at(behind(y, k) * BLOCK + i * SIDE, SIDE)
+                mixed = (m0[rows, cols] + m1[rows, cols]) + (m2[rows, cols] + m3[rows, cols])
+                edge = 4 * half + i
+                mixed = mixed - jnp.where(row == 7 * half, part[edge : edge + 1, 4 * BLOCK :], 0.0)
+                at = half * BLOCK + i * SIDE
+                adjoint = part[:, at : at + SIDE]
+                at += 2 * BLOCK
+                adjoint_ref[rows, cols] = adjoint
+                grad_ref[rows, cols] = -(part[:, at : at + SIDE] * state_ref[rows, cols] + adjoint * mixed)
 
 
 def call(kernel, outs, n_in, smem=0, scratch=(), flops=1000, size=100000, hbm=0, limit=32):
@@ -384,7 +389,7 @@
     field = (VARS, TALL, WIDE)
     parts = call(
         main_kernel,
-        [(2 * ROWS // 8 + 1, 8, BLOCK)] * 4,
+        [(8, 4 * BLOCK + SIDE)] * 4,
         12,
         smem=1,
         scratch=[pltpu.VMEM(field, jnp.float32)] * 5 + [pltpu.VMEM((TALL, WIDE), jnp.float32)],

time: 52.7 us -> 52.4 us (level)
  transfers between devices with their start and end apart: 16 -> 16, of which waited for: 7 -> 6; matrix products, arithmetic and copies ran while one was open for 0% -> 0% of each run, Pallas kernels for 14% -> 14%
where the time goes in v6:
time: 52.4 us; the launch traced here: 52.2 us
  starting transfers between devices  31.2 us (60%)
  Pallas kernels  9.85 us (19%)
  waiting for transfers between devices  9.26 us (18%)
  local copies, waits for them, and re-layouts  0.97 us (2%)
  between operations  0.73 us (1%)
    ppermute x12, starting transfers between devices, around(): lax.ppermute(x, 'var', [(i, (i // 2 + k) % GROUPS * 2 + i % 2) for i in r...  17.9 us
    ppermute x12, waiting for transfers between devices, around(): lax.ppermute(x, 'var', [(i, (i // 2 + k) % GROUPS * 2 + i % 2) for i in r...  9.25 us
    ppermute x2, starting transfers between devices, across(): return lax.ppermute(x, 'var', [(i, i ^ 1) for i in range(VARS)])  7.28 us
    ppermute x2, starting transfers between devices, beside(): return lax.ppermute(x, ('tile', 'var'), pairs)  5.98 us
    pallas_call x1, Pallas kernels, per_device(): call(main_kernel, [(8, 4 * BLOCK + SIDE)] * 4, 12, smem=1, scratch=[pltpu...  4.33 us
    pallas_call x1, Pallas kernels, per_device(): call(scatter_kernel, [(VARS, ROWS, WIDE), edges, edges], 9, scratch=[pltp...  1.97 us
    pallas_call x1, Pallas kernels, per_device(): call(first_kernel, [(8, EXTRA + 2 * BLOCK)], 3, hbm=3, limit=56, scratch=...  1.64 us
  transfers between devices with their start and end apart: 16, of which 6 were waited for; matrix products, arithmetic and copies ran while one was open for 0% of the time, Pallas kernels for 14%

profile of v6, /device:TPU:2, one launch (start us, length us, event | category | flops | bytes accessed | tf_op | source)
XLA Modules:
  0.0 52.2 jit_solution(4668921091198617476)
XLA Ops:
  0.6 1.6 %shard_map.68.sent_ref = f32[8,5120]{1,0:T(8,128)} custom-call(f32[16,2048]{1,0:T(8,128)} %bitcast.8, f32[1,4096]{1,0:T(1,128)} %obs_hbm.1, f32[16,2048]{1,0:T(8,128)} %bitcast.5), custom_call_target="tpu_custom_call" | custom-call | flops 1000 | bytes 100000 | tf_op jit(solution)/shard_map/pallas_call | solution.py:355
  2.3 7.3 %collective-permute-start.3 = (f32[8,5120]{1,0:T(8,128)}, f32[8,5120]{1,0:T(8,128)S(1)}, u32[]{:S(2)}, u32[]{:S(2)}) collective-permute-start(f32[8,5120]{1,0:T(8,128)} %shard_map.68.sent_ref), channel_id=1, source_target_pairs={{0,1},{1,0},{2,3},{3,2},{4,5},{5,4},{6,7},{7,6},{8,9},{9,8},{10,11... | collective-permute-start | bytes 491528 | tf_op jit(solution)/shard_map/ppermute | solution.py:335
  9.6 0.9 %copy-done.1 = f32[8,5120]{1,0:T(8,128)S(1)} copy-done((f32[8,5120]{1,0:T(8,128)S(1)}, f32[8,5120]{1,0:T(8,128)}, u32[]{:S(2)}) %copy-start.1) | copy-done | bytes 163864
  10.7 1.6 %collective-permute-start = (f32[8,1792]{1,0:T(8,128)S(1)}, f32[8,1792]{1,0:T(8,128)S(1)}, u32[]{:S(2)}, u32[]{:S(2)}) collective-permute-start(f32[8,1792]{1,0:T(8,128)S(1)} %get-tuple-element.32), channel_id=1, source_target_pairs={{0,2},{1,3},{2,4},{3,5},{4,6},{5,7},{6,0},{7,1},{8,10},{9,11},{10,... | collective-permute-start | bytes 172040 | tf_op jit(solution)/shard_map/ppermute | solution.py:339
  12.4 3.7 %collective-permute-done.refs_1_ = f32[8,1792]{1,0:T(8,128)S(1)} collective-permute-done((f32[8,1792]{1,0:T(8,128)S(1)}, f32[8,1792]{1,0:T(8,128)S(1)}, u32[]{:S(2)}, u32[]{:S(2)}) %collective-permute-start) | collective-permute-done | bytes 57376 | tf_op jit(solution)/shard_map/ppermute | solution.py:339
  16.1 2.0 %collective-permute-start.1 = (f32[8,1792]{1,0:T(8,128)S(1)}, f32[8,1792]{1,0:T(8,128)S(1)}, u32[]{:S(2)}, u32[]{:S(2)}) collective-permute-start(f32[8,1792]{1,0:T(8,128)S(1)} %get-tuple-element.34), channel_id=1, source_target_pairs={{0,4},{1,5},{2,6},{3,7},{4,0},{5,1},{6,2},{7,3},{8,12},{9,13},{10,... | collective-permute-start | bytes 172040 | tf_op jit(solution)/shard_map/ppermute | solution.py:339
  18.1 1.1 %collective-permute-start.2 = (f32[8,1792]{1,0:T(8,128)S(1)}, f32[8,1792]{1,0:T(8,128)S(1)}, u32[]{:S(2)}, u32[]{:S(2)}) collective-permute-start(f32[8,1792]{1,0:T(8,128)S(1)} %get-tuple-element.35), channel_id=1, source_target_pairs={{0,6},{1,7},{2,0},{3,1},{4,2},{5,3},{6,4},{7,5},{8,14},{9,15},{10,... | collective-permute-start | bytes 172040 | tf_op jit(solution)/shard_map/ppermute | solution.py:339
  19.3 1.0 %collective-permute-start.4 = (f32[8,1792]{1,0:T(8,128)S(1)}, f32[8,1792]{1,0:T(8,128)S(1)}, u32[]{:S(2)}, u32[]{:S(2)}) collective-permute-start(f32[8,1792]{1,0:T(8,128)S(1)} %get-tuple-element.37), channel_id=1, source_target_pairs={{0,2},{1,3},{2,4},{3,5},{4,6},{5,7},{6,0},{7,1},{8,10},{9,11},{10,... | collective-permute-start | bytes 172040 | tf_op jit(solution)/shard_map/ppermute | solution.py:339
  20.3 1.5 %collective-permute-start.5 = (f32[8,1792]{1,0:T(8,128)S(1)}, f32[8,1792]{1,0:T(8,128)S(1)}, u32[]{:S(2)}, u32[]{:S(2)}) collective-permute-start(f32[8,1792]{1,0:T(8,128)S(1)} %get-tuple-element.38), channel_id=1, source_target_pairs={{0,4},{1,5},{2,6},{3,7},{4,0},{5,1},{6,2},{7,3},{8,12},{9,13},{10,... | collective-permute-start | bytes 172040 | tf_op jit(solution)/shard_map/ppermute | solution.py:339
  21.9 1.8 %collective-permute-start.6 = (f32[8,1792]{1,0:T(8,128)S(1)}, f32[8,1792]{1,0:T(8,128)S(1)}, u32[]{:S(2)}, u32[]{:S(2)}) collective-permute-start(f32[8,1792]{1,0:T(8,128)S(1)} %get-tuple-element.39), channel_id=1, source_target_pairs={{0,6},{1,7},{2,0},{3,1},{4,2},{5,3},{6,4},{7,5},{8,14},{9,15},{10,... | collective-permute-start | bytes 172040 | tf_op jit(solution)/shard_map/ppermute | solution.py:339
  23.7 1.1 %collective-permute-done.4.refs_5_ = f32[8,1792]{1,0:T(8,128)S(1)} collective-permute-done((f32[8,1792]{1,0:T(8,128)S(1)}, f32[8,1792]{1,0:T(8,128)S(1)}, u32[]{:S(2)}, u32[]{:S(2)}) %collective-permute-start.4) | collective-permute-done | bytes 57376 | tf_op jit(solution)/shard_map/ppermute | solution.py:339
  24.7 1.3 %collective-permute-done.5.refs_6_ = f32[8,1792]{1,0:T(8,128)S(1)} collective-permute-done((f32[8,1792]{1,0:T(8,128)S(1)}, f32[8,1792]{1,0:T(8,128)S(1)}, u32[]{:S(2)}, u32[]{:S(2)}) %collective-permute-start.5) | collective-permute-done | bytes 57376 | tf_op jit(solution)/shard_map/ppermute | solution.py:339
  26.2 2.0 %shard_map.73 = (f32[8,16,640]{2,1,0:T(8,128)S(1)}, f32[8,8960]{1,0:T(8,128)S(1)}, f32[8,8960]{1,0:T(8,128)S(1)}) custom-call(s32[1,4096]{1,0:T(1,128)S(1)} %bitcast.10, f32[8,1792]{1,0:T(8,128)S(1)} %get-tuple-element.31.refs_0_, f32[8,1792]{1,0:T(8,128)S(1)} %collective-permute-done.refs_1_, f32[8,1792]{1,0:T(8,128)S(1)} %collective-permute-done.1.refs_2_, ...), custom_call_target="tpu_custom_call" | custom-call | flops 1000 | bytes 100000 | tf_op jit(solution)/shard_map/pallas_call | solution.py:375
  28.2 3.1 %collective-permute-start.9 = (f32[8,8960]{1,0:T(8,128)S(1)}, f32[8,8960]{1,0:T(8,128)S(1)}, u32[]{:S(2)}, u32[]{:S(2)}) collective-permute-start(f32[8,8960]{1,0:T(8,128)S(1)} %get-tuple-element.49), channel_id=1, source_target_pairs={{8,16},{16,8},{9,17},{17,9},{10,18},{18,10},{11,19},{19,11},{12,20... | collective-permute-start | bytes 860168 | tf_op jit(solution)/shard_map/ppermute | solution.py:348
  31.5 0.7 %shard_map.74 = (f32[16,2048]{1,0:T(8,128)S(1)}, f32[16,2048]{1,0:T(8,128)S(1)}, f32[16,2048]{1,0:T(8,128)S(1)}, f32[16,2048]{1,0:T(8,128)S(1)}) custom-call(f32[8,8]{1,0:T(8,128)S(1)} %convolution_multiply_fusion.mix_ref, f32[16,2048]{1,0:T(8,128)S(1)} %shard_map.71.own_ref, f32[16,2048]{1,0:T(8,128)S(1)} %collective-permute-done.7.other_ref), custom_call_target="tpu_custom_call" | custom-call | flops 1000 | bytes 100000 | tf_op jit(solution)/shard_map/pallas_call | solution.py:384
  32.2 2.9 %collective-permute-start.8 = (f32[8,8960]{1,0:T(8,128)S(1)}, f32[8,8960]{1,0:T(8,128)S(1)}, u32[]{:S(2)}, u32[]{:S(2)}) collective-permute-start(f32[8,8960]{1,0:T(8,128)S(1)} %get-tuple-element.48), channel_id=1, source_target_pairs={{0,8},{8,0},{1,9},{9,1},{2,10},{10,2},{3,11},{11,3},{4,12},{12,4},... | collective-permute-start | bytes 860168 | tf_op jit(solution)/shard_map/ppermute | solution.py:348
  35.3 3.8 %collective-permute-start.14 = (f32[16,2048]{1,0:T(8,128)S(1)}, f32[16,2048]{1,0:T(8,128)S(1)}, u32[]{:S(2)}, u32[]{:S(2)}) collective-permute-start(f32[16,2048]{1,0:T(8,128)S(1)} %get-tuple-element.56), channel_id=1, source_target_pairs={{0,4},{1,5},{2,6},{3,7},{4,0},{5,1},{6,2},{7,3},{8,12},{9,13},{10,... | collective-permute-start | bytes 393224 | tf_op jit(solution)/shard_map/ppermute | solution.py:339
  39.3 4.3 %shard_map.76 = (f32[8,2176]{1,0:T(8,128)S(1)}, f32[8,2176]{1,0:T(8,128)S(1)}, f32[8,2176]{1,0:T(8,128)S(1)}, f32[8,2176]{1,0:T(8,128)S(1)}) custom-call(f32[8,8]{1,0:T(8,128)S(1)} %convolution_multiply_fusion.mix_ref, f32[8,16,640]{2,1,0:T(8,128)S(1)} %get-tuple-element.40.source_ref, f32[8,8960]{1,0:T(8,128)S(1)} %collective-permute-done.8.near_ref, ...), custom_call_target="tpu_custom_call" | custom-call | flops 1000 | bytes 100000 | tf_op jit(solution)/shard_map/pallas_call | solution.py:390
  43.6 2.0 %collective-permute-start.10 = (f32[8,2176]{1,0:T(8,128)S(1)}, f32[8,2176]{1,0:T(8,128)S(1)}, u32[]{:S(2)}, u32[]{:S(2)}) collective-permute-start(f32[8,2176]{1,0:T(8,128)S(1)} %get-tuple-element.51), channel_id=1, source_target_pairs={{0,2},{1,3},{2,4},{3,5},{4,6},{5,7},{6,0},{7,1},{8,10},{9,11},{10,... | collective-permute-start | bytes 208904 | tf_op jit(solution)/shard_map/ppermute | solution.py:339
  45.6 1.4 %collective-permute-start.11 = (f32[8,2176]{1,0:T(8,128)S(1)}, f32[8,2176]{1,0:T(8,128)S(1)}, u32[]{:S(2)}, u32[]{:S(2)}) collective-permute-start(f32[8,2176]{1,0:T(8,128)S(1)} %get-tuple-element.52), channel_id=1, source_target_pairs={{0,4},{1,5},{2,6},{3,7},{4,0},{5,1},{6,2},{7,3},{8,12},{9,13},{10,... | collective-permute-start | bytes 208904 | tf_op jit(solution)/shard_map/ppermute | solution.py:339
  47.0 1.3 %collective-permute-start.12 = (f32[8,2176]{1,0:T(8,128)S(1)}, f32[8,2176]{1,0:T(8,128)S(1)}, u32[]{:S(2)}, u32[]{:S(2)}) collective-permute-start(f32[8,2176]{1,0:T(8,128)S(1)} %get-tuple-element.53), channel_id=1, source_target_pairs={{0,6},{1,7},{2,0},{3,1},{4,2},{5,3},{6,4},{7,5},{8,14},{9,15},{10,... | collective-permute-start | bytes 208904 | tf_op jit(solution)/shard_map/ppermute | solution.py:339
  48.4 1.4 %collective-permute-done.10.p1 = f32[8,2176]{1,0:T(8,128)S(1)} collective-permute-done((f32[8,2176]{1,0:T(8,128)S(1)}, f32[8,2176]{1,0:T(8,128)S(1)}, u32[]{:S(2)}, u32[]{:S(2)}) %collective-permute-start.10) | collective-permute-done | bytes 69664 | tf_op jit(solution)/shard_map/ppermute | solution.py:339
  49.7 1.7 %collective-permute-done.11.p2 = f32[8,2176]{1,0:T(8,128)S(1)} collective-permute-done((f32[8,2176]{1,0:T(8,128)S(1)}, f32[8,2176]{1,0:T(8,128)S(1)}, u32[]{:S(2)}, u32[]{:S(2)}) %collective-permute-start.11) | collective-permute-done | bytes 69664 | tf_op jit(solution)/shard_map/ppermute | solution.py:339
  51.4 0.8 %shard_map.77 = (f32[16,2048]{1,0:T(8,128)}, f32[16,2048]{1,0:T(8,128)}) custom-call(f32[8,2176]{1,0:T(8,128)S(1)} %get-tuple-element.50.p0, f32[8,2176]{1,0:T(8,128)S(1)} %collective-permute-done.10.p1, f32[8,2176]{1,0:T(8,128)S(1)} %collective-permute-done.11.p2, f32[8,2176]{1,0:T(8,128)S(1)} %collective-permute-done.12.p3, ...), custom_call_target="tpu_custom_call" | custom-call | flops 1000 | bytes 100000 | tf_op jit(solution)/shard_map/pallas_call | solution.py:398
  (29 shorter events, 1.2 us)
Async XLA Ops:
  2.3 16.9 %collective-permute-start.3 = (f32[8,5120]{1,0:T(8,128)}, f32[8,5120]{1,0:T(8,128)S(1)}, u32[]{:S(2)}, u32[]{:S(2)}) collective-permute-start(f32[8,5120]{1,0:T(8,128)} %shard_map.68.sent_ref), channel_id=1, source_target_pairs={{0,1},{1,0},{2,3},{3,2},{4,5},{5,4},{6,7},{7,6},{8,9},{9,8},{10,11... | collective-permute-start | bytes 491528 | tf_op jit(solution)/shard_map/ppermute | solution.py:335
  9.6 0.9 %copy-start.1 = (f32[8,5120]{1,0:T(8,128)S(1)}, f32[8,5120]{1,0:T(8,128)}, u32[]{:S(2)}) copy-start(f32[8,5120]{1,0:T(8,128)} %shard_map.68.sent_ref) | copy-start | bytes 491524
  10.5 1.8 %copy-start.2 = (f32[1,16,2048]{2,1,0:T(8,128)S(1)}, f32[1,16,2048]{2,1,0:T(8,128)}, u32[]{:S(2)}) copy-start(f32[1,16,2048]{2,1,0:T(8,128)} %param.5) | copy-start | bytes 393220
  10.5 1.8 %copy-start = (f32[1,16,2048]{2,1,0:T(8,128)S(1)}, f32[1,16,2048]{2,1,0:T(8,128)}, u32[]{:S(2)}) copy-start(f32[1,16,2048]{2,1,0:T(8,128)} %param.6) | copy-start | bytes 393220
  10.7 5.4 %collective-permute-start = (f32[8,1792]{1,0:T(8,128)S(1)}, f32[8,1792]{1,0:T(8,128)S(1)}, u32[]{:S(2)}, u32[]{:S(2)}) collective-permute-start(f32[8,1792]{1,0:T(8,128)S(1)} %get-tuple-element.32), channel_id=1, source_target_pairs={{0,2},{1,3},{2,4},{3,5},{4,6},{5,7},{6,0},{7,1},{8,10},{9,11},{10,... | collective-permute-start | bytes 172040 | tf_op jit(solution)/shard_map/ppermute | solution.py:339
  16.1 12.1 %collective-permute-start.7 = (f32[16,2048]{1,0:T(8,128)S(1)}, f32[16,2048]{1,0:T(8,128)S(1)}, u32[]{:S(2)}, u32[]{:S(2)}) collective-permute-start(f32[16,2048]{1,0:T(8,128)S(1)} %shard_map.71.own_ref), channel_id=1, source_target_pairs={{0,1},{1,0},{2,3},{3,2},{4,5},{5,4},{6,7},{7,6},{8,9},{9,8},{10,11... | collective-permute-start | bytes 393224 | tf_op jit(solution)/shard_map/ppermute | solution.py:335
  16.1 5.7 %collective-permute-start.1 = (f32[8,1792]{1,0:T(8,128)S(1)}, f32[8,1792]{1,0:T(8,128)S(1)}, u32[]{:S(2)}, u32[]{:S(2)}) collective-permute-start(f32[8,1792]{1,0:T(8,128)S(1)} %get-tuple-element.34), channel_id=1, source_target_pairs={{0,4},{1,5},{2,6},{3,7},{4,0},{5,1},{6,2},{7,3},{8,12},{9,13},{10,... | collective-permute-start | bytes 172040 | tf_op jit(solution)/shard_map/ppermute | solution.py:339
  18.1 5.6 %collective-permute-start.2 = (f32[8,1792]{1,0:T(8,128)S(1)}, f32[8,1792]{1,0:T(8,128)S(1)}, u32[]{:S(2)}, u32[]{:S(2)}) collective-permute-start(f32[8,1792]{1,0:T(8,128)S(1)} %get-tuple-element.35), channel_id=1, source_target_pairs={{0,6},{1,7},{2,0},{3,1},{4,2},{5,3},{6,4},{7,5},{8,14},{9,15},{10,... | collective-permute-start | bytes 172040 | tf_op jit(solution)/shard_map/ppermute | solution.py:339
  19.2 7.0 %copy-start.3 = (s32[4096]{0:T(1024)S(1)}, s32[4096]{0:T(1024)}, u32[]{:S(2)}) copy-start(s32[4096]{0:T(1024)} %param.8) | copy-start | bytes 49156
  19.3 5.4 %collective-permute-start.4 = (f32[8,1792]{1,0:T(8,128)S(1)}, f32[8,1792]{1,0:T(8,128)S(1)}, u32[]{:S(2)}, u32[]{:S(2)}) collective-permute-start(f32[8,1792]{1,0:T(8,128)S(1)} %get-tuple-element.37), channel_id=1, source_target_pairs={{0,2},{1,3},{2,4},{3,5},{4,6},{5,7},{6,0},{7,1},{8,10},{9,11},{10,... | collective-permute-start | bytes 172040 | tf_op jit(solution)/shard_map/ppermute | solution.py:339
  20.3 5.7 %collective-permute-start.5 = (f32[8,1792]{1,0:T(8,128)S(1)}, f32[8,1792]{1,0:T(8,128)S(1)}, u32[]{:S(2)}, u32[]{:S(2)}) collective-permute-start(f32[8,1792]{1,0:T(8,128)S(1)} %get-tuple-element.38), channel_id=1, source_target_pairs={{0,4},{1,5},{2,6},{3,7},{4,0},{5,1},{6,2},{7,3},{8,12},{9,13},{10,... | collective-permute-start | bytes 172040 | tf_op jit(solution)/shard_map/ppermute | solution.py:339
  21.9 4.3 %collective-permute-start.6 = (f32[8,1792]{1,0:T(8,128)S(1)}, f32[8,1792]{1,0:T(8,128)S(1)}, u32[]{:S(2)}, u32[]{:S(2)}) collective-permute-start(f32[8,1792]{1,0:T(8,128)S(1)} %get-tuple-element.39), channel_id=1, source_target_pairs={{0,6},{1,7},{2,0},{3,1},{4,2},{5,3},{6,4},{7,5},{8,14},{9,15},{10,... | collective-permute-start | bytes 172040 | tf_op jit(solution)/shard_map/ppermute | solution.py:339
  26.2 5.1 %copy-start.4 = (f32[8,8]{1,0:T(8,128)S(1)}, f32[8,8]{1,0:T(8,128)}, u32[]{:S(2)}) copy-start(f32[8,8]{1,0:T(8,128)} %param.7) | copy-start | bytes 772
  28.2 11.0 %collective-permute-start.9 = (f32[8,8960]{1,0:T(8,128)S(1)}, f32[8,8960]{1,0:T(8,128)S(1)}, u32[]{:S(2)}, u32[]{:S(2)}) collective-permute-start(f32[8,8960]{1,0:T(8,128)S(1)} %get-tuple-element.49), channel_id=1, source_target_pairs={{8,16},{16,8},{9,17},{17,9},{10,18},{18,10},{11,19},{19,11},{12,20... | collective-permute-start | bytes 860168 | tf_op jit(solution)/shard_map/ppermute | solution.py:348
  32.2 7.0 %collective-permute-start.8 = (f32[8,8960]{1,0:T(8,128)S(1)}, f32[8,8960]{1,0:T(8,128)S(1)}, u32[]{:S(2)}, u32[]{:S(2)}) collective-permute-start(f32[8,8960]{1,0:T(8,128)S(1)} %get-tuple-element.48), channel_id=1, source_target_pairs={{0,8},{8,0},{1,9},{9,1},{2,10},{10,2},{3,11},{11,3},{4,12},{12,4},... | collective-permute-start | bytes 860168 | tf_op jit(solution)/shard_map/ppermute | solution.py:348
  35.1 11.9 %collective-permute-start.13 = (f32[16,2048]{1,0:T(8,128)S(1)}, f32[16,2048]{1,0:T(8,128)S(1)}, u32[]{:S(2)}, u32[]{:S(2)}) collective-permute-start(f32[16,2048]{1,0:T(8,128)S(1)} %get-tuple-element.55), channel_id=1, source_target_pairs={{0,2},{1,3},{2,4},{3,5},{4,6},{5,7},{6,0},{7,1},{8,10},{9,11},{10,... | collective-permute-start | bytes 393224 | tf_op jit(solution)/shard_map/ppermute | solution.py:339
  35.3 13.1 %collective-permute-start.14 = (f32[16,2048]{1,0:T(8,128)S(1)}, f32[16,2048]{1,0:T(8,128)S(1)}, u32[]{:S(2)}, u32[]{:S(2)}) collective-permute-start(f32[16,2048]{1,0:T(8,128)S(1)} %get-tuple-element.56), channel_id=1, source_target_pairs={{0,4},{1,5},{2,6},{3,7},{4,0},{5,1},{6,2},{7,3},{8,12},{9,13},{10,... | collective-permute-start | bytes 393224 | tf_op jit(solution)/shard_map/ppermute | solution.py:339
  39.1 9.3 %collective-permute-start.15 = (f32[16,2048]{1,0:T(8,128)S(1)}, f32[16,2048]{1,0:T(8,128)S(1)}, u32[]{:S(2)}, u32[]{:S(2)}) collective-permute-start(f32[16,2048]{1,0:T(8,128)S(1)} %get-tuple-element.57), channel_id=1, source_target_pairs={{0,6},{1,7},{2,0},{3,1},{4,2},{5,3},{6,4},{7,5},{8,14},{9,15},{10,... | collective-permute-start | bytes 393224 | tf_op jit(solution)/shard_map/ppermute | solution.py:339
  43.6 6.1 %collective-permute-start.10 = (f32[8,2176]{1,0:T(8,128)S(1)}, f32[8,2176]{1,0:T(8,128)S(1)}, u32[]{:S(2)}, u32[]{:S(2)}) collective-permute-start(f32[8,2176]{1,0:T(8,128)S(1)} %get-tuple-element.51), channel_id=1, source_target_pairs={{0,2},{1,3},{2,4},{3,5},{4,6},{5,7},{6,0},{7,1},{8,10},{9,11},{10,... | collective-permute-start | bytes 208904 | tf_op jit(solution)/shard_map/ppermute | solution.py:339
  45.6 5.8 %collective-permute-start.11 = (f32[8,2176]{1,0:T(8,128)S(1)}, f32[8,2176]{1,0:T(8,128)S(1)}, u32[]{:S(2)}, u32[]{:S(2)}) collective-permute-start(f32[8,2176]{1,0:T(8,128)S(1)} %get-tuple-element.52), channel_id=1, source_target_pairs={{0,4},{1,5},{2,6},{3,7},{4,0},{5,1},{6,2},{7,3},{8,12},{9,13},{10,... | collective-permute-start | bytes 208904 | tf_op jit(solution)/shard_map/ppermute | solution.py:339
  47.0 4.4 %collective-permute-start.12 = (f32[8,2176]{1,0:T(8,128)S(1)}, f32[8,2176]{1,0:T(8,128)S(1)}, u32[]{:S(2)}, u32[]{:S(2)}) collective-permute-start(f32[8,2176]{1,0:T(8,128)S(1)} %get-tuple-element.53), channel_id=1, source_target_pairs={{0,6},{1,7},{2,0},{3,1},{4,2},{5,3},{6,4},{7,5},{8,14},{9,15},{10,... | collective-permute-start | bytes 208904 | tf_op jit(solution)/shard_map/ppermute | solution.py:339

commit v7 on v6

--- a/solution.py
+++ b/solution.py
@@ -246,7 +246,10 @@
 
     def shape(src, var):
         u = src[var]
-        return kp[var] * u - shape_rows(u) * mask_ref[...]
+        beside = shape_rows(u)
+        side = beside[:ROWS, BLOCK:] * mask_ref[:ROWS, BLOCK:]
+        own = jnp.concatenate([beside[:ROWS, :BLOCK], side], axis=1)
+        return kp[var] * u - jnp.concatenate([own, beside[ROWS:] * mask_ref[ROWS:]], axis=0)
 
     def couple(ref):
         for r in range(0, TALL, 8):

time: 52.4 us -> 52.3 us (level)
  no operation moved by 1% of the time
where the time goes in v7:
time: 52.3 us; the launch traced here: 52.2 us
  starting transfers between devices  31.2 us (60%)
  Pallas kernels  9.82 us (19%)
  waiting for transfers between devices  9.26 us (18%)
  local copies, waits for them, and re-layouts  0.97 us (2%)
  between operations  0.73 us (1%)
    ppermute x12, starting transfers between devices, around(): lax.ppermute(x, 'var', [(i, (i // 2 + k) % GROUPS * 2 + i % 2) for i in r...  17.9 us
    ppermute x12, waiting for transfers between devices, around(): lax.ppermute(x, 'var', [(i, (i // 2 + k) % GROUPS * 2 + i % 2) for i in r...  9.25 us
    ppermute x2, starting transfers between devices, across(): return lax.ppermute(x, 'var', [(i, i ^ 1) for i in range(VARS)])  7.28 us
    ppermute x2, starting transfers between devices, beside(): return lax.ppermute(x, ('tile', 'var'), pairs)  5.98 us
    pallas_call x1, Pallas kernels, per_device(): call(main_kernel, [(8, 4 * BLOCK + SIDE)] * 4, 12, smem=1, scratch=[pltpu...  4.3 us
    pallas_call x1, Pallas kernels, per_device(): call(scatter_kernel, [(VARS, ROWS, WIDE), edges, edges], 9, scratch=[pltp...  1.97 us
    pallas_call x1, Pallas kernels, per_device(): call(first_kernel, [(8, EXTRA + 2 * BLOCK)], 3, hbm=3, limit=56, scratch=...  1.64 us
  transfers between devices with their start and end apart: 16, of which 6 were waited for; matrix products, arithmetic and copies ran while one was open for 0% of the time, Pallas kernels for 14%

profile of v7, /device:TPU:2, one launch (start us, length us, event | category | flops | bytes accessed | tf_op | source)
XLA Modules:
  0.0 52.2 jit_solution(8060401600622774913)
XLA Ops:
  0.6 1.6 %shard_map.68.sent_ref = f32[8,5120]{1,0:T(8,128)} custom-call(f32[16,2048]{1,0:T(8,128)} %bitcast.8, f32[1,4096]{1,0:T(1,128)} %obs_hbm.1, f32[16,2048]{1,0:T(8,128)} %bitcast.5), custom_call_target="tpu_custom_call" | custom-call | flops 1000 | bytes 100000 | tf_op jit(solution)/shard_map/pallas_call | solution.py:358
  2.3 7.3 %collective-permute-start.3 = (f32[8,5120]{1,0:T(8,128)}, f32[8,5120]{1,0:T(8,128)S(1)}, u32[]{:S(2)}, u32[]{:S(2)}) collective-permute-start(f32[8,5120]{1,0:T(8,128)} %shard_map.68.sent_ref), channel_id=1, source_target_pairs={{0,1},{1,0},{2,3},{3,2},{4,5},{5,4},{6,7},{7,6},{8,9},{9,8},{10,11... | collective-permute-start | bytes 491528 | tf_op jit(solution)/shard_map/ppermute | solution.py:338
  9.6 0.9 %copy-done.1 = f32[8,5120]{1,0:T(8,128)S(1)} copy-done((f32[8,5120]{1,0:T(8,128)S(1)}, f32[8,5120]{1,0:T(8,128)}, u32[]{:S(2)}) %copy-start.1) | copy-done | bytes 163864
  10.7 1.6 %collective-permute-start = (f32[8,1792]{1,0:T(8,128)S(1)}, f32[8,1792]{1,0:T(8,128)S(1)}, u32[]{:S(2)}, u32[]{:S(2)}) collective-permute-start(f32[8,1792]{1,0:T(8,128)S(1)} %get-tuple-element.32), channel_id=1, source_target_pairs={{0,2},{1,3},{2,4},{3,5},{4,6},{5,7},{6,0},{7,1},{8,10},{9,11},{10,... | collective-permute-start | bytes 172040 | tf_op jit(solution)/shard_map/ppermute | solution.py:342
  12.4 3.7 %collective-permute-done.refs_1_ = f32[8,1792]{1,0:T(8,128)S(1)} collective-permute-done((f32[8,1792]{1,0:T(8,128)S(1)}, f32[8,1792]{1,0:T(8,128)S(1)}, u32[]{:S(2)}, u32[]{:S(2)}) %collective-permute-start) | collective-permute-done | bytes 57376 | tf_op jit(solution)/shard_map/ppermute | solution.py:342
  16.1 2.0 %collective-permute-start.1 = (f32[8,1792]{1,0:T(8,128)S(1)}, f32[8,1792]{1,0:T(8,128)S(1)}, u32[]{:S(2)}, u32[]{:S(2)}) collective-permute-start(f32[8,1792]{1,0:T(8,128)S(1)} %get-tuple-element.34), channel_id=1, source_target_pairs={{0,4},{1,5},{2,6},{3,7},{4,0},{5,1},{6,2},{7,3},{8,12},{9,13},{10,... | collective-permute-start | bytes 172040 | tf_op jit(solution)/shard_map/ppermute | solution.py:342
  18.1 1.1 %collective-permute-start.2 = (f32[8,1792]{1,0:T(8,128)S(1)}, f32[8,1792]{1,0:T(8,128)S(1)}, u32[]{:S(2)}, u32[]{:S(2)}) collective-permute-start(f32[8,1792]{1,0:T(8,128)S(1)} %get-tuple-element.35), channel_id=1, source_target_pairs={{0,6},{1,7},{2,0},{3,1},{4,2},{5,3},{6,4},{7,5},{8,14},{9,15},{10,... | collective-permute-start | bytes 172040 | tf_op jit(solution)/shard_map/ppermute | solution.py:342
  19.3 1.0 %collective-permute-start.4 = (f32[8,1792]{1,0:T(8,128)S(1)}, f32[8,1792]{1,0:T(8,128)S(1)}, u32[]{:S(2)}, u32[]{:S(2)}) collective-permute-start(f32[8,1792]{1,0:T(8,128)S(1)} %get-tuple-element.37), channel_id=1, source_target_pairs={{0,2},{1,3},{2,4},{3,5},{4,6},{5,7},{6,0},{7,1},{8,10},{9,11},{10,... | collective-permute-start | bytes 172040 | tf_op jit(solution)/shard_map/ppermute | solution.py:342
  20.3 1.5 %collective-permute-start.5 = (f32[8,1792]{1,0:T(8,128)S(1)}, f32[8,1792]{1,0:T(8,128)S(1)}, u32[]{:S(2)}, u32[]{:S(2)}) collective-permute-start(f32[8,1792]{1,0:T(8,128)S(1)} %get-tuple-element.38), channel_id=1, source_target_pairs={{0,4},{1,5},{2,6},{3,7},{4,0},{5,1},{6,2},{7,3},{8,12},{9,13},{10,... | collective-permute-start | bytes 172040 | tf_op jit(solution)/shard_map/ppermute | solution.py:342
  21.9 1.8 %collective-permute-start.6 = (f32[8,1792]{1,0:T(8,128)S(1)}, f32[8,1792]{1,0:T(8,128)S(1)}, u32[]{:S(2)}, u32[]{:S(2)}) collective-permute-start(f32[8,1792]{1,0:T(8,128)S(1)} %get-tuple-element.39), channel_id=1, source_target_pairs={{0,6},{1,7},{2,0},{3,1},{4,2},{5,3},{6,4},{7,5},{8,14},{9,15},{10,... | collective-permute-start | bytes 172040 | tf_op jit(solution)/shard_map/ppermute | solution.py:342
  23.7 1.1 %collective-permute-done.4.refs_5_ = f32[8,1792]{1,0:T(8,128)S(1)} collective-permute-done((f32[8,1792]{1,0:T(8,128)S(1)}, f32[8,1792]{1,0:T(8,128)S(1)}, u32[]{:S(2)}, u32[]{:S(2)}) %collective-permute-start.4) | collective-permute-done | bytes 57376 | tf_op jit(solution)/shard_map/ppermute | solution.py:342
  24.7 1.3 %collective-permute-done.5.refs_6_ = f32[8,1792]{1,0:T(8,128)S(1)} collective-permute-done((f32[8,1792]{1,0:T(8,128)S(1)}, f32[8,1792]{1,0:T(8,128)S(1)}, u32[]{:S(2)}, u32[]{:S(2)}) %collective-permute-start.5) | collective-permute-done | bytes 57376 | tf_op jit(solution)/shard_map/ppermute | solution.py:342
  26.2 2.0 %shard_map.73 = (f32[8,16,640]{2,1,0:T(8,128)S(1)}, f32[8,8960]{1,0:T(8,128)S(1)}, f32[8,8960]{1,0:T(8,128)S(1)}) custom-call(s32[1,4096]{1,0:T(1,128)S(1)} %bitcast.10, f32[8,1792]{1,0:T(8,128)S(1)} %get-tuple-element.31.refs_0_, f32[8,1792]{1,0:T(8,128)S(1)} %collective-permute-done.refs_1_, f32[8,1792]{1,0:T(8,128)S(1)} %collective-permute-done.1.refs_2_, ...), custom_call_target="tpu_custom_call" | custom-call | flops 1000 | bytes 100000 | tf_op jit(solution)/shard_map/pallas_call | solution.py:378
  28.2 3.1 %collective-permute-start.9 = (f32[8,8960]{1,0:T(8,128)S(1)}, f32[8,8960]{1,0:T(8,128)S(1)}, u32[]{:S(2)}, u32[]{:S(2)}) collective-permute-start(f32[8,8960]{1,0:T(8,128)S(1)} %get-tuple-element.49), channel_id=1, source_target_pairs={{8,16},{16,8},{9,17},{17,9},{10,18},{18,10},{11,19},{19,11},{12,20... | collective-permute-start | bytes 860168 | tf_op jit(solution)/shard_map/ppermute | solution.py:351
  31.5 0.7 %shard_map.74 = (f32[16,2048]{1,0:T(8,128)S(1)}, f32[16,2048]{1,0:T(8,128)S(1)}, f32[16,2048]{1,0:T(8,128)S(1)}, f32[16,2048]{1,0:T(8,128)S(1)}) custom-call(f32[8,8]{1,0:T(8,128)S(1)} %convolution_multiply_fusion.mix_ref, f32[16,2048]{1,0:T(8,128)S(1)} %shard_map.71.own_ref, f32[16,2048]{1,0:T(8,128)S(1)} %collective-permute-done.7.other_ref), custom_call_target="tpu_custom_call" | custom-call | flops 1000 | bytes 100000 | tf_op jit(solution)/shard_map/pallas_call | solution.py:387
  32.2 2.9 %collective-permute-start.8 = (f32[8,8960]{1,0:T(8,128)S(1)}, f32[8,8960]{1,0:T(8,128)S(1)}, u32[]{:S(2)}, u32[]{:S(2)}) collective-permute-start(f32[8,8960]{1,0:T(8,128)S(1)} %get-tuple-element.48), channel_id=1, source_target_pairs={{0,8},{8,0},{1,9},{9,1},{2,10},{10,2},{3,11},{11,3},{4,12},{12,4},... | collective-permute-start | bytes 860168 | tf_op jit(solution)/shard_map/ppermute | solution.py:351
  35.3 3.8 %collective-permute-start.14 = (f32[16,2048]{1,0:T(8,128)S(1)}, f32[16,2048]{1,0:T(8,128)S(1)}, u32[]{:S(2)}, u32[]{:S(2)}) collective-permute-start(f32[16,2048]{1,0:T(8,128)S(1)} %get-tuple-element.56), channel_id=1, source_target_pairs={{0,4},{1,5},{2,6},{3,7},{4,0},{5,1},{6,2},{7,3},{8,12},{9,13},{10,... | collective-permute-start | bytes 393224 | tf_op jit(solution)/shard_map/ppermute | solution.py:342
  39.3 4.3 %shard_map.76 = (f32[8,2176]{1,0:T(8,128)S(1)}, f32[8,2176]{1,0:T(8,128)S(1)}, f32[8,2176]{1,0:T(8,128)S(1)}, f32[8,2176]{1,0:T(8,128)S(1)}) custom-call(f32[8,8]{1,0:T(8,128)S(1)} %convolution_multiply_fusion.mix_ref, f32[8,16,640]{2,1,0:T(8,128)S(1)} %get-tuple-element.40.source_ref, f32[8,8960]{1,0:T(8,128)S(1)} %collective-permute-done.8.near_ref, ...), custom_call_target="tpu_custom_call" | custom-call | flops 1000 | bytes 100000 | tf_op jit(solution)/shard_map/pallas_call | solution.py:393
  43.6 2.0 %collective-permute-start.10 = (f32[8,2176]{1,0:T(8,128)S(1)}, f32[8,2176]{1,0:T(8,128)S(1)}, u32[]{:S(2)}, u32[]{:S(2)}) collective-permute-start(f32[8,2176]{1,0:T(8,128)S(1)} %get-tuple-element.51), channel_id=1, source_target_pairs={{0,2},{1,3},{2,4},{3,5},{4,6},{5,7},{6,0},{7,1},{8,10},{9,11},{10,... | collective-permute-start | bytes 208904 | tf_op jit(solution)/shard_map/ppermute | solution.py:342
  45.6 1.4 %collective-permute-start.11 = (f32[8,2176]{1,0:T(8,128)S(1)}, f32[8,2176]{1,0:T(8,128)S(1)}, u32[]{:S(2)}, u32[]{:S(2)}) collective-permute-start(f32[8,2176]{1,0:T(8,128)S(1)} %get-tuple-element.52), channel_id=1, source_target_pairs={{0,4},{1,5},{2,6},{3,7},{4,0},{5,1},{6,2},{7,3},{8,12},{9,13},{10,... | collective-permute-start | bytes 208904 | tf_op jit(solution)/shard_map/ppermute | solution.py:342
  47.0 1.3 %collective-permute-start.12 = (f32[8,2176]{1,0:T(8,128)S(1)}, f32[8,2176]{1,0:T(8,128)S(1)}, u32[]{:S(2)}, u32[]{:S(2)}) collective-permute-start(f32[8,2176]{1,0:T(8,128)S(1)} %get-tuple-element.53), channel_id=1, source_target_pairs={{0,6},{1,7},{2,0},{3,1},{4,2},{5,3},{6,4},{7,5},{8,14},{9,15},{10,... | collective-permute-start | bytes 208904 | tf_op jit(solution)/shard_map/ppermute | solution.py:342
  48.3 1.4 %collective-permute-done.10.p1 = f32[8,2176]{1,0:T(8,128)S(1)} collective-permute-done((f32[8,2176]{1,0:T(8,128)S(1)}, f32[8,2176]{1,0:T(8,128)S(1)}, u32[]{:S(2)}, u32[]{:S(2)}) %collective-permute-start.10) | collective-permute-done | bytes 69664 | tf_op jit(solution)/shard_map/ppermute | solution.py:342
  49.7 1.6 %collective-permute-done.11.p2 = f32[8,2176]{1,0:T(8,128)S(1)} collective-permute-done((f32[8,2176]{1,0:T(8,128)S(1)}, f32[8,2176]{1,0:T(8,128)S(1)}, u32[]{:S(2)}, u32[]{:S(2)}) %collective-permute-start.11) | collective-permute-done | bytes 69664 | tf_op jit(solution)/shard_map/ppermute | solution.py:342
  51.4 0.8 %shard_map.77 = (f32[16,2048]{1,0:T(8,128)}, f32[16,2048]{1,0:T(8,128)}) custom-call(f32[8,2176]{1,0:T(8,128)S(1)} %get-tuple-element.50.p0, f32[8,2176]{1,0:T(8,128)S(1)} %collective-permute-done.10.p1, f32[8,2176]{1,0:T(8,128)S(1)} %collective-permute-done.11.p2, f32[8,2176]{1,0:T(8,128)S(1)} %collective-permute-done.12.p3, ...), custom_call_target="tpu_custom_call" | custom-call | flops 1000 | bytes 100000 | tf_op jit(solution)/shard_map/pallas_call | solution.py:401
  (29 shorter events, 1.2 us)
Async XLA Ops:
  2.3 16.9 %collective-permute-start.3 = (f32[8,5120]{1,0:T(8,128)}, f32[8,5120]{1,0:T(8,128)S(1)}, u32[]{:S(2)}, u32[]{:S(2)}) collective-permute-start(f32[8,5120]{1,0:T(8,128)} %shard_map.68.sent_ref), channel_id=1, source_target_pairs={{0,1},{1,0},{2,3},{3,2},{4,5},{5,4},{6,7},{7,6},{8,9},{9,8},{10,11... | collective-permute-start | bytes 491528 | tf_op jit(solution)/shard_map/ppermute | solution.py:338
  9.6 0.9 %copy-start.1 = (f32[8,5120]{1,0:T(8,128)S(1)}, f32[8,5120]{1,0:T(8,128)}, u32[]{:S(2)}) copy-start(f32[8,5120]{1,0:T(8,128)} %shard_map.68.sent_ref) | copy-start | bytes 491524
  10.5 1.8 %copy-start.2 = (f32[1,16,2048]{2,1,0:T(8,128)S(1)}, f32[1,16,2048]{2,1,0:T(8,128)}, u32[]{:S(2)}) copy-start(f32[1,16,2048]{2,1,0:T(8,128)} %param.5) | copy-start | bytes 393220
  10.5 1.8 %copy-start = (f32[1,16,2048]{2,1,0:T(8,128)S(1)}, f32[1,16,2048]{2,1,0:T(8,128)}, u32[]{:S(2)}) copy-start(f32[1,16,2048]{2,1,0:T(8,128)} %param.6) | copy-start | bytes 393220
  10.7 5.4 %collective-permute-start = (f32[8,1792]{1,0:T(8,128)S(1)}, f32[8,1792]{1,0:T(8,128)S(1)}, u32[]{:S(2)}, u32[]{:S(2)}) collective-permute-start(f32[8,1792]{1,0:T(8,128)S(1)} %get-tuple-element.32), channel_id=1, source_target_pairs={{0,2},{1,3},{2,4},{3,5},{4,6},{5,7},{6,0},{7,1},{8,10},{9,11},{10,... | collective-permute-start | bytes 172040 | tf_op jit(solution)/shard_map/ppermute | solution.py:342
  16.1 12.1 %collective-permute-start.7 = (f32[16,2048]{1,0:T(8,128)S(1)}, f32[16,2048]{1,0:T(8,128)S(1)}, u32[]{:S(2)}, u32[]{:S(2)}) collective-permute-start(f32[16,2048]{1,0:T(8,128)S(1)} %shard_map.71.own_ref), channel_id=1, source_target_pairs={{0,1},{1,0},{2,3},{3,2},{4,5},{5,4},{6,7},{7,6},{8,9},{9,8},{10,11... | collective-permute-start | bytes 393224 | tf_op jit(solution)/shard_map/ppermute | solution.py:338
  16.1 5.7 %collective-permute-start.1 = (f32[8,1792]{1,0:T(8,128)S(1)}, f32[8,1792]{1,0:T(8,128)S(1)}, u32[]{:S(2)}, u32[]{:S(2)}) collective-permute-start(f32[8,1792]{1,0:T(8,128)S(1)} %get-tuple-element.34), channel_id=1, source_target_pairs={{0,4},{1,5},{2,6},{3,7},{4,0},{5,1},{6,2},{7,3},{8,12},{9,13},{10,... | collective-permute-start | bytes 172040 | tf_op jit(solution)/shard_map/ppermute | solution.py:342
  18.1 5.6 %collective-permute-start.2 = (f32[8,1792]{1,0:T(8,128)S(1)}, f32[8,1792]{1,0:T(8,128)S(1)}, u32[]{:S(2)}, u32[]{:S(2)}) collective-permute-start(f32[8,1792]{1,0:T(8,128)S(1)} %get-tuple-element.35), channel_id=1, source_target_pairs={{0,6},{1,7},{2,0},{3,1},{4,2},{5,3},{6,4},{7,5},{8,14},{9,15},{10,... | collective-permute-start | bytes 172040 | tf_op jit(solution)/shard_map/ppermute | solution.py:342
  19.2 7.0 %copy-start.3 = (s32[4096]{0:T(1024)S(1)}, s32[4096]{0:T(1024)}, u32[]{:S(2)}) copy-start(s32[4096]{0:T(1024)} %param.8) | copy-start | bytes 49156
  19.3 5.4 %collective-permute-start.4 = (f32[8,1792]{1,0:T(8,128)S(1)}, f32[8,1792]{1,0:T(8,128)S(1)}, u32[]{:S(2)}, u32[]{:S(2)}) collective-permute-start(f32[8,1792]{1,0:T(8,128)S(1)} %get-tuple-element.37), channel_id=1, source_target_pairs={{0,2},{1,3},{2,4},{3,5},{4,6},{5,7},{6,0},{7,1},{8,10},{9,11},{10,... | collective-permute-start | bytes 172040 | tf_op jit(solution)/shard_map/ppermute | solution.py:342
  20.3 5.7 %collective-permute-start.5 = (f32[8,1792]{1,0:T(8,128)S(1)}, f32[8,1792]{1,0:T(8,128)S(1)}, u32[]{:S(2)}, u32[]{:S(2)}) collective-permute-start(f32[8,1792]{1,0:T(8,128)S(1)} %get-tuple-element.38), channel_id=1, source_target_pairs={{0,4},{1,5},{2,6},{3,7},{4,0},{5,1},{6,2},{7,3},{8,12},{9,13},{10,... | collective-permute-start | bytes 172040 | tf_op jit(solution)/shard_map/ppermute | solution.py:342
  21.9 4.3 %collective-permute-start.6 = (f32[8,1792]{1,0:T(8,128)S(1)}, f32[8,1792]{1,0:T(8,128)S(1)}, u32[]{:S(2)}, u32[]{:S(2)}) collective-permute-start(f32[8,1792]{1,0:T(8,128)S(1)} %get-tuple-element.39), channel_id=1, source_target_pairs={{0,6},{1,7},{2,0},{3,1},{4,2},{5,3},{6,4},{7,5},{8,14},{9,15},{10,... | collective-permute-start | bytes 172040 | tf_op jit(solution)/shard_map/ppermute | solution.py:342
  26.2 5.1 %copy-start.4 = (f32[8,8]{1,0:T(8,128)S(1)}, f32[8,8]{1,0:T(8,128)}, u32[]{:S(2)}) copy-start(f32[8,8]{1,0:T(8,128)} %param.7) | copy-start | bytes 772
  28.2 11.0 %collective-permute-start.9 = (f32[8,8960]{1,0:T(8,128)S(1)}, f32[8,8960]{1,0:T(8,128)S(1)}, u32[]{:S(2)}, u32[]{:S(2)}) collective-permute-start(f32[8,8960]{1,0:T(8,128)S(1)} %get-tuple-element.49), channel_id=1, source_target_pairs={{8,16},{16,8},{9,17},{17,9},{10,18},{18,10},{11,19},{19,11},{12,20... | collective-permute-start | bytes 860168 | tf_op jit(solution)/shard_map/ppermute | solution.py:351
  32.2 7.0 %collective-permute-start.8 = (f32[8,8960]{1,0:T(8,128)S(1)}, f32[8,8960]{1,0:T(8,128)S(1)}, u32[]{:S(2)}, u32[]{:S(2)}) collective-permute-start(f32[8,8960]{1,0:T(8,128)S(1)} %get-tuple-element.48), channel_id=1, source_target_pairs={{0,8},{8,0},{1,9},{9,1},{2,10},{10,2},{3,11},{11,3},{4,12},{12,4},... | collective-permute-start | bytes 860168 | tf_op jit(solution)/shard_map/ppermute | solution.py:351
  35.1 11.9 %collective-permute-start.13 = (f32[16,2048]{1,0:T(8,128)S(1)}, f32[16,2048]{1,0:T(8,128)S(1)}, u32[]{:S(2)}, u32[]{:S(2)}) collective-permute-start(f32[16,2048]{1,0:T(8,128)S(1)} %get-tuple-element.55), channel_id=1, source_target_pairs={{0,2},{1,3},{2,4},{3,5},{4,6},{5,7},{6,0},{7,1},{8,10},{9,11},{10,... | collective-permute-start | bytes 393224 | tf_op jit(solution)/shard_map/ppermute | solution.py:342
  35.3 13.1 %collective-permute-start.14 = (f32[16,2048]{1,0:T(8,128)S(1)}, f32[16,2048]{1,0:T(8,128)S(1)}, u32[]{:S(2)}, u32[]{:S(2)}) collective-permute-start(f32[16,2048]{1,0:T(8,128)S(1)} %get-tuple-element.56), channel_id=1, source_target_pairs={{0,4},{1,5},{2,6},{3,7},{4,0},{5,1},{6,2},{7,3},{8,12},{9,13},{10,... | collective-permute-start | bytes 393224 | tf_op jit(solution)/shard_map/ppermute | solution.py:342
  39.1 9.2 %collective-permute-start.15 = (f32[16,2048]{1,0:T(8,128)S(1)}, f32[16,2048]{1,0:T(8,128)S(1)}, u32[]{:S(2)}, u32[]{:S(2)}) collective-permute-start(f32[16,2048]{1,0:T(8,128)S(1)} %get-tuple-element.57), channel_id=1, source_target_pairs={{0,6},{1,7},{2,0},{3,1},{4,2},{5,3},{6,4},{7,5},{8,14},{9,15},{10,... | collective-permute-start | bytes 393224 | tf_op jit(solution)/shard_map/ppermute | solution.py:342
  43.6 6.1 %collective-permute-start.10 = (f32[8,2176]{1,0:T(8,128)S(1)}, f32[8,2176]{1,0:T(8,128)S(1)}, u32[]{:S(2)}, u32[]{:S(2)}) collective-permute-start(f32[8,2176]{1,0:T(8,128)S(1)} %get-tuple-element.51), channel_id=1, source_target_pairs={{0,2},{1,3},{2,4},{3,5},{4,6},{5,7},{6,0},{7,1},{8,10},{9,11},{10,... | collective-permute-start | bytes 208904 | tf_op jit(solution)/shard_map/ppermute | solution.py:342
  45.6 5.8 %collective-permute-start.11 = (f32[8,2176]{1,0:T(8,128)S(1)}, f32[8,2176]{1,0:T(8,128)S(1)}, u32[]{:S(2)}, u32[]{:S(2)}) collective-permute-start(f32[8,2176]{1,0:T(8,128)S(1)} %get-tuple-element.52), channel_id=1, source_target_pairs={{0,4},{1,5},{2,6},{3,7},{4,0},{5,1},{6,2},{7,3},{8,12},{9,13},{10,... | collective-permute-start | bytes 208904 | tf_op jit(solution)/shard_map/ppermute | solution.py:342
  47.0 4.4 %collective-permute-start.12 = (f32[8,2176]{1,0:T(8,128)S(1)}, f32[8,2176]{1,0:T(8,128)S(1)}, u32[]{:S(2)}, u32[]{:S(2)}) collective-permute-start(f32[8,2176]{1,0:T(8,128)S(1)} %get-tuple-element.53), channel_id=1, source_target_pairs={{0,6},{1,7},{2,0},{3,1},{4,2},{5,3},{6,4},{7,5},{8,14},{9,15},{10,... | collective-permute-start | bytes 208904 | tf_op jit(solution)/shard_map/ppermute | solution.py:342
